TPU v7x, 32 devices: a whole 2x2x4 slice. The times are simulated.
32 devices in a mesh: grp: 4 (over y, x), tok: 2 (over core), head: 4 (over z).
Axes of the slice: x: 2, y: 2, z: 4, core: 2. Of those that a mesh axis runs over, the one named last changes fastest.
Arguments:
- tokens: bfloat16 [4, 256, 1024], P('grp', 'tok'), may hold values from -6 to 6
- lengths: int32 [4, 8], P('grp'), may hold values from 1 to 192, 256 in all within a row
- block_position: int32 [4, 32], P('grp'), may hold values from 0 to 31, each once within a row
- prefix_pool: bfloat16 [4, 32, 16, 2, 1024], P('grp', ('tok', 'head'))
- cross_cache: bfloat16 [4, 256, 2, 1024], P('grp', None, None, 'head')
- w_query: bfloat16 [1024, 1024], P(None, 'head'), may hold values from -0.5 to 0.5
- w_keyvalue: bfloat16 [1024, 2, 1024], P(None, None, 'head'), may hold values from -0.1875 to 0.1875
- w_out: bfloat16 [1024, 1024], P('head'), may hold values from -0.1875 to 0.1875
- w_cross_query: bfloat16 [1024, 1024], P(None, 'head'), may hold values from -0.5 to 0.5
- w_cross_out: bfloat16 [1024, 1024], P('head'), may hold values from -0.1875 to 0.1875
- w_up: bfloat16 [1024, 8192], P(None, 'head'), may hold values from -0.1875 to 0.1875
- w_down: bfloat16 [8192, 1024], P('head'), may hold values from -0.0625 to 0.0625
Outputs:
- layer_out: bfloat16 [4, 256, 1024], P('grp', ('tok', 'head'))
Inputs may be any that keep to these rules, and one draw needn't show every extreme that they name: Each group's 8 lengths sum to 256; the longest is exactly 192. `block_position`: each group's row is a permutation of 0 to 31.
All inputs are finite; a program needn't handle non-finite values.
Results may differ from a plain program's by a relative error of at most 0.034.
The roundings to bfloat16 on the way count: a program that leaves them out, or rounds other values in their place, can miss the bound.
Values may be sent and summed in bfloat16 or wider, within the bound.
No kernel may reach another device: no remote copies, remote signals or barrier semaphores. Data moves between devices by JAX's collectives and lax.ppermute only.
A program may use at most 128 MiB of HBM per device.

v0:
```python
import jax
import jax.numpy as jnp
from jax import lax
from jax.sharding import PartitionSpec as P

HEAD_DIM = 64
SPAN = 8
SINK = 4
WINDOW = 1024


eps = 1e-05
masked = -1e30


def from_behind(array, axis, by):
    count = lax.axis_size(axis)
    pairs = [(i, i + by) for i in range(count) if 0 <= i + by < count]
    return lax.ppermute(array, axis, pairs)


def layer_norm(values):
    center = values - jnp.mean(values, axis=-1, keepdims=True)
    spread = jnp.mean(center * center, axis=-1, keepdims=True)
    return center * lax.rsqrt(spread + eps)


def request_info(token_ids, lengths_row):
    request_ends = jnp.cumsum(lengths_row, dtype=jnp.int32)
    before = request_ends[None, :] <= token_ids[:, None]
    request = jnp.sum(before.astype(jnp.int32), axis=1, dtype=jnp.int32)
    first_token = jnp.sum(jnp.where(before, lengths_row[None, :], 0), axis=1, dtype=jnp.int32)
    return (request, token_ids - first_token)


def attend_block(queries, key_heads, value_heads, allowed, score_scale):
    scores = (
        jnp.einsum("qhd,khd->hqk", queries, key_heads, preferred_element_type=jnp.float32)
        * score_scale
    )
    scores = jnp.where(allowed[None], scores, masked)
    row_max = jnp.max(scores, axis=-1)
    weights = jnp.where(allowed[None], jnp.exp(scores - row_max[..., None]), 0.0)
    row_sum = jnp.sum(weights, axis=-1)
    summed = jnp.einsum(
        "hqk,khd->hqd",
        weights.astype(jnp.bfloat16),
        value_heads,
        preferred_element_type=jnp.float32,
    )
    return (row_max, row_sum, summed)


def combine(earlier, later):
    row_max = jnp.maximum(earlier[0], later[0])
    left_scale = jnp.exp(earlier[0] - row_max)
    right_scale = jnp.exp(later[0] - row_max)
    row_sum = earlier[1] * left_scale + later[1] * right_scale
    summed = earlier[2] * left_scale[..., None] + later[2] * right_scale[..., None]
    return (row_max, row_sum, summed)


def finish(partial_value, row_count, group_width):
    result = partial_value[2] / partial_value[1][..., None]
    return jnp.transpose(result, (1, 0, 2)).reshape(row_count, group_width).astype(jnp.bfloat16)


def on_device(
    tokens,
    lengths,
    block_position,
    prefix_pool,
    cross_cache,
    w_query,
    w_keyvalue,
    w_out,
    w_cross_query,
    w_cross_out,
    w_up,
    w_down,
):
    row_total = tokens.shape[1]
    model_width = tokens.shape[2]
    group_width = w_query.shape[1]
    heads_here = group_width // HEAD_DIM
    score_scale = HEAD_DIM ** (-0.5)
    tok_index = lax.axis_index("tok")
    head_index = lax.axis_index("head")
    head_count = lax.axis_size("head")
    tok_count = lax.axis_size("tok")
    share_rows = row_total // head_count
    lengths_row = lengths[0]
    residual = tokens[0].astype(jnp.float32)
    normed = layer_norm(residual).astype(jnp.bfloat16)
    queries = (
        jnp.dot(normed, w_query, preferred_element_type=jnp.float32)
        .astype(jnp.bfloat16)
        .reshape(row_total, heads_here, HEAD_DIM)
    )
    keyvalue = (
        jnp.dot(
            normed,
            w_keyvalue.reshape(model_width, 2 * group_width),
            preferred_element_type=jnp.float32,
        )
        .astype(jnp.bfloat16)
        .reshape(row_total, 2, group_width)
    )
    own_ids = tok_index * row_total + jnp.arange(row_total, dtype=jnp.int32)
    own_request, own_offset = request_info(own_ids, lengths_row)
    key_blocks = [keyvalue]
    key_ids = [own_ids]
    for distance in range(1, min(SPAN, tok_count - 1) + 1):
        key_blocks.append(from_behind(keyvalue, "tok", distance))
        key_ids.append((tok_index - distance) * row_total + jnp.arange(row_total, dtype=jnp.int32))
    near_keys = jnp.concatenate(key_blocks, axis=0)
    near_ids = jnp.concatenate(key_ids, axis=0)
    near_request = request_info(near_ids, lengths_row)[0]
    near_allowed = (
        (near_ids[None, :] >= 0)
        & (near_request[None, :] == own_request[:, None])
        & (near_ids[None, :] <= own_ids[:, None])
        & (own_ids[:, None] - near_ids[None, :] < WINDOW)
    )
    suffix_part = attend_block(
        queries,
        near_keys[:, 0].reshape(-1, heads_here, HEAD_DIM),
        near_keys[:, 1].reshape(-1, heads_here, HEAD_DIM),
        near_allowed,
        score_scale,
    )
    blocks_total = block_position.shape[1]
    block_len = prefix_pool.shape[2]
    prefix_len = blocks_total * block_len
    block_table = block_position[0]
    start_carry = (
        jnp.full((heads_here, row_total), masked, jnp.float32),
        jnp.zeros((heads_here, row_total), jnp.float32),
        jnp.zeros((heads_here, row_total, HEAD_DIM), jnp.float32),
    )
    columns = lax.dynamic_slice_in_dim(
        lax.all_gather(prefix_pool, ("tok", "head"), axis=1, tiled=True)[0],
        head_index * group_width,
        group_width,
        3,
    )
    slot_blocks = columns.shape[0]
    physical = jnp.arange(slot_blocks, dtype=jnp.int32)
    logical = jnp.sum(
        jnp.where(
            physical[:, None] == jnp.arange(blocks_total, dtype=jnp.int32)[None, :],
            block_table[None, :],
            0,
        ),
        axis=1,
        dtype=jnp.int32,
    )
    places = (
        logical[:, None] * block_len + jnp.arange(block_len, dtype=jnp.int32)[None, :]
    ).reshape(-1)
    flat_slots = columns.reshape(slot_blocks * block_len, 2, heads_here, HEAD_DIM)
    allowed = (places[None, :] < SINK) | (
        places[None, :] > prefix_len + own_offset[:, None] - WINDOW
    )
    prefix_part = combine(
        start_carry, attend_block(queries, flat_slots[:, 0], flat_slots[:, 1], allowed, score_scale)
    )
    attended = finish(combine(suffix_part, prefix_part), row_total, group_width)
    cross_keys = cross_cache[0][:, 0].reshape(-1, heads_here, HEAD_DIM)
    cross_values = cross_cache[0][:, 1].reshape(-1, heads_here, HEAD_DIM)

    def heads_total(partial_term):
        return lax.psum(partial_term, "head")

    after_self = residual + heads_total(
        jnp.dot(attended, w_out, preferred_element_type=jnp.float32)
    )
    cross_query = jnp.dot(
        layer_norm(after_self).astype(jnp.bfloat16),
        w_cross_query,
        preferred_element_type=jnp.float32,
    ).astype(jnp.bfloat16)
    query_rows = cross_query.shape[0]
    allowed = jnp.ones((query_rows, cross_keys.shape[0]), dtype=bool)
    partial_value = attend_block(
        cross_query.reshape(query_rows, heads_here, HEAD_DIM),
        cross_keys,
        cross_values,
        allowed,
        score_scale,
    )
    cross_out = finish(partial_value, query_rows, group_width)
    after_cross = after_self + heads_total(
        jnp.dot(cross_out, w_cross_out, preferred_element_type=jnp.float32)
    )
    hidden = jax.nn.relu(
        jnp.dot(
            layer_norm(after_cross).astype(jnp.bfloat16), w_up, preferred_element_type=jnp.float32
        )
    ).astype(jnp.bfloat16)
    kept_rows = lax.dynamic_slice_in_dim(after_cross, head_index * share_rows, share_rows, 0)
    result = kept_rows + lax.psum_scatter(
        jnp.dot(hidden, w_down, preferred_element_type=jnp.float32),
        "head",
        scatter_dimension=0,
        tiled=True,
    )
    return result.astype(jnp.bfloat16)[None]


def solution(mesh):
    return jax.shard_map(
        on_device,
        mesh=mesh,
        in_specs=(
            P("grp", "tok", None),
            P("grp", None),
            P("grp", None),
            P("grp", ("tok", "head"), None, None, None),
            P("grp", None, None, "head"),
            P(None, "head"),
            P(None, None, "head"),
            P("head", None),
            P(None, "head"),
            P("head", None),
            P(None, "head"),
            P("head", None),
        ),
        out_specs=P("grp", ("tok", "head"), None),
        check_vma=False,
    )
```

profile of v0, /device:TPU:0, one launch (start us, length us, event | category | flops | bytes accessed | tf_op | source)
XLA Modules:
  0.0 165.3 jit_solution(2714514256199240417)
XLA Ops:
  6.6 1.8 %copy.43 = bf16[1,4,16,2,1024]{4,2,3,0,1:T(8,128)(2,1)} copy(bf16[1,4,16,2,1024]{4,3,2,1,0:T(2,128)(2,1)} %param.15) | data formatting | bytes 524288 | tf_op args[3]
  8.5 1.1 convert_reduce_fusion
  9.6 1.2 fusion.19
  10.7 1.5 copy.52
  12.2 1.3 convolution_convert_fusion
  13.6 2.4 %collective-permute-start = (bf16[128,2,256]{2,1,0:T(2,128)(2,1)S(1)}, bf16[128,2,256]{2,1,0:T(2,128)(2,1)S(1)}, u32[]{:S(2)}, u32[]{:S(2)}) collective-permute-start(bf16[128,2,256]{2,1,0:T(2,128)(2,1)S(1)} %reshape.338), channel_id=1, source_target_pairs={{0,4},{1,5},{2,6},{3,7},{8,12},{9,13},{10,14},{11,15},{16,20},{17,... | collective-permute-start | bytes 393224 | tf_op jit(solution)/shard_map/ppermute | solution.py:19
  17.6 0.4 fusion.77
  17.9 0.8 copy.42
  18.9 0.4 fusion.79
  19.5 21.4 %all-gather.2.cloned.1.call-done = bf16[1,32,16,2,1024]{4,2,3,0,1:T(8,128)(2,1)} async-done(((bf16[1,4,16,2,1024]{4,2,3,0,1:T(8,128)(2,1)}), bf16[1,32,16,2,1024]{4,2,3,0,1:T(8,128)(2,1)}) %all-gather.2.cloned.1.call-update) | async-done | bytes 2097168 | tf_op jit(solution)/shard_map/all_gather | solution.py:142
  40.9 1.1 constant_dynamic-slice_fusion
  42.0 0.4 reshape.339
  42.4 0.4 fusion.75
  42.8 0.3 copy.51
  43.1 0.3 copy.50
  43.4 0.4 fusion.78
  43.9 0.4 fusion.13
  44.3 0.4 fusion.9
  44.7 0.3 fusion.10
  45.0 1.1 fusion.81
  46.2 0.4 fusion.76
  46.8 37.2 %all-reduce.3.cloned.1.call-done = f32[128,1024]{1,0:T(8,128)} async-done(((f32[128,1024]{1,0:T(8,128)}), f32[128,1024]{1,0:T(8,128)}) %all-reduce.3.cloned.1.call-update) | async-done | bytes 524304 | tf_op jit(solution)/shard_map/psum | solution.py:173
  84.1 1.2 fusion.57
  85.3 1.2 multiply_reduce_fusion.1
  86.6 1.3 convolution_convert_fusion.1
  88.0 0.4 fusion.80
  89.0 1.1 fusion.82
  90.1 38.4 %all-reduce.5.cloned.1.call-done = f32[128,1024]{1,0:T(8,128)} async-done(((f32[128,1024]{1,0:T(8,128)}), f32[128,1024]{1,0:T(8,128)}) %all-reduce.5.cloned.1.call-update) | async-done | bytes 524304 | tf_op jit(solution)/shard_map/psum | solution.py:173
  128.5 1.2 fusion.71
  129.9 5.6 %fusion.12 = f32[128,1024]{1,0:T(8,128)} fusion(bf16[2048,1024]{1,0:T(8,128)(2,1)} %param.23, bf16[1024,2048]{1,0:T(8,128)(2,1)} %param.22, f32[128,1024]{1,0:T(8,128)S(1)} %get-tuple-element.8, f32[128]{0:T(128)S(1)} %add_rsqrt_fusion, f32[128]{0:T(128)S(1)} %broadcast_multiply_fusion.1), kind=kOutput, calls=%fused_computation.23 | convolution fusion | flops 1074659328 | bytes 9438208 | tf_op jit(solution)/shard_map/dot_general | solution.py:203
  135.5 21.8 %reduce-scatter.2.cloned.1.call-done = f32[32,1024]{1,0:T(8,128)} async-done(((f32[128,1024]{1,0:T(8,128)}), f32[32,1024]{1,0:T(8,128)}) %reduce-scatter.2.cloned.1.call-update) | async-done | bytes 131088 | tf_op jit(solution)/shard_map/reduce_scatter | solution.py:202
  157.3 1.5 fusion.54
  (68 shorter events, 3.5 us)
Async XLA Ops:
  6.5 38.5 %copy-start = (bf16[256,1024]{1,0:T(8,128)(2,1)S(1)}, bf16[256,1024]{1,0:T(8,128)(2,1)}, u32[]{:S(2)}) copy-start(bf16[256,1024]{1,0:T(8,128)(2,1)} %param.19) | copy-start | bytes 1572868
  6.5 10.2 %copy-start.1 = (bf16[1,128,1024]{2,1,0:T(8,128)(2,1)S(1)}, bf16[1,128,1024]{2,1,0:T(8,128)(2,1)}, u32[]{:S(2)}) copy-start(bf16[1,128,1024]{2,1,0:T(8,128)(2,1)} %param.12) | copy-start | bytes 786436
  6.5 9.4 %copy-start.11 = (s32[1,32]{1,0:T(1,128)S(1)}, s32[1,32]{1,0:T(1,128)}, u32[]{:S(2)}) copy-start(s32[1,32]{1,0:T(1,128)} %param.14) | copy-start | bytes 388
  6.5 9.7 %copy-start.9 = (s32[1,8]{1,0:T(1,128)S(1)}, s32[1,8]{1,0:T(1,128)}, u32[]{:S(2)}) copy-start(s32[1,8]{1,0:T(1,128)} %param.13) | copy-start | bytes 100
  6.5 10.2 %copy-start.10 = (bf16[1024,256]{1,0:T(8,128)(2,1)S(1)}, bf16[1024,256]{1,0:T(8,128)(2,1)}, u32[]{:S(2)}) copy-start(bf16[1024,256]{1,0:T(8,128)(2,1)} %param.17) | copy-start | bytes 1572868
  6.5 34.3 %all-gather.2.cloned.1.call-start = ((), (), s32[]{:S(2)}) async-start(), calls=%async_computation.1 | async-start | bytes 2359296 | tf_op jit(solution)/shard_map/all_gather | solution.py:142
  8.4 75.6 %all-reduce.3.cloned.1.call-start = ((), (), s32[]{:S(2)}) async-start(), calls=%async_computation.2 | async-start | bytes 1048576 | tf_op jit(solution)/shard_map/psum | solution.py:173
  13.6 3.9 %collective-permute-start = (bf16[128,2,256]{2,1,0:T(2,128)(2,1)S(1)}, bf16[128,2,256]{2,1,0:T(2,128)(2,1)S(1)}, u32[]{:S(2)}, u32[]{:S(2)}) collective-permute-start(bf16[128,2,256]{2,1,0:T(2,128)(2,1)S(1)} %reshape.338), channel_id=1, source_target_pairs={{0,4},{1,5},{2,6},{3,7},{8,12},{9,13},{10,14},{11,15},{16,20},{17,... | collective-permute-start | bytes 393224 | tf_op jit(solution)/shard_map/ppermute | solution.py:19
  17.2 24.8 %copy-start.6 = (pred[128,256]{1,0:T(8,128)(4,1)}, pred[128,256]{1,0:T(8,128)(4,1)S(1)}, u32[]{:S(2)}) copy-start(pred[128,256]{1,0:T(8,128)(4,1)S(1)} %fusion.53) | copy-start | bytes 98308
  42.8 1.9 %copy-start.7 = (pred[128,256]{1,0:T(8,128)(4,1)S(1)}, pred[128,256]{1,0:T(8,128)(4,1)}, u32[]{:S(2)}) copy-start(pred[128,256]{1,0:T(8,128)(4,1)} %copy-done.6) | copy-start | bytes 98308
  42.8 1.9 %copy-start.8 = (bf16[256,1,256]{0,2,1:T(8,128)(2,1)S(1)}, bf16[256,1,256]{0,2,1:T(8,128)(2,1)}, u32[]{:S(2)}) copy-start(bf16[256,1,256]{0,2,1:T(8,128)(2,1)} %copy.42) | copy-start | bytes 393220
  43.1 3.0 %copy-start.3 = (bf16[1,256,2,256]{3,2,1,0:T(2,128)(2,1)S(1)}, bf16[1,256,2,256]{3,2,1,0:T(2,128)(2,1)}, u32[]{:S(2)}) copy-start(bf16[1,256,2,256]{3,2,1,0:T(2,128)(2,1)} %param.16) | copy-start | bytes 786436
  44.2 42.4 %copy-start.4 = (bf16[1024,256]{1,0:T(8,128)(2,1)S(1)}, bf16[1024,256]{1,0:T(8,128)(2,1)}, u32[]{:S(2)}) copy-start(bf16[1024,256]{1,0:T(8,128)(2,1)} %param.20) | copy-start | bytes 1572868
  45.0 44.0 %copy-start.5 = (bf16[256,1024]{1,0:T(8,128)(2,1)S(1)}, bf16[256,1024]{1,0:T(8,128)(2,1)}, u32[]{:S(2)}) copy-start(bf16[256,1024]{1,0:T(8,128)(2,1)} %param.21) | copy-start | bytes 1572868
  46.1 82.4 %all-reduce.5.cloned.1.call-start = ((), (), s32[]{:S(2)}) async-start(), calls=%async_computation.3 | async-start | bytes 1048576 | tf_op jit(solution)/shard_map/psum | solution.py:173
  84.1 44.4 %copy-start.2 = (f32[128,1024]{1,0:T(8,128)S(1)}, f32[128,1024]{1,0:T(8,128)}, u32[]{:S(2)}) copy-start(f32[128,1024]{1,0:T(8,128)} %all-reduce.3.cloned.1.call-done) | copy-start | bytes 1572868
  90.0 67.2 %reduce-scatter.2.cloned.1.call-start = ((), (), s32[]{:S(2)}) async-start(), calls=%async_computation.4 | async-start | bytes 655360 | tf_op jit(solution)/shard_map/reduce_scatter | solution.py:202
Sparse Core Ops, SparseCore 0:
  9.0 31.8 all-gather.1
  46.2 37.7 all-reduce.2
  90.2 38.2 all-reduce.4
  135.6 21.6 reduce-scatter.1
where the time goes:
time: 166 us; the launch traced here: 165 us
  waiting for transfers between devices  119 us (72%)
  between operations  13.5 us (8%)
  matrix products  12.8 us (8%)
  other arithmetic  9.43 us (6%)
  local copies, waits for them, and re-layouts  8.31 us (5%)
  starting transfers between devices  2.53 us (2%)
    psum x2, waiting for transfers between devices, heads_total(): return lax.psum(partial_term, 'head')  75.6 us
    reduce_scatter x1, waiting for transfers between devices, on_device(): lax.psum_scatter(jnp.dot(hidden, w_down, preferred_element_type=jnp.float...  21.8 us
    all_gather x1, waiting for transfers between devices, on_device(): lax.all_gather(prefix_pool, ('tok', 'head'), axis=1, tiled=True)[0]  21.4 us
    dot_general x1, matrix products, on_device(): jnp.dot(hidden, w_down, preferred_element_type=jnp.float32)  5.57 us
    unnamed x29, local copies, waits for them, and re-layouts  4.02 us
    reduce_sum x3, other arithmetic, layer_norm(): center = values - jnp.mean(values, axis=-1, keepdims=True)  3.51 us
  transfers between devices with their start and end apart: 5, of which 4 were waited for; matrix products, arithmetic and copies ran while one was open for 6% of the time, Pallas kernels for 0%

commit v1 on v0

--- a/solution.py
+++ b/solution.py
@@ -17,6 +17,20 @@
     count = lax.axis_size(axis)
     pairs = [(i, i + by) for i in range(count) if 0 <= i + by < count]
     return lax.ppermute(array, axis, pairs)
+
+
+def swap(array, axis, by):
+    count = lax.axis_size(axis)
+    return lax.ppermute(array, axis, [(i, i ^ by) for i in range(count)])
+
+
+def gather_heads(array):
+    count = lax.axis_size("head")
+    return [array] + [swap(array, "head", by) for by in range(1, count)]
+
+
+def scatter_heads(pieces):
+    return pieces[:1] + [swap(piece, "head", by) for by, piece in enumerate(pieces) if by]
 
 
 def layer_norm(values):
@@ -138,14 +152,27 @@
         jnp.zeros((heads_here, row_total), jnp.float32),
         jnp.zeros((heads_here, row_total, HEAD_DIM), jnp.float32),
     )
-    columns = lax.dynamic_slice_in_dim(
-        lax.all_gather(prefix_pool, ("tok", "head"), axis=1, tiled=True)[0],
-        head_index * group_width,
-        group_width,
-        3,
+    shard_blocks = prefix_pool.shape[1]
+    own_pool = prefix_pool[0]
+    pieces = scatter_heads(
+        [
+            lax.dynamic_slice_in_dim(own_pool, (head_index ^ by) * group_width, group_width, 3)
+            for by in range(head_count)
+        ]
+    )
+    own_columns = jnp.concatenate(pieces, axis=0)
+    columns = jnp.concatenate(
+        [own_columns] + [swap(own_columns, "tok", by) for by in range(1, tok_count)], axis=0
     )
     slot_blocks = columns.shape[0]
-    physical = jnp.arange(slot_blocks, dtype=jnp.int32)
+    physical = jnp.concatenate(
+        [
+            ((tok_index ^ far) * head_count + (head_index ^ by)) * shard_blocks
+            + jnp.arange(shard_blocks, dtype=jnp.int32)
+            for far in range(tok_count)
+            for by in range(head_count)
+        ]
+    )
     logical = jnp.sum(
         jnp.where(
             physical[:, None] == jnp.arange(blocks_total, dtype=jnp.int32)[None, :],
@@ -169,14 +196,20 @@
     cross_keys = cross_cache[0][:, 0].reshape(-1, heads_here, HEAD_DIM)
     cross_values = cross_cache[0][:, 1].reshape(-1, heads_here, HEAD_DIM)
 
+    def row_share(array, by):
+        return lax.dynamic_slice_in_dim(array, (head_index ^ by) * share_rows, share_rows, 0)
+
     def heads_total(partial_term):
-        return lax.psum(partial_term, "head")
-
-    after_self = residual + heads_total(
+        partial_term = partial_term.astype(jnp.bfloat16)
+        terms = scatter_heads([row_share(partial_term, by) for by in range(head_count)])
+        return sum(term.astype(jnp.float32) for term in terms)
+
+    after_self = row_share(residual, 0) + heads_total(
         jnp.dot(attended, w_out, preferred_element_type=jnp.float32)
     )
+    normed_cross = jnp.concatenate(gather_heads(layer_norm(after_self).astype(jnp.bfloat16)), 0)
     cross_query = jnp.dot(
-        layer_norm(after_self).astype(jnp.bfloat16),
+        normed_cross,
         w_cross_query,
         preferred_element_type=jnp.float32,
     ).astype(jnp.bfloat16)
@@ -190,21 +223,22 @@
         score_scale,
     )
     cross_out = finish(partial_value, query_rows, group_width)
-    after_cross = after_self + heads_total(
-        jnp.dot(cross_out, w_cross_out, preferred_element_type=jnp.float32)
-    )
+    cross_partial = jnp.dot(cross_out, w_cross_out, preferred_element_type=jnp.float32).astype(
+        jnp.bfloat16
+    )
+    cross_terms = scatter_heads(
+        [cross_partial[by * share_rows : (by + 1) * share_rows] for by in range(head_count)]
+    )
+    after_cross = after_self + sum(term.astype(jnp.float32) for term in cross_terms)
+    normed_hidden = jnp.concatenate(gather_heads(layer_norm(after_cross).astype(jnp.bfloat16)), 0)
     hidden = jax.nn.relu(
-        jnp.dot(
-            layer_norm(after_cross).astype(jnp.bfloat16), w_up, preferred_element_type=jnp.float32
-        )
+        jnp.dot(normed_hidden, w_up, preferred_element_type=jnp.float32)
     ).astype(jnp.bfloat16)
-    kept_rows = lax.dynamic_slice_in_dim(after_cross, head_index * share_rows, share_rows, 0)
-    result = kept_rows + lax.psum_scatter(
-        jnp.dot(hidden, w_down, preferred_element_type=jnp.float32),
-        "head",
-        scatter_dimension=0,
-        tiled=True,
-    )
+    down = jnp.dot(hidden, w_down, preferred_element_type=jnp.float32).astype(jnp.bfloat16)
+    down_terms = scatter_heads(
+        [down[by * share_rows : (by + 1) * share_rows] for by in range(head_count)]
+    )
+    result = after_cross + sum(term.astype(jnp.float32) for term in down_terms)
     return result.astype(jnp.bfloat16)[None]
 
 

time: 166 us -> 73.5 us (0.44)
  waiting for transfers between devices: 119 us -> 21.2 us
  starting transfers between devices: 2.53 us -> 29.5 us
  between operations: 13.5 us -> 0.68 us
  other arithmetic: 9.43 us -> 5.69 us
  matrix products: 12.8 us -> 9.2 us
    psum x2 -> x0, waiting for transfers between devices: 75.6 us -> none  [heads_total(): return lax.psum(partial_term, 'head')]
    ppermute x0 -> x19, starting transfers between devices: none -> 28.2 us  [swap(): return lax.ppermute(array, axis, [(i, i ^ by) for i in range(count)])]
    reduce_scatter x1 -> x0, waiting for transfers between devices: 21.8 us -> none  [on_device(): lax.psum_scatter(jnp.dot(hidden, w_down, preferred_element_type=jnp.float...]
    all_gather x1 -> x0, waiting for transfers between devices: 21.4 us -> none  [on_device(): lax.all_gather(prefix_pool, ('tok', 'head'), axis=1, tiled=True)[0]]
    ppermute x0 -> x19, waiting for transfers between devices: none -> 21.2 us  [swap(): return lax.ppermute(array, axis, [(i, i ^ by) for i in range(count)])]
    reduce_sum x3, other arithmetic: 3.51 us -> 1.36 us  [layer_norm(): center = values - jnp.mean(values, axis=-1, keepdims=True)]
    unnamed x29 -> x34, local copies, waits for them, and re-layouts: 4.02 us -> 2.27 us
  transfers between devices with their start and end apart: 5 -> 20, of which waited for: 4 -> 10; matrix products, arithmetic and copies ran while one was open for 6% -> 13% of each run, Pallas kernels for 0% -> 0%
where the time goes in v1:
time: 73.5 us; the launch traced here: 73.2 us
  starting transfers between devices  29.5 us (40%)
  waiting for transfers between devices  21.2 us (29%)
  matrix products  9.2 us (13%)
  local copies, waits for them, and re-layouts  6.87 us (9%)
  other arithmetic  5.69 us (8%)
    ppermute x19, starting transfers between devices, swap(): return lax.ppermute(array, axis, [(i, i ^ by) for i in range(count)])  28.2 us
    ppermute x19, waiting for transfers between devices, swap(): return lax.ppermute(array, axis, [(i, i ^ by) for i in range(count)])  21.2 us
    dot_general x1, matrix products, on_device(): jnp.dot(hidden, w_down, preferred_element_type=jnp.float32)  4.74 us
    unnamed x34, local copies, waits for them, and re-layouts  2.27 us
    reduce_sum x3, other arithmetic, layer_norm(): spread = jnp.mean(center * center, axis=-1, keepdims=True)  1.55 us
  transfers between devices with their start and end apart: 20, of which 10 were waited for; matrix products, arithmetic and copies ran while one was open for 13% of the time, Pallas kernels for 0%

profile of v1, /device:TPU:0, one launch (start us, length us, event | category | flops | bytes accessed | tf_op | source)
XLA Modules:
  0.0 73.2 jit_solution(6423853906584385170)
XLA Ops:
  0.0 1.2 %constant_dynamic-slice_fusion.3 = (bf16[1,4,16,2,256]{4,3,2,1,0:T(2,128)(2,1)S(1)}, bf16[1,4,16,2,256]{4,3,2,1,0:T(2,128)(2,1)S(1)}, bf16[1,4,16,2,256]{4,3,2,1,0:T(2,128)(2,1)S(1)}, bf16[1,4,16,2,256]{4,3,2,1,0:T(2,128)(2,1)S(1)}) fusion(bf16[1,4,16,2,1024]{4,3,2,1,0:T(2,128)(2,1)} %param.15, s32[]{:T(128)S(6)} %select_n.57, s32[]{:T(128)S(6)} %select_n.56, ...), kind=kLoop, calls=%fused_computation.106 | loop fusion | bytes 524304 | tf_op jit(solution)/shard_map/dynamic_slice | solution.py:159
  1.3 3.1 %collective-permute-start.1 = (bf16[4,16,2,256]{3,1,2,0:T(8,128)(2,1)S(1)}, bf16[4,16,2,256]{3,1,2,0:T(8,128)(2,1)S(1)}, u32[]{:S(2)}, u32[]{:S(2)}) collective-permute-start(bf16[4,16,2,256]{3,1,2,0:T(8,128)(2,1)S(1)} %bitcast.136), channel_id=1, source_target_pairs={{0,1},{1,0},{2,3},{3,2},{4,5},{5,4},{6,7},{7,6},{8,9},{9,8},{10,11... | collective-permute-start | bytes 196616 | tf_op jit(solution)/shard_map/ppermute | solution.py:24
  4.4 2.7 %collective-permute-start.2 = (bf16[4,16,2,256]{3,1,2,0:T(8,128)(2,1)S(1)}, bf16[4,16,2,256]{3,1,2,0:T(8,128)(2,1)S(1)}, u32[]{:S(2)}, u32[]{:S(2)}) collective-permute-start(bf16[4,16,2,256]{3,1,2,0:T(8,128)(2,1)S(1)} %bitcast.137), channel_id=1, source_target_pairs={{0,2},{1,3},{2,0},{3,1},{4,6},{5,7},{6,4},{7,5},{8,10},{9,11},{10,... | collective-permute-start | bytes 196616 | tf_op jit(solution)/shard_map/ppermute | solution.py:24
  7.1 1.1 %convert_reduce_fusion = f32[128]{0:T(128)S(1)} fusion(bf16[1,128,1024]{2,1,0:T(8,128)(2,1)} %param.12), kind=kLoop, calls=%fused_computation.38 | loop fusion | flops 262016 | bytes 262656 | tf_op jit(solution)/shard_map/reduce_sum | solution.py:37
  8.2 1.2 %multiply_reduce_fusion = f32[128]{0:T(128)S(1)} fusion(bf16[1,128,1024]{2,1,0:T(8,128)(2,1)} %param.12, f32[128]{0:T(128)S(1)} %broadcast_multiply_fusion.3), kind=kLoop, calls=%fused_computation.36 | loop fusion | flops 524160 | bytes 263168 | tf_op jit(solution)/shard_map/reduce_sum | solution.py:38
  9.4 1.5 %copy.52 = bf16[128,8,2,256]{3,1,2,0:T(8,128)(2,1)S(1)} copy(bf16[128,8,2,256]{3,2,1,0:T(2,128)(2,1)} %bitcast.126) | data formatting | bytes 2097152
  10.9 1.3 %convolution_convert_fusion.3 = bf16[128,512]{1,0:T(8,128)(2,1)S(1)} fusion(bf16[1024,512]{1,0:T(8,128)(2,1)S(1)} %bitcast.125, bf16[1,128,1024]{2,1,0:T(8,128)(2,1)} %param.12, f32[128]{0:T(128)S(1)} %add_rsqrt_fusion.2, f32[128]{0:T(128)S(1)} %broadcast_multiply_fusion.3), kind=kOutput, calls=%fused_computation.10 | convolution fusion | flops 134807552 | bytes 1442816 | tf_op jit(solution)/shard_map/dot_general | solution.py:115
  12.2 1.3 %collective-permute-start = (bf16[128,2,256]{2,1,0:T(2,128)(2,1)S(1)}, bf16[128,2,256]{2,1,0:T(2,128)(2,1)S(1)}, u32[]{:S(2)}, u32[]{:S(2)}) collective-permute-start(bf16[128,2,256]{2,1,0:T(2,128)(2,1)S(1)} %reshape.342), channel_id=1, source_target_pairs={{0,4},{1,5},{2,6},{3,7},{8,12},{9,13},{10,14},{11,15},{16,20},{17,... | collective-permute-start | bytes 393224 | tf_op jit(solution)/shard_map/ppermute | solution.py:19
  16.5 0.8 %copy.35 = bf16[256,1,256]{0,2,1:T(8,128)(2,1)} copy(bf16[256,1,256]{2,1,0:T(2,128)(2,1)S(1)} %get-tuple-element.27) | data formatting | bytes 262144 | tf_op jit(solution)/shard_map/slice | solution.py:142
  21.0 3.9 %collective-permute-start.7 = (bf16[32,1024]{1,0:T(8,128)(2,1)S(1)}, bf16[32,1024]{1,0:T(8,128)(2,1)S(1)}, u32[]{:S(2)}, u32[]{:S(2)}) collective-permute-start(bf16[32,1024]{1,0:T(8,128)(2,1)S(1)} %get-tuple-element.25), channel_id=1, source_target_pairs={{0,3},{1,2},{2,1},{3,0},{4,7},{5,6},{6,5},{7,4},{8,11},{9,10},{10,... | collective-permute-start | bytes 196616 | tf_op jit(solution)/shard_map/ppermute | solution.py:24
  24.8 0.6 collective-permute-start.5
  25.5 2.3 %collective-permute-done.7 = bf16[32,1024]{1,0:T(8,128)(2,1)S(1)} collective-permute-done((bf16[32,1024]{1,0:T(8,128)(2,1)S(1)}, bf16[32,1024]{1,0:T(8,128)(2,1)S(1)}, u32[]{:S(2)}, u32[]{:S(2)}) %collective-permute-start.7) | collective-permute-done | bytes 65568 | tf_op jit(solution)/shard_map/ppermute | solution.py:24
  27.8 2.7 %collective-permute-done.6 = bf16[32,1024]{1,0:T(8,128)(2,1)S(1)} collective-permute-done((bf16[32,1024]{1,0:T(8,128)(2,1)S(1)}, bf16[32,1024]{1,0:T(8,128)(2,1)S(1)}, u32[]{:S(2)}, u32[]{:S(2)}) %collective-permute-start.6) | collective-permute-done | bytes 65568 | tf_op jit(solution)/shard_map/ppermute | solution.py:24
  31.0 2.7 %collective-permute-start.10 = (bf16[32,1024]{1,0:T(8,128)(2,1)S(1)}, bf16[32,1024]{1,0:T(8,128)(2,1)S(1)}, u32[]{:S(2)}, u32[]{:S(2)}) collective-permute-start(bf16[32,1024]{1,0:T(8,128)(2,1)S(1)} %multiply_convert_fusion.4), channel_id=1, source_target_pairs={{0,3},{1,2},{2,1},{3,0},{4,7},{5,6},{6,5},{7,4},{8,11},{9,10},{10,... | collective-permute-start | bytes 196616 | tf_op jit(solution)/shard_map/ppermute | solution.py:24
  33.6 0.5 collective-permute-start.9
  34.2 1.3 %collective-permute-start.8 = (bf16[32,1024]{1,0:T(8,128)(2,1)S(1)}, bf16[32,1024]{1,0:T(8,128)(2,1)S(1)}, u32[]{:S(2)}, u32[]{:S(2)}) collective-permute-start(bf16[32,1024]{1,0:T(8,128)(2,1)S(1)} %multiply_convert_fusion.4), channel_id=1, source_target_pairs={{0,1},{1,0},{2,3},{3,2},{4,5},{5,4},{6,7},{7,6},{8,9},{9,8},{10,11... | collective-permute-start | bytes 196616 | tf_op jit(solution)/shard_map/ppermute | solution.py:24
  36.1 1.2 %collective-permute-done.10 = bf16[32,1024]{1,0:T(8,128)(2,1)S(1)} collective-permute-done((bf16[32,1024]{1,0:T(8,128)(2,1)S(1)}, bf16[32,1024]{1,0:T(8,128)(2,1)S(1)}, u32[]{:S(2)}, u32[]{:S(2)}) %collective-permute-start.10) | collective-permute-done | bytes 65568 | tf_op jit(solution)/shard_map/ppermute | solution.py:24
  37.4 2.7 %collective-permute-done.9 = bf16[32,1024]{1,0:T(8,128)(2,1)S(1)} collective-permute-done((bf16[32,1024]{1,0:T(8,128)(2,1)S(1)}, bf16[32,1024]{1,0:T(8,128)(2,1)S(1)}, u32[]{:S(2)}, u32[]{:S(2)}) %collective-permute-start.9) | collective-permute-done | bytes 65568 | tf_op jit(solution)/shard_map/ppermute | solution.py:24
  41.6 2.0 %collective-permute-start.13 = (bf16[32,1024]{1,0:T(8,128)(2,1)S(1)}, bf16[32,1024]{1,0:T(8,128)(2,1)S(1)}, u32[]{:S(2)}, u32[]{:S(2)}) collective-permute-start(bf16[32,1024]{1,0:T(8,128)(2,1)S(1)} %get-tuple-element.20), channel_id=1, source_target_pairs={{0,3},{1,2},{2,1},{3,0},{4,7},{5,6},{6,5},{7,4},{8,11},{9,10},{10,... | collective-permute-start | bytes 196616 | tf_op jit(solution)/shard_map/ppermute | solution.py:24
  43.7 2.4 %collective-permute-start.11 = (bf16[32,1024]{1,0:T(8,128)(2,1)S(1)}, bf16[32,1024]{1,0:T(8,128)(2,1)S(1)}, u32[]{:S(2)}, u32[]{:S(2)}) collective-permute-start(bf16[32,1024]{1,0:T(8,128)(2,1)S(1)} %get-tuple-element.19), channel_id=1, source_target_pairs={{0,1},{1,0},{2,3},{3,2},{4,5},{5,4},{6,7},{7,6},{8,9},{9,8},{10,11... | collective-permute-start | bytes 196616 | tf_op jit(solution)/shard_map/ppermute | solution.py:24
  46.1 1.7 %collective-permute-done.13 = bf16[32,1024]{1,0:T(8,128)(2,1)S(1)} collective-permute-done((bf16[32,1024]{1,0:T(8,128)(2,1)S(1)}, bf16[32,1024]{1,0:T(8,128)(2,1)S(1)}, u32[]{:S(2)}, u32[]{:S(2)}) %collective-permute-start.13) | collective-permute-done | bytes 65568 | tf_op jit(solution)/shard_map/ppermute | solution.py:24
  47.8 2.1 %collective-permute-done.12 = bf16[32,1024]{1,0:T(8,128)(2,1)S(1)} collective-permute-done((bf16[32,1024]{1,0:T(8,128)(2,1)S(1)}, bf16[32,1024]{1,0:T(8,128)(2,1)S(1)}, u32[]{:S(2)}, u32[]{:S(2)}) %collective-permute-start.12) | collective-permute-done | bytes 65568 | tf_op jit(solution)/shard_map/ppermute | solution.py:24
  50.3 2.4 %collective-permute-start.16 = (bf16[32,1024]{1,0:T(8,128)(2,1)S(1)}, bf16[32,1024]{1,0:T(8,128)(2,1)S(1)}, u32[]{:S(2)}, u32[]{:S(2)}) collective-permute-start(bf16[32,1024]{1,0:T(8,128)(2,1)S(1)} %multiply_convert_fusion.3), channel_id=1, source_target_pairs={{0,3},{1,2},{2,1},{3,0},{4,7},{5,6},{6,5},{7,4},{8,11},{9,10},{10,... | collective-permute-start | bytes 196616 | tf_op jit(solution)/shard_map/ppermute | solution.py:24
  52.7 2.1 %collective-permute-start.14 = (bf16[32,1024]{1,0:T(8,128)(2,1)S(1)}, bf16[32,1024]{1,0:T(8,128)(2,1)S(1)}, u32[]{:S(2)}, u32[]{:S(2)}) collective-permute-start(bf16[32,1024]{1,0:T(8,128)(2,1)S(1)} %multiply_convert_fusion.3), channel_id=1, source_target_pairs={{0,1},{1,0},{2,3},{3,2},{4,5},{5,4},{6,7},{7,6},{8,9},{9,8},{10,11... | collective-permute-start | bytes 196616 | tf_op jit(solution)/shard_map/ppermute | solution.py:24
  54.8 2.3 %collective-permute-done.16 = bf16[32,1024]{1,0:T(8,128)(2,1)S(1)} collective-permute-done((bf16[32,1024]{1,0:T(8,128)(2,1)S(1)}, bf16[32,1024]{1,0:T(8,128)(2,1)S(1)}, u32[]{:S(2)}, u32[]{:S(2)}) %collective-permute-start.16) | collective-permute-done | bytes 65568 | tf_op jit(solution)/shard_map/ppermute | solution.py:24
  57.1 2.0 %collective-permute-done.15 = bf16[32,1024]{1,0:T(8,128)(2,1)S(1)} collective-permute-done((bf16[32,1024]{1,0:T(8,128)(2,1)S(1)}, bf16[32,1024]{1,0:T(8,128)(2,1)S(1)}, u32[]{:S(2)}, u32[]{:S(2)}) %collective-permute-start.15) | collective-permute-done | bytes 65568 | tf_op jit(solution)/shard_map/ppermute | solution.py:24
  59.1 4.7 %convolution_convert_fusion.2 = bf16[128,1024]{1,0:T(8,128)(2,1)S(1)} fusion(bf16[2048,1024]{1,0:T(8,128)(2,1)} %param.23, bf16[1024,2048]{1,0:T(8,128)(2,1)} %param.22, bf16[32,1024]{1,0:T(8,128)(2,1)S(1)} %collective-permute-done.16, bf16[32,1024]{1,0:T(8,128)(2,1)S(1)} %collective-permute-done.15, bf16[32,1024]{1,0:T(8,128)(2,1)S(1)} %collective-permute-done.14, ...), kind=kOutput, calls=%fused_computation.9 | convolution fusion | flops 1075445760 | bytes 8912896 | tf_op jit(solution)/shard_map/dot_general | solution.py:237
  63.8 2.3 %collective-permute-start.19 = (bf16[32,1024]{1,0:T(8,128)(2,1)S(1)}, bf16[32,1024]{1,0:T(8,128)(2,1)S(1)}, u32[]{:S(2)}, u32[]{:S(2)}) collective-permute-start(bf16[32,1024]{1,0:T(8,128)(2,1)S(1)} %get-tuple-element.17), channel_id=1, source_target_pairs={{0,3},{1,2},{2,1},{3,0},{4,7},{5,6},{6,5},{7,4},{8,11},{9,10},{10,... | collective-permute-start | bytes 196616 | tf_op jit(solution)/shard_map/ppermute | solution.py:24
  66.2 2.1 %collective-permute-start.17 = (bf16[32,1024]{1,0:T(8,128)(2,1)S(1)}, bf16[32,1024]{1,0:T(8,128)(2,1)S(1)}, u32[]{:S(2)}, u32[]{:S(2)}) collective-permute-start(bf16[32,1024]{1,0:T(8,128)(2,1)S(1)} %get-tuple-element.16), channel_id=1, source_target_pairs={{0,1},{1,0},{2,3},{3,2},{4,5},{5,4},{6,7},{7,6},{8,9},{9,8},{10,11... | collective-permute-start | bytes 196616 | tf_op jit(solution)/shard_map/ppermute | solution.py:24
  68.3 2.2 %collective-permute-done.19 = bf16[32,1024]{1,0:T(8,128)(2,1)S(1)} collective-permute-done((bf16[32,1024]{1,0:T(8,128)(2,1)S(1)}, bf16[32,1024]{1,0:T(8,128)(2,1)S(1)}, u32[]{:S(2)}, u32[]{:S(2)}) %collective-permute-start.19) | collective-permute-done | bytes 65568 | tf_op jit(solution)/shard_map/ppermute | solution.py:24
  70.5 2.0 %collective-permute-done.18 = bf16[32,1024]{1,0:T(8,128)(2,1)S(1)} collective-permute-done((bf16[32,1024]{1,0:T(8,128)(2,1)S(1)}, bf16[32,1024]{1,0:T(8,128)(2,1)S(1)}, u32[]{:S(2)}, u32[]{:S(2)}) %collective-permute-start.18) | collective-permute-done | bytes 65568 | tf_op jit(solution)/shard_map/ppermute | solution.py:24
  72.5 0.7 fusion.59
  (112 shorter events, 9.5 us)
Async XLA Ops:
  0.0 20.7 %copy-start = (bf16[256,1024]{1,0:T(8,128)(2,1)S(1)}, bf16[256,1024]{1,0:T(8,128)(2,1)}, u32[]{:S(2)}) copy-start(bf16[256,1024]{1,0:T(8,128)(2,1)} %param.19) | copy-start | bytes 1572868
  0.0 13.6 %copy-start.1 = (bf16[1,128,1024]{2,1,0:T(8,128)(2,1)S(1)}, bf16[1,128,1024]{2,1,0:T(8,128)(2,1)}, u32[]{:S(2)}) copy-start(bf16[1,128,1024]{2,1,0:T(8,128)(2,1)} %param.12) | copy-start | bytes 786436
  0.0 13.6 %copy-start.8 = (bf16[1024,256]{1,0:T(8,128)(2,1)S(1)}, bf16[1024,256]{1,0:T(8,128)(2,1)}, u32[]{:S(2)}) copy-start(bf16[1024,256]{1,0:T(8,128)(2,1)} %param.17) | copy-start | bytes 1572868
  0.0 14.2 %copy-start.10 = (s32[1,32]{1,0:T(1,128)S(1)}, s32[1,32]{1,0:T(1,128)}, u32[]{:S(2)}) copy-start(s32[1,32]{1,0:T(1,128)} %param.14) | copy-start | bytes 388
  0.0 14.6 %copy-start.7 = (s32[1,8]{1,0:T(1,128)S(1)}, s32[1,8]{1,0:T(1,128)}, u32[]{:S(2)}) copy-start(s32[1,8]{1,0:T(1,128)} %param.13) | copy-start | bytes 100
  1.3 14.1 %collective-permute-start.1 = (bf16[4,16,2,256]{3,1,2,0:T(8,128)(2,1)S(1)}, bf16[4,16,2,256]{3,1,2,0:T(8,128)(2,1)S(1)}, u32[]{:S(2)}, u32[]{:S(2)}) collective-permute-start(bf16[4,16,2,256]{3,1,2,0:T(8,128)(2,1)S(1)} %bitcast.136), channel_id=1, source_target_pairs={{0,1},{1,0},{2,3},{3,2},{4,5},{5,4},{6,7},{7,6},{8,9},{9,8},{10,11... | collective-permute-start | bytes 196616 | tf_op jit(solution)/shard_map/ppermute | solution.py:24
  4.4 11.0 %collective-permute-start.2 = (bf16[4,16,2,256]{3,1,2,0:T(8,128)(2,1)S(1)}, bf16[4,16,2,256]{3,1,2,0:T(8,128)(2,1)S(1)}, u32[]{:S(2)}, u32[]{:S(2)}) collective-permute-start(bf16[4,16,2,256]{3,1,2,0:T(8,128)(2,1)S(1)} %bitcast.137), channel_id=1, source_target_pairs={{0,2},{1,3},{2,0},{3,1},{4,6},{5,7},{6,4},{7,5},{8,10},{9,11},{10,... | collective-permute-start | bytes 196616 | tf_op jit(solution)/shard_map/ppermute | solution.py:24
  7.1 8.3 %collective-permute-start.3 = (bf16[4,16,2,256]{3,1,2,0:T(8,128)(2,1)S(1)}, bf16[4,16,2,256]{3,1,2,0:T(8,128)(2,1)S(1)}, u32[]{:S(2)}, u32[]{:S(2)}) collective-permute-start(bf16[4,16,2,256]{3,1,2,0:T(8,128)(2,1)S(1)} %bitcast.138), channel_id=1, source_target_pairs={{0,3},{1,2},{2,1},{3,0},{4,7},{5,6},{6,5},{7,4},{8,11},{9,10},{10,... | collective-permute-start | bytes 196616 | tf_op jit(solution)/shard_map/ppermute | solution.py:24
  12.2 3.3 %collective-permute-start = (bf16[128,2,256]{2,1,0:T(2,128)(2,1)S(1)}, bf16[128,2,256]{2,1,0:T(2,128)(2,1)S(1)}, u32[]{:S(2)}, u32[]{:S(2)}) collective-permute-start(bf16[128,2,256]{2,1,0:T(2,128)(2,1)S(1)} %reshape.342), channel_id=1, source_target_pairs={{0,4},{1,5},{2,6},{3,7},{8,12},{9,13},{10,14},{11,15},{16,20},{17,... | collective-permute-start | bytes 393224 | tf_op jit(solution)/shard_map/ppermute | solution.py:19
  15.2 2.4 %copy-start.4 = (pred[128,256]{1,0:T(8,128)(4,1)}, pred[128,256]{1,0:T(8,128)(4,1)S(1)}, u32[]{:S(2)}) copy-start(pred[128,256]{1,0:T(8,128)(4,1)S(1)} %fusion.58) | copy-start | bytes 98308
  15.4 2.2 %collective-permute-start.4 = (bf16[16,16,2,256]{3,1,2,0:T(8,128)(2,1)S(1)}, bf16[16,16,2,256]{3,1,2,0:T(8,128)(2,1)S(1)}, u32[]{:S(2)}, u32[]{:S(2)}) collective-permute-start(bf16[16,16,2,256]{3,1,2,0:T(8,128)(2,1)S(1)} %pad_maximum_fusion), channel_id=1, source_target_pairs={{0,4},{4,0},{1,5},{5,1},{2,6},{6,2},{3,7},{7,3},{8,12},{12,8},{9,1... | collective-permute-start | bytes 786440 | tf_op jit(solution)/shard_map/ppermute | solution.py:24
  18.5 1.9 %copy-start.5 = (pred[128,256]{1,0:T(8,128)(4,1)S(1)}, pred[128,256]{1,0:T(8,128)(4,1)}, u32[]{:S(2)}) copy-start(pred[128,256]{1,0:T(8,128)(4,1)} %copy-done.4) | copy-start | bytes 98308
  18.5 1.9 %copy-start.6 = (bf16[256,1,256]{0,2,1:T(8,128)(2,1)S(1)}, bf16[256,1,256]{0,2,1:T(8,128)(2,1)}, u32[]{:S(2)}) copy-start(bf16[256,1,256]{0,2,1:T(8,128)(2,1)} %copy.35) | copy-start | bytes 393220
  19.1 16.3 %copy-start.2 = (bf16[1,256,2,256]{3,2,1,0:T(2,128)(2,1)S(1)}, bf16[1,256,2,256]{3,2,1,0:T(2,128)(2,1)}, u32[]{:S(2)}) copy-start(bf16[1,256,2,256]{3,2,1,0:T(2,128)(2,1)} %param.16) | copy-start | bytes 786436
  19.6 20.5 %copy-start.9 = (bf16[1024,256]{1,0:T(8,128)(2,1)S(1)}, bf16[1024,256]{1,0:T(8,128)(2,1)}, u32[]{:S(2)}) copy-start(bf16[1024,256]{1,0:T(8,128)(2,1)} %param.20) | copy-start | bytes 1572868
  20.7 20.7 %copy-start.3 = (bf16[256,1024]{1,0:T(8,128)(2,1)S(1)}, bf16[256,1024]{1,0:T(8,128)(2,1)}, u32[]{:S(2)}) copy-start(bf16[256,1024]{1,0:T(8,128)(2,1)} %param.21) | copy-start | bytes 1572868
  21.0 6.8 %collective-permute-start.7 = (bf16[32,1024]{1,0:T(8,128)(2,1)S(1)}, bf16[32,1024]{1,0:T(8,128)(2,1)S(1)}, u32[]{:S(2)}, u32[]{:S(2)}) collective-permute-start(bf16[32,1024]{1,0:T(8,128)(2,1)S(1)} %get-tuple-element.25), channel_id=1, source_target_pairs={{0,3},{1,2},{2,1},{3,0},{4,7},{5,6},{6,5},{7,4},{8,11},{9,10},{10,... | collective-permute-start | bytes 196616 | tf_op jit(solution)/shard_map/ppermute | solution.py:24
  24.8 5.7 %collective-permute-start.6 = (bf16[32,1024]{1,0:T(8,128)(2,1)S(1)}, bf16[32,1024]{1,0:T(8,128)(2,1)S(1)}, u32[]{:S(2)}, u32[]{:S(2)}) collective-permute-start(bf16[32,1024]{1,0:T(8,128)(2,1)S(1)} %get-tuple-element.26), channel_id=1, source_target_pairs={{0,2},{1,3},{2,0},{3,1},{4,6},{5,7},{6,4},{7,5},{8,10},{9,11},{10,... | collective-permute-start | bytes 196616 | tf_op jit(solution)/shard_map/ppermute | solution.py:24
  24.8 5.7 %collective-permute-start.5 = (bf16[32,1024]{1,0:T(8,128)(2,1)S(1)}, bf16[32,1024]{1,0:T(8,128)(2,1)S(1)}, u32[]{:S(2)}, u32[]{:S(2)}) collective-permute-start(bf16[32,1024]{1,0:T(8,128)(2,1)S(1)} %get-tuple-element.24), channel_id=1, source_target_pairs={{0,1},{1,0},{2,3},{3,2},{4,5},{5,4},{6,7},{7,6},{8,9},{9,8},{10,11... | collective-permute-start | bytes 196616 | tf_op jit(solution)/shard_map/ppermute | solution.py:24
  31.0 6.4 %collective-permute-start.10 = (bf16[32,1024]{1,0:T(8,128)(2,1)S(1)}, bf16[32,1024]{1,0:T(8,128)(2,1)S(1)}, u32[]{:S(2)}, u32[]{:S(2)}) collective-permute-start(bf16[32,1024]{1,0:T(8,128)(2,1)S(1)} %multiply_convert_fusion.4), channel_id=1, source_target_pairs={{0,3},{1,2},{2,1},{3,0},{4,7},{5,6},{6,5},{7,4},{8,11},{9,10},{10,... | collective-permute-start | bytes 196616 | tf_op jit(solution)/shard_map/ppermute | solution.py:24
  33.6 6.4 %collective-permute-start.9 = (bf16[32,1024]{1,0:T(8,128)(2,1)S(1)}, bf16[32,1024]{1,0:T(8,128)(2,1)S(1)}, u32[]{:S(2)}, u32[]{:S(2)}) collective-permute-start(bf16[32,1024]{1,0:T(8,128)(2,1)S(1)} %multiply_convert_fusion.4), channel_id=1, source_target_pairs={{0,2},{1,3},{2,0},{3,1},{4,6},{5,7},{6,4},{7,5},{8,10},{9,11},{10,... | collective-permute-start | bytes 196616 | tf_op jit(solution)/shard_map/ppermute | solution.py:24
  34.2 5.9 %collective-permute-start.8 = (bf16[32,1024]{1,0:T(8,128)(2,1)S(1)}, bf16[32,1024]{1,0:T(8,128)(2,1)S(1)}, u32[]{:S(2)}, u32[]{:S(2)}) collective-permute-start(bf16[32,1024]{1,0:T(8,128)(2,1)S(1)} %multiply_convert_fusion.4), channel_id=1, source_target_pairs={{0,1},{1,0},{2,3},{3,2},{4,5},{5,4},{6,7},{7,6},{8,9},{9,8},{10,11... | collective-permute-start | bytes 196616 | tf_op jit(solution)/shard_map/ppermute | solution.py:24
  41.6 6.2 %collective-permute-start.13 = (bf16[32,1024]{1,0:T(8,128)(2,1)S(1)}, bf16[32,1024]{1,0:T(8,128)(2,1)S(1)}, u32[]{:S(2)}, u32[]{:S(2)}) collective-permute-start(bf16[32,1024]{1,0:T(8,128)(2,1)S(1)} %get-tuple-element.20), channel_id=1, source_target_pairs={{0,3},{1,2},{2,1},{3,0},{4,7},{5,6},{6,5},{7,4},{8,11},{9,10},{10,... | collective-permute-start | bytes 196616 | tf_op jit(solution)/shard_map/ppermute | solution.py:24
  43.7 6.2 %collective-permute-start.12 = (bf16[32,1024]{1,0:T(8,128)(2,1)S(1)}, bf16[32,1024]{1,0:T(8,128)(2,1)S(1)}, u32[]{:S(2)}, u32[]{:S(2)}) collective-permute-start(bf16[32,1024]{1,0:T(8,128)(2,1)S(1)} %get-tuple-element.21), channel_id=1, source_target_pairs={{0,2},{1,3},{2,0},{3,1},{4,6},{5,7},{6,4},{7,5},{8,10},{9,11},{10,... | collective-permute-start | bytes 196616 | tf_op jit(solution)/shard_map/ppermute | solution.py:24
  43.7 6.2 %collective-permute-start.11 = (bf16[32,1024]{1,0:T(8,128)(2,1)S(1)}, bf16[32,1024]{1,0:T(8,128)(2,1)S(1)}, u32[]{:S(2)}, u32[]{:S(2)}) collective-permute-start(bf16[32,1024]{1,0:T(8,128)(2,1)S(1)} %get-tuple-element.19), channel_id=1, source_target_pairs={{0,1},{1,0},{2,3},{3,2},{4,5},{5,4},{6,7},{7,6},{8,9},{9,8},{10,11... | collective-permute-start | bytes 196616 | tf_op jit(solution)/shard_map/ppermute | solution.py:24
  50.3 6.7 %collective-permute-start.16 = (bf16[32,1024]{1,0:T(8,128)(2,1)S(1)}, bf16[32,1024]{1,0:T(8,128)(2,1)S(1)}, u32[]{:S(2)}, u32[]{:S(2)}) collective-permute-start(bf16[32,1024]{1,0:T(8,128)(2,1)S(1)} %multiply_convert_fusion.3), channel_id=1, source_target_pairs={{0,3},{1,2},{2,1},{3,0},{4,7},{5,6},{6,5},{7,4},{8,11},{9,10},{10,... | collective-permute-start | bytes 196616 | tf_op jit(solution)/shard_map/ppermute | solution.py:24
  52.7 6.3 %collective-permute-start.15 = (bf16[32,1024]{1,0:T(8,128)(2,1)S(1)}, bf16[32,1024]{1,0:T(8,128)(2,1)S(1)}, u32[]{:S(2)}, u32[]{:S(2)}) collective-permute-start(bf16[32,1024]{1,0:T(8,128)(2,1)S(1)} %multiply_convert_fusion.3), channel_id=1, source_target_pairs={{0,2},{1,3},{2,0},{3,1},{4,6},{5,7},{6,4},{7,5},{8,10},{9,11},{10,... | collective-permute-start | bytes 196616 | tf_op jit(solution)/shard_map/ppermute | solution.py:24
  52.7 6.3 %collective-permute-start.14 = (bf16[32,1024]{1,0:T(8,128)(2,1)S(1)}, bf16[32,1024]{1,0:T(8,128)(2,1)S(1)}, u32[]{:S(2)}, u32[]{:S(2)}) collective-permute-start(bf16[32,1024]{1,0:T(8,128)(2,1)S(1)} %multiply_convert_fusion.3), channel_id=1, source_target_pairs={{0,1},{1,0},{2,3},{3,2},{4,5},{5,4},{6,7},{7,6},{8,9},{9,8},{10,11... | collective-permute-start | bytes 196616 | tf_op jit(solution)/shard_map/ppermute | solution.py:24
  63.8 6.7 %collective-permute-start.19 = (bf16[32,1024]{1,0:T(8,128)(2,1)S(1)}, bf16[32,1024]{1,0:T(8,128)(2,1)S(1)}, u32[]{:S(2)}, u32[]{:S(2)}) collective-permute-start(bf16[32,1024]{1,0:T(8,128)(2,1)S(1)} %get-tuple-element.17), channel_id=1, source_target_pairs={{0,3},{1,2},{2,1},{3,0},{4,7},{5,6},{6,5},{7,4},{8,11},{9,10},{10,... | collective-permute-start | bytes 196616 | tf_op jit(solution)/shard_map/ppermute | solution.py:24
  66.2 6.3 %collective-permute-start.18 = (bf16[32,1024]{1,0:T(8,128)(2,1)S(1)}, bf16[32,1024]{1,0:T(8,128)(2,1)S(1)}, u32[]{:S(2)}, u32[]{:S(2)}) collective-permute-start(bf16[32,1024]{1,0:T(8,128)(2,1)S(1)} %get-tuple-element.18), channel_id=1, source_target_pairs={{0,2},{1,3},{2,0},{3,1},{4,6},{5,7},{6,4},{7,5},{8,10},{9,11},{10,... | collective-permute-start | bytes 196616 | tf_op jit(solution)/shard_map/ppermute | solution.py:24
  66.2 6.3 %collective-permute-start.17 = (bf16[32,1024]{1,0:T(8,128)(2,1)S(1)}, bf16[32,1024]{1,0:T(8,128)(2,1)S(1)}, u32[]{:S(2)}, u32[]{:S(2)}) collective-permute-start(bf16[32,1024]{1,0:T(8,128)(2,1)S(1)} %get-tuple-element.16), channel_id=1, source_target_pairs={{0,1},{1,0},{2,3},{3,2},{4,5},{5,4},{6,7},{7,6},{8,9},{9,8},{10,11... | collective-permute-start | bytes 196616 | tf_op jit(solution)/shard_map/ppermute | solution.py:24

commit v2 on v0

v2 whole, which is shorter than its diff:
```python
import functools

import jax
import jax.numpy as jnp
from jax import lax
from jax.experimental import pallas as pl
from jax.experimental.pallas import tpu as pltpu
from jax.sharding import PartitionSpec as P

HEAD_DIM = 64
SPAN = 8
SINK = 4
WINDOW = 1024
SCALE = HEAD_DIM ** (-0.5)
EPS = 1e-05
VMEM_BYTES = 48 << 20
WIDE_SCORES = 8 << 20

bf16 = jnp.bfloat16
f32 = jnp.float32
i32 = jnp.int32


def swap(array, axis, by):
    count = lax.axis_size(axis)
    return lax.ppermute(array, axis, [(i, i ^ by) for i in range(count)])


def from_behind(array, axis, by):
    count = lax.axis_size(axis)
    return lax.ppermute(array, axis, [(i, (i + by) % count) for i in range(count)])


def gather_heads(array):
    return [array] + [swap(array, "head", by) for by in range(1, lax.axis_size("head"))]


def scatter_heads(pieces):
    return [pieces[0]] + [swap(piece, "head", by) for by, piece in enumerate(pieces) if by]


def kernel_call(body, outs, flops, *args):
    smem = {jnp.dtype(i32)}
    return pl.pallas_call(
        body,
        out_shape=outs,
        in_specs=[
            pl.BlockSpec(memory_space=pltpu.SMEM if a.dtype in smem else pltpu.VMEM) for a in args
        ],
        compiler_params=pltpu.CompilerParams(vmem_limit_bytes=VMEM_BYTES),
        cost_estimate=pl.CostEstimate(
            flops=flops, bytes_accessed=sum(a.nbytes for a in args), transcendentals=0
        ),
    )(*args)


def layer_norm(values):
    center = values - jnp.mean(values, axis=-1, keepdims=True)
    spread = jnp.mean(center * center, axis=-1, keepdims=True)
    return center * lax.rsqrt(spread + EPS)


def dot(left, right):
    return jnp.dot(left, right, preferred_element_type=f32)


def split_pair(pairs):
    rows, _, width = pairs.shape
    flat = pairs.astype(f32).reshape(rows, 2 * width).astype(bf16)
    return flat[:, :width], flat[:, width:]


def head_lanes(shape):
    return lax.broadcasted_iota(i32, shape, len(shape) - 1) // HEAD_DIM


def attend_heads(queries, keys, values, allowed, heads):
    rows, width = queries.shape
    lanes = head_lanes((rows, width))
    stacked = jnp.concatenate(
        [jnp.where(lanes == h, queries, jnp.zeros_like(queries)) for h in heads], axis=0
    )
    scores = lax.dot_general(
        stacked, keys, (((1,), (1,)), ((), ())), preferred_element_type=f32
    ).reshape(len(heads), rows, keys.shape[0])
    scores = scores * SCALE
    if allowed is not None:
        scores = jnp.where(allowed[None], scores, -jnp.inf)
    row_max = jnp.max(scores, axis=-1, keepdims=True)
    weights = jnp.exp(scores - row_max)
    row_sum = jnp.sum(weights, axis=-1, keepdims=True)
    summed = dot(weights.astype(bf16).reshape(len(heads) * rows, -1), values)
    summed = summed.reshape(len(heads), rows, width) / row_sum
    result = jnp.zeros((rows, width), f32)
    for i, h in enumerate(heads):
        result = jnp.where(lanes == h, summed[i], result)
    return result


def attend(queries, keys, values, allowed):
    rows, width = queries.shape
    heads = list(range(width // HEAD_DIM))
    if len(heads) * rows * keys.shape[0] * 4 <= WIDE_SCORES:
        return attend_heads(queries, keys, values, allowed, heads).astype(bf16)
    result = attend_heads(queries, keys, values, allowed, heads[:1])
    for h in heads[1:]:
        result = result + attend_heads(queries, keys, values, allowed, [h])
    return result.astype(bf16)


def project_body(tokens, w_query, w_keyvalue, queries, keyvalue):
    normed = layer_norm(tokens[0].astype(f32)).astype(bf16)
    queries[...] = dot(normed, w_query[...]).astype(bf16)
    w_key, w_value = split_pair(w_keyvalue[...])
    width = w_key.shape[1]
    keyvalue[:, :width] = dot(normed, w_key).astype(bf16)
    keyvalue[:, width:] = dot(normed, w_value).astype(bf16)


def request_info(token_ids, lengths):
    request = jnp.zeros_like(token_ids)
    first_token = jnp.zeros_like(token_ids)
    end = jnp.int32(0)
    for i in range(lengths.shape[1]):
        end = end + lengths[0, i]
        before = end <= token_ids
        request = request + before.astype(i32)
        first_token = jnp.where(before, first_token + lengths[0, i], first_token)
    return request, token_ids - first_token


def self_body(near, head_count, tok_count, place, lengths, table, queries, w_out, *refs):
    tok_index, head_index = place[0], place[1]
    near_refs, refs = refs[:near], refs[near:]
    slot_refs, outs = refs[:-head_count], refs[-head_count:]
    rows, width = queries.shape
    own_ids = tok_index * rows + lax.broadcasted_iota(i32, (rows, 1), 0)
    own_request, own_offset = request_info(own_ids, lengths)
    keys, values, allowed = [], [], []
    for distance, ref in enumerate(near_refs):
        keys.append(ref[:, :width])
        values.append(ref[:, width:])
        ids = (tok_index - distance) * rows + lax.broadcasted_iota(i32, (1, rows), 1)
        allowed.append(
            (ids >= 0)
            & (request_info(ids, lengths)[0] == own_request)
            & (ids <= own_ids)
            & (own_ids - ids < WINDOW)
        )
    block_len = slot_refs[0].shape[1]
    shard_blocks = slot_refs[0].shape[0]
    prefix_len = table.shape[1] * block_len
    piece_of = 0
    for ref in slot_refs:
        count = ref.shape[0] * block_len
        key, value = split_pair(ref[...].reshape(count, 2, width))
        keys.append(key)
        values.append(value)
        slot = lax.broadcasted_iota(i32, (1, count), 1)
        places = slot % block_len
        for block in range(ref.shape[0]):
            piece = piece_of + block // shard_blocks
            far, by = piece // head_count, piece % head_count
            physical = ((tok_index ^ far) * head_count + (head_index ^ by)) * shard_blocks
            logical = table[0, physical + block % shard_blocks]
            places = places + jnp.where(slot // block_len == block, logical * block_len, 0)
        piece_of += ref.shape[0] // shard_blocks
        allowed.append((places < SINK) | (places > prefix_len + own_offset - WINDOW))
    attended = attend(
        queries[...],
        jnp.concatenate(keys, axis=0),
        jnp.concatenate(values, axis=0),
        jnp.concatenate([a.astype(i32) for a in allowed], axis=1) != 0,
    )
    share = rows // head_count
    for by, out in enumerate(outs):
        out[...] = jnp.zeros_like(out)
    term = dot(attended, w_out[...]).astype(bf16)
    for owner in range(head_count):
        for by, out in enumerate(outs):

            @pl.when((head_index ^ by) == owner)
            def _(out=out, owner=owner):
                out[...] = term[owner * share : (owner + 1) * share]


def after_self_body(place, tokens, *refs):
    terms, (after, normed) = refs[:-2], refs[-2:]
    share = after.shape[0]
    start = pl.multiple_of(place[1] * share, share)
    total = tokens[0, pl.ds(start, share), :].astype(f32)
    total = total + sum(term[...].astype(f32) for term in terms)
    after[...] = total
    normed[...] = layer_norm(total).astype(bf16)


def cross_body(head_count, w_cross_query, cross_cache, w_cross_out, *refs):
    rows_in, outs = refs[:head_count], refs[head_count:]
    normed = jnp.concatenate([ref[...] for ref in rows_in], axis=0)
    queries = dot(normed, w_cross_query[...]).astype(bf16)
    keys, values = split_pair(cross_cache[0])
    cross_out = attend(queries, keys, values, None)
    term = dot(cross_out, w_cross_out[...]).astype(bf16)
    share = rows_in[0].shape[0]
    for by, out in enumerate(outs):
        out[...] = term[by * share : (by + 1) * share]


def after_cross_body(before, *refs):
    terms, (after, normed) = refs[:-2], refs[-2:]
    total = before[...] + sum(term[...].astype(f32) for term in terms)
    after[...] = total
    normed[...] = layer_norm(total).astype(bf16)


def hidden_body(head_count, w_up, w_down, *refs):
    rows_in, outs = refs[:head_count], refs[head_count:]
    normed = jnp.concatenate([ref[...] for ref in rows_in], axis=0)
    hidden = jax.nn.relu(dot(normed, w_up[...])).astype(bf16)
    term = dot(hidden, w_down[...]).astype(bf16)
    share = rows_in[0].shape[0]
    for by, out in enumerate(outs):
        out[...] = term[by * share : (by + 1) * share]


def on_device(
    tokens,
    lengths,
    block_position,
    prefix_pool,
    cross_cache,
    w_query,
    w_keyvalue,
    w_out,
    w_cross_query,
    w_cross_out,
    w_up,
    w_down,
):
    rows, model_width = tokens.shape[1:]
    width = w_query.shape[1]
    tok_index, head_index = lax.axis_index("tok"), lax.axis_index("head")
    tok_count, head_count = lax.axis_size("tok"), lax.axis_size("head")
    share = rows // head_count
    place = jnp.stack([tok_index, head_index]).astype(i32)
    shape = jax.ShapeDtypeStruct
    row_pieces = [shape((share, model_width), bf16)] * head_count
    stats = [shape((share, model_width), f32), shape((share, model_width), bf16)]

    slots = scatter_heads(
        [
            lax.dynamic_slice_in_dim(prefix_pool[0], (head_index ^ by) * width, width, 3)
            for by in range(head_count)
        ]
    )
    queries, keyvalue = kernel_call(
        project_body,
        [shape((rows, width), bf16), shape((rows, 2 * width), bf16)],
        6 * rows * model_width * width,
        tokens,
        w_query,
        w_keyvalue,
    )
    near = [keyvalue] + [
        from_behind(keyvalue, "tok", distance)
        for distance in range(1, min(SPAN, tok_count - 1) + 1)
    ]
    own_slots = jnp.concatenate(slots, axis=0)
    far_slots = [swap(own_slots, "tok", by) for by in range(1, tok_count)]
    slot_rows = tok_count * own_slots.shape[0] * own_slots.shape[1]
    terms = kernel_call(
        functools.partial(self_body, len(near), head_count, tok_count),
        row_pieces,
        4 * rows * width * (len(near) * rows + slot_rows) + 2 * rows * width * model_width,
        place,
        lengths,
        block_position,
        queries,
        w_out,
        *near,
        *slots,
        *far_slots,
    )
    after_self, normed = kernel_call(
        after_self_body, stats, 0, place, tokens, *scatter_heads(terms)
    )
    terms = kernel_call(
        functools.partial(cross_body, head_count),
        row_pieces,
        4 * rows * model_width * width,
        w_cross_query,
        cross_cache,
        w_cross_out,
        *gather_heads(normed),
    )
    after_cross, normed = kernel_call(
        after_cross_body, stats, 0, after_self, *scatter_heads(terms)
    )
    terms = kernel_call(
        functools.partial(hidden_body, head_count),
        row_pieces,
        4 * rows * model_width * w_up.shape[1],
        w_up,
        w_down,
        *gather_heads(normed),
    )
    result = after_cross + sum(term.astype(f32) for term in scatter_heads(terms))
    return result.astype(bf16)[None]


def solution(mesh):
    return jax.shard_map(
        on_device,
        mesh=mesh,
        in_specs=(
            P("grp", "tok", None),
            P("grp", None),
            P("grp", None),
            P("grp", ("tok", "head"), None, None, None),
            P("grp", None, None, "head"),
            P(None, "head"),
            P(None, None, "head"),
            P("head", None),
            P(None, "head"),
            P("head", None),
            P(None, "head"),
            P("head", None),
        ),
        out_specs=P("grp", ("tok", "head"), None),
        check_vma=False,
    )
```

time: 166 us -> 77.6 us (0.47)
  waiting for transfers between devices: 119 us -> 28.8 us
  starting transfers between devices: 2.53 us -> 28.6 us
  between operations: 13.5 us -> 0.12 us
  matrix products: 12.8 us -> 0 us
  Pallas kernels: 0 us -> 8.49 us
  other arithmetic: 9.43 us -> 1.14 us
  local copies, waits for them, and re-layouts: 8.31 us -> 10 us
    psum x2 -> x0, waiting for transfers between devices: 75.6 us -> none  [heads_total(): return lax.psum(partial_term, 'head')]
    ppermute x1 -> x20, waiting for transfers between devices: 0.01 us -> 28.8 us  [the longest x19 27.9 us: swap(): return lax.ppermute(array, axis, [(i, i ^ by) for i in range(count)])]
    ppermute x1 -> x20, starting transfers between devices: 2.37 us -> 28.6 us  [the longest x19 28 us: swap(): return lax.ppermute(array, axis, [(i, i ^ by) for i in range(count)])]
    reduce_scatter x1 -> x0, waiting for transfers between devices: 21.8 us -> none  [on_device(): lax.psum_scatter(jnp.dot(hidden, w_down, preferred_element_type=jnp.float...]
    all_gather x1 -> x0, waiting for transfers between devices: 21.4 us -> none  [on_device(): lax.all_gather(prefix_pool, ('tok', 'head'), axis=1, tiled=True)[0]]
    dot_general x12 -> x0, matrix products: 12.8 us -> none  [the longest x1 5.57 us: on_device(): jnp.dot(hidden, w_down, preferred_element_type=jnp.float32)]
    pallas_call x0 -> x6, Pallas kernels: none -> 8.49 us  [kernel_call(): pl.pallas_call(body, out_shape=outs, in_specs=[pl.BlockSpec(memory_space=...]
    reduce_sum x12 -> x0, other arithmetic: 7.29 us -> none  [the longest x3 3.51 us: layer_norm(): center = values - jnp.mean(values, axis=-1, keepdims=True)]
  transfers between devices with their start and end apart: 5 -> 20, of which waited for: 4 -> 17; matrix products, arithmetic and copies ran while one was open for 6% -> 0% of each run, Pallas kernels for 0% -> 1%
where the time goes in v2:
time: 77.6 us; the launch traced here: 77.2 us
  waiting for transfers between devices  28.8 us (37%)
  starting transfers between devices  28.6 us (37%)
  local copies, waits for them, and re-layouts  10 us (13%)
  Pallas kernels  8.49 us (11%)
  other arithmetic  1.14 us (1%)
    ppermute x19, starting transfers between devices, swap(): return lax.ppermute(array, axis, [(i, i ^ by) for i in range(count)])  28 us
    ppermute x19, waiting for transfers between devices, swap(): return lax.ppermute(array, axis, [(i, i ^ by) for i in range(count)])  27.9 us
    unnamed x22, local copies, waits for them, and re-layouts  8.8 us
    pallas_call x6, Pallas kernels, kernel_call(): pl.pallas_call(body, out_shape=outs, in_specs=[pl.BlockSpec(memory_space=...  8.49 us
  transfers between devices with their start and end apart: 20, of which 17 were waited for; matrix products, arithmetic and copies ran while one was open for 0% of the time, Pallas kernels for 1%

profile of v2, /device:TPU:0, one launch (start us, length us, event | category | flops | bytes accessed | tf_op | source)
XLA Modules:
  0.0 77.2 jit_solution(395006777291627492)
XLA Ops:
  0.0 1.2 %dynamic-slice_bitcast_fusion = (bf16[4,16,2,256]{3,2,1,0:T(2,128)(2,1)S(1)}, bf16[4,16,2,256]{3,2,1,0:T(2,128)(2,1)S(1)}, bf16[4,16,2,256]{3,2,1,0:T(2,128)(2,1)S(1)}, bf16[4,16,2,256]{3,2,1,0:T(2,128)(2,1)S(1)}) fusion(bf16[1,4,16,2,1024]{4,3,2,1,0:T(2,128)(2,1)} %param.15, s32[]{:T(128)S(6)} %select_n.15, s32[]{:T(128)S(6)} %select_n.13, s32[]{:T(128)S(6)} %select_n.12, ...), kind=kLoop, calls=%fused_computation.3 | loop fusion | bytes 524304 | tf_op jit(solution)/shard_map/dynamic_slice | solution.py:252
  1.2 3.1 %collective-permute-start.1 = (bf16[4,16,2,256]{3,2,1,0:T(2,128)(2,1)S(1)}, bf16[4,16,2,256]{3,2,1,0:T(2,128)(2,1)S(1)}, u32[]{:S(2)}, u32[]{:S(2)}) collective-permute-start(bf16[4,16,2,256]{3,2,1,0:T(2,128)(2,1)S(1)} %get-tuple-element.42), channel_id=1, source_target_pairs={{0,1},{1,0},{2,3},{3,2},{4,5},{5,4},{6,7},{7,6},{8,9},{9,8},{10,11... | collective-permute-start | bytes 196616 | tf_op jit(solution)/shard_map/ppermute | solution.py:26
  4.3 2.6 %collective-permute-start.2 = (bf16[4,16,2,256]{3,2,1,0:T(2,128)(2,1)S(1)}, bf16[4,16,2,256]{3,2,1,0:T(2,128)(2,1)S(1)}, u32[]{:S(2)}, u32[]{:S(2)}) collective-permute-start(bf16[4,16,2,256]{3,2,1,0:T(2,128)(2,1)S(1)} %get-tuple-element.44), channel_id=1, source_target_pairs={{0,2},{1,3},{2,0},{3,1},{4,6},{5,7},{6,4},{7,5},{8,10},{9,11},{10,... | collective-permute-start | bytes 196616 | tf_op jit(solution)/shard_map/ppermute | solution.py:26
  6.9 4.7 %collective-permute-done.2.refs_4_ = bf16[4,16,2,256]{3,2,1,0:T(2,128)(2,1)S(1)} collective-permute-done((bf16[4,16,2,256]{3,2,1,0:T(2,128)(2,1)S(1)}, bf16[4,16,2,256]{3,2,1,0:T(2,128)(2,1)S(1)}, u32[]{:S(2)}, u32[]{:S(2)}) %collective-permute-start.2) | collective-permute-done | bytes 65568 | tf_op jit(solution)/shard_map/ppermute | solution.py:26
  11.6 1.4 %collective-permute-done.3.refs_5_ = bf16[4,16,2,256]{3,2,1,0:T(2,128)(2,1)S(1)} collective-permute-done((bf16[4,16,2,256]{3,2,1,0:T(2,128)(2,1)S(1)}, bf16[4,16,2,256]{3,2,1,0:T(2,128)(2,1)S(1)}, u32[]{:S(2)}, u32[]{:S(2)}) %collective-permute-start.3) | collective-permute-done | bytes 65568 | tf_op jit(solution)/shard_map/ppermute | solution.py:26
  13.5 0.9 %copy-done.1 = bf16[1,128,1024]{2,1,0:T(8,128)(2,1)S(1)} copy-done((bf16[1,128,1024]{2,1,0:T(8,128)(2,1)S(1)}, bf16[1,128,1024]{2,1,0:T(8,128)(2,1)}, u32[]{:S(2)}) %copy-start.1) | copy-done | bytes 262168
  14.4 1.2 %copy-done.3 = bf16[1024,2,256]{2,1,0:T(2,128)(2,1)S(1)} copy-done((bf16[1024,2,256]{2,1,0:T(2,128)(2,1)S(1)}, bf16[1024,2,256]{2,1,0:T(2,128)(2,1)}, u32[]{:S(2)}) %copy-start.3) | copy-done | bytes 1048600
  15.7 1.0 %copy-done.4 = bf16[1024,256]{1,0:T(8,128)(2,1)S(1)} copy-done((bf16[1024,256]{1,0:T(8,128)(2,1)S(1)}, bf16[1024,256]{1,0:T(8,128)(2,1)}, u32[]{:S(2)}) %copy-start.4) | copy-done | bytes 524312
  16.7 0.9 %shard_map.118 = (bf16[128,256]{1,0:T(8,128)(2,1)S(1)}, bf16[128,512]{1,0:T(8,128)(2,1)S(1)}) custom-call(bf16[1,128,1024]{2,1,0:T(8,128)(2,1)S(1)} %copy-done.1, bf16[1024,256]{1,0:T(8,128)(2,1)S(1)} %copy-done.4, bf16[1024,2,256]{2,1,0:T(2,128)(2,1)S(1)} %copy-done.3), custom_call_target="tpu_custom_call" | custom-call | flops 201326592 | bytes 1835008 | tf_op jit(solution)/shard_map/pallas_call | solution.py:44
  19.2 1.0 %copy-done.7 = bf16[256,1024]{1,0:T(8,128)(2,1)S(1)} copy-done((bf16[256,1024]{1,0:T(8,128)(2,1)S(1)}, bf16[256,1024]{1,0:T(8,128)(2,1)}, u32[]{:S(2)}) %copy-start.7) | copy-done | bytes 524312
  21.6 2.2 %shard_map.119 = (bf16[32,1024]{1,0:T(8,128)(2,1)S(1)}, bf16[32,1024]{1,0:T(8,128)(2,1)S(1)}, bf16[32,1024]{1,0:T(8,128)(2,1)S(1)}, bf16[32,1024]{1,0:T(8,128)(2,1)S(1)}) custom-call(s32[2]{0:T(128)S(1)} %pad_add_fusion.place, s32[1,8]{1,0:T(1,128)S(1)} %copy-done.9, s32[1,32]{1,0:T(1,128)S(1)} %copy-done.10, ...), custom_call_target="tpu_custom_call" | custom-call | flops 167772160 | bytes 1376424 | tf_op jit(solution)/shard_map/pallas_call | solution.py:44
  23.8 2.3 %collective-permute-start.6 = (bf16[32,1024]{1,0:T(8,128)(2,1)S(1)}, bf16[32,1024]{1,0:T(8,128)(2,1)S(1)}, u32[]{:S(2)}, u32[]{:S(2)}) collective-permute-start(bf16[32,1024]{1,0:T(8,128)(2,1)S(1)} %get-tuple-element.27), channel_id=1, source_target_pairs={{0,2},{1,3},{2,0},{3,1},{4,6},{5,7},{6,4},{7,5},{8,10},{9,11},{10,... | collective-permute-start | bytes 196616 | tf_op jit(solution)/shard_map/ppermute | solution.py:26
  26.2 2.0 %collective-permute-start.7 = (bf16[32,1024]{1,0:T(8,128)(2,1)S(1)}, bf16[32,1024]{1,0:T(8,128)(2,1)S(1)}, u32[]{:S(2)}, u32[]{:S(2)}) collective-permute-start(bf16[32,1024]{1,0:T(8,128)(2,1)S(1)} %get-tuple-element.28), channel_id=1, source_target_pairs={{0,3},{1,2},{2,1},{3,0},{4,7},{5,6},{6,5},{7,4},{8,11},{9,10},{10,... | collective-permute-start | bytes 196616 | tf_op jit(solution)/shard_map/ppermute | solution.py:26
  28.2 1.2 %collective-permute-done.5.refs_1_ = bf16[32,1024]{1,0:T(8,128)(2,1)S(1)} collective-permute-done((bf16[32,1024]{1,0:T(8,128)(2,1)S(1)}, bf16[32,1024]{1,0:T(8,128)(2,1)S(1)}, u32[]{:S(2)}, u32[]{:S(2)}) %collective-permute-start.5) | collective-permute-done | bytes 65568 | tf_op jit(solution)/shard_map/ppermute | solution.py:26
  29.4 2.1 %collective-permute-done.6.refs_2_ = bf16[32,1024]{1,0:T(8,128)(2,1)S(1)} collective-permute-done((bf16[32,1024]{1,0:T(8,128)(2,1)S(1)}, bf16[32,1024]{1,0:T(8,128)(2,1)S(1)}, u32[]{:S(2)}, u32[]{:S(2)}) %collective-permute-start.6) | collective-permute-done | bytes 65568 | tf_op jit(solution)/shard_map/ppermute | solution.py:26
  33.1 2.7 %collective-permute-start.10 = (bf16[32,1024]{1,0:T(8,128)(2,1)S(1)}, bf16[32,1024]{1,0:T(8,128)(2,1)S(1)}, u32[]{:S(2)}, u32[]{:S(2)}) collective-permute-start(bf16[32,1024]{1,0:T(8,128)(2,1)S(1)} %get-tuple-element.30.refs_0_), channel_id=1, source_target_pairs={{0,3},{1,2},{2,1},{3,0},{4,7},{5,6},{6,5},{7,4},{8,11},{9,10},{10,... | collective-permute-start | bytes 196616 | tf_op jit(solution)/shard_map/ppermute | solution.py:26
  36.5 1.0 %collective-permute-start.9 = (bf16[32,1024]{1,0:T(8,128)(2,1)S(1)}, bf16[32,1024]{1,0:T(8,128)(2,1)S(1)}, u32[]{:S(2)}, u32[]{:S(2)}) collective-permute-start(bf16[32,1024]{1,0:T(8,128)(2,1)S(1)} %get-tuple-element.30.refs_0_), channel_id=1, source_target_pairs={{0,2},{1,3},{2,0},{3,1},{4,6},{5,7},{6,4},{7,5},{8,10},{9,11},{10,... | collective-permute-start | bytes 196616 | tf_op jit(solution)/shard_map/ppermute | solution.py:26
  37.5 2.3 %collective-permute-done.10.refs_3_ = bf16[32,1024]{1,0:T(8,128)(2,1)S(1)} collective-permute-done((bf16[32,1024]{1,0:T(8,128)(2,1)S(1)}, bf16[32,1024]{1,0:T(8,128)(2,1)S(1)}, u32[]{:S(2)}, u32[]{:S(2)}) %collective-permute-start.10) | collective-permute-done | bytes 65568 | tf_op jit(solution)/shard_map/ppermute | solution.py:26
  39.8 1.2 %collective-permute-done.8.refs_1_ = bf16[32,1024]{1,0:T(8,128)(2,1)S(1)} collective-permute-done((bf16[32,1024]{1,0:T(8,128)(2,1)S(1)}, bf16[32,1024]{1,0:T(8,128)(2,1)S(1)}, u32[]{:S(2)}, u32[]{:S(2)}) %collective-permute-start.8) | collective-permute-done | bytes 65568 | tf_op jit(solution)/shard_map/ppermute | solution.py:26
  41.7 1.0 %copy-done.6 = bf16[256,1024]{1,0:T(8,128)(2,1)S(1)} copy-done((bf16[256,1024]{1,0:T(8,128)(2,1)S(1)}, bf16[256,1024]{1,0:T(8,128)(2,1)}, u32[]{:S(2)}) %copy-start.6) | copy-done | bytes 524312
  43.7 1.3 %collective-permute-start.11 = (bf16[32,1024]{1,0:T(8,128)(2,1)S(1)}, bf16[32,1024]{1,0:T(8,128)(2,1)S(1)}, u32[]{:S(2)}, u32[]{:S(2)}) collective-permute-start(bf16[32,1024]{1,0:T(8,128)(2,1)S(1)} %get-tuple-element.32), channel_id=1, source_target_pairs={{0,1},{1,0},{2,3},{3,2},{4,5},{5,4},{6,7},{7,6},{8,9},{9,8},{10,11... | collective-permute-start | bytes 196616 | tf_op jit(solution)/shard_map/ppermute | solution.py:26
  45.0 2.2 %collective-permute-start.12 = (bf16[32,1024]{1,0:T(8,128)(2,1)S(1)}, bf16[32,1024]{1,0:T(8,128)(2,1)S(1)}, u32[]{:S(2)}, u32[]{:S(2)}) collective-permute-start(bf16[32,1024]{1,0:T(8,128)(2,1)S(1)} %get-tuple-element.33), channel_id=1, source_target_pairs={{0,2},{1,3},{2,0},{3,1},{4,6},{5,7},{6,4},{7,5},{8,10},{9,11},{10,... | collective-permute-start | bytes 196616 | tf_op jit(solution)/shard_map/ppermute | solution.py:26
  48.1 3.4 %collective-permute-done.12.refs_2_ = bf16[32,1024]{1,0:T(8,128)(2,1)S(1)} collective-permute-done((bf16[32,1024]{1,0:T(8,128)(2,1)S(1)}, bf16[32,1024]{1,0:T(8,128)(2,1)S(1)}, u32[]{:S(2)}, u32[]{:S(2)}) %collective-permute-start.12) | collective-permute-done | bytes 65568 | tf_op jit(solution)/shard_map/ppermute | solution.py:26
  51.6 1.8 %collective-permute-done.13.refs_3_ = bf16[32,1024]{1,0:T(8,128)(2,1)S(1)} collective-permute-done((bf16[32,1024]{1,0:T(8,128)(2,1)S(1)}, bf16[32,1024]{1,0:T(8,128)(2,1)S(1)}, u32[]{:S(2)}, u32[]{:S(2)}) %collective-permute-start.13) | collective-permute-done | bytes 65568 | tf_op jit(solution)/shard_map/ppermute | solution.py:26
  53.7 1.4 %collective-permute-start.15 = (bf16[32,1024]{1,0:T(8,128)(2,1)S(1)}, bf16[32,1024]{1,0:T(8,128)(2,1)S(1)}, u32[]{:S(2)}, u32[]{:S(2)}) collective-permute-start(bf16[32,1024]{1,0:T(8,128)(2,1)S(1)} %get-tuple-element.36.refs_0_), channel_id=1, source_target_pairs={{0,2},{1,3},{2,0},{3,1},{4,6},{5,7},{6,4},{7,5},{8,10},{9,11},{10,... | collective-permute-start | bytes 196616 | tf_op jit(solution)/shard_map/ppermute | solution.py:26
  55.1 3.0 %collective-permute-start.16 = (bf16[32,1024]{1,0:T(8,128)(2,1)S(1)}, bf16[32,1024]{1,0:T(8,128)(2,1)S(1)}, u32[]{:S(2)}, u32[]{:S(2)}) collective-permute-start(bf16[32,1024]{1,0:T(8,128)(2,1)S(1)} %get-tuple-element.36.refs_0_), channel_id=1, source_target_pairs={{0,3},{1,2},{2,1},{3,0},{4,7},{5,6},{6,5},{7,4},{8,11},{9,10},{10,... | collective-permute-start | bytes 196616 | tf_op jit(solution)/shard_map/ppermute | solution.py:26
  59.0 2.2 %collective-permute-done.16.refs_3_ = bf16[32,1024]{1,0:T(8,128)(2,1)S(1)} collective-permute-done((bf16[32,1024]{1,0:T(8,128)(2,1)S(1)}, bf16[32,1024]{1,0:T(8,128)(2,1)S(1)}, u32[]{:S(2)}, u32[]{:S(2)}) %collective-permute-start.16) | collective-permute-done | bytes 65568 | tf_op jit(solution)/shard_map/ppermute | solution.py:26
  61.2 2.2 %copy-done = bf16[1024,2048]{1,0:T(8,128)(2,1)S(1)} copy-done((bf16[1024,2048]{1,0:T(8,128)(2,1)S(1)}, bf16[1024,2048]{1,0:T(8,128)(2,1)}, u32[]{:S(2)}) %copy-start) | copy-done | bytes 4194328
  63.4 3.5 %shard_map.123 = (bf16[32,1024]{1,0:T(8,128)(2,1)S(1)}, bf16[32,1024]{1,0:T(8,128)(2,1)S(1)}, bf16[32,1024]{1,0:T(8,128)(2,1)S(1)}, bf16[32,1024]{1,0:T(8,128)(2,1)S(1)}) custom-call(bf16[1024,2048]{1,0:T(8,128)(2,1)S(1)} %copy-done, bf16[2048,1024]{1,0:T(8,128)(2,1)} %w_down.1, bf16[32,1024]{1,0:T(8,128)(2,1)S(1)} %get-tuple-element.36.refs_0_, ...), custom_call_target="tpu_custom_call" | custom-call | flops 1073741824 | bytes 8650752 | tf_op jit(solution)/shard_map/pallas_call | solution.py:44
  67.7 2.8 %collective-permute-start.18 = (bf16[32,1024]{1,0:T(8,128)(2,1)S(1)}, bf16[32,1024]{1,0:T(8,128)(2,1)S(1)}, u32[]{:S(2)}, u32[]{:S(2)}) collective-permute-start(bf16[32,1024]{1,0:T(8,128)(2,1)S(1)} %get-tuple-element.39), channel_id=1, source_target_pairs={{0,2},{1,3},{2,0},{3,1},{4,6},{5,7},{6,4},{7,5},{8,10},{9,11},{10,... | collective-permute-start | bytes 196616 | tf_op jit(solution)/shard_map/ppermute | solution.py:26
  71.8 1.0 %collective-permute-done.18 = bf16[32,1024]{1,0:T(8,128)(2,1)S(1)} collective-permute-done((bf16[32,1024]{1,0:T(8,128)(2,1)S(1)}, bf16[32,1024]{1,0:T(8,128)(2,1)S(1)}, u32[]{:S(2)}, u32[]{:S(2)}) %collective-permute-start.18) | collective-permute-done | bytes 65568 | tf_op jit(solution)/shard_map/ppermute | solution.py:26
  72.8 3.7 %collective-permute-done.19 = bf16[32,1024]{1,0:T(8,128)(2,1)S(1)} collective-permute-done((bf16[32,1024]{1,0:T(8,128)(2,1)S(1)}, bf16[32,1024]{1,0:T(8,128)(2,1)S(1)}, u32[]{:S(2)}, u32[]{:S(2)}) %collective-permute-start.19) | collective-permute-done | bytes 65568 | tf_op jit(solution)/shard_map/ppermute | solution.py:26
  (40 shorter events, 12.3 us)
Async XLA Ops:
  0.0 32.3 %copy-start.2 = (bf16[1,128,1024]{2,1,0:T(8,128)(2,1)S(1)}, bf16[1,128,1024]{2,1,0:T(8,128)(2,1)}, u32[]{:S(2)}) copy-start(bf16[1,128,1024]{2,1,0:T(8,128)(2,1)} %tokens.3) | copy-start | bytes 786436
  0.0 41.7 %copy-start.8 = (bf16[1,256,2,256]{3,2,1,0:T(2,128)(2,1)S(1)}, bf16[1,256,2,256]{3,2,1,0:T(2,128)(2,1)}, u32[]{:S(2)}) copy-start(bf16[1,256,2,256]{3,2,1,0:T(2,128)(2,1)} %cross_cache.1) | copy-start | bytes 786436
  0.0 41.7 %copy-start.5 = (bf16[1024,256]{1,0:T(8,128)(2,1)S(1)}, bf16[1024,256]{1,0:T(8,128)(2,1)}, u32[]{:S(2)}) copy-start(bf16[1024,256]{1,0:T(8,128)(2,1)} %w_cross_query.1) | copy-start | bytes 1572868
  1.2 5.7 %collective-permute-start.1 = (bf16[4,16,2,256]{3,2,1,0:T(2,128)(2,1)S(1)}, bf16[4,16,2,256]{3,2,1,0:T(2,128)(2,1)S(1)}, u32[]{:S(2)}, u32[]{:S(2)}) collective-permute-start(bf16[4,16,2,256]{3,2,1,0:T(2,128)(2,1)S(1)} %get-tuple-element.42), channel_id=1, source_target_pairs={{0,1},{1,0},{2,3},{3,2},{4,5},{5,4},{6,7},{7,6},{8,9},{9,8},{10,11... | collective-permute-start | bytes 196616 | tf_op jit(solution)/shard_map/ppermute | solution.py:26
  4.3 7.3 %collective-permute-start.2 = (bf16[4,16,2,256]{3,2,1,0:T(2,128)(2,1)S(1)}, bf16[4,16,2,256]{3,2,1,0:T(2,128)(2,1)S(1)}, u32[]{:S(2)}, u32[]{:S(2)}) collective-permute-start(bf16[4,16,2,256]{3,2,1,0:T(2,128)(2,1)S(1)} %get-tuple-element.44), channel_id=1, source_target_pairs={{0,2},{1,3},{2,0},{3,1},{4,6},{5,7},{6,4},{7,5},{8,10},{9,11},{10,... | collective-permute-start | bytes 196616 | tf_op jit(solution)/shard_map/ppermute | solution.py:26
  6.9 6.1 %collective-permute-start.3 = (bf16[4,16,2,256]{3,2,1,0:T(2,128)(2,1)S(1)}, bf16[4,16,2,256]{3,2,1,0:T(2,128)(2,1)S(1)}, u32[]{:S(2)}, u32[]{:S(2)}) collective-permute-start(bf16[4,16,2,256]{3,2,1,0:T(2,128)(2,1)S(1)} %get-tuple-element.41), channel_id=1, source_target_pairs={{0,3},{1,2},{2,1},{3,0},{4,7},{5,6},{6,5},{7,4},{8,11},{9,10},{10,... | collective-permute-start | bytes 196616 | tf_op jit(solution)/shard_map/ppermute | solution.py:26
  13.4 5.8 %collective-permute-start.4 = (bf16[16,16,2,256]{3,2,1,0:T(2,128)(2,1)S(1)}, bf16[16,16,2,256]{3,2,1,0:T(2,128)(2,1)S(1)}, u32[]{:S(2)}, u32[]{:S(2)}) collective-permute-start(bf16[16,16,2,256]{3,2,1,0:T(2,128)(2,1)S(1)} %pad_maximum_fusion), channel_id=1, source_target_pairs={{0,4},{4,0},{1,5},{5,1},{2,6},{6,2},{3,7},{7,3},{8,12},{12,8},{9,1... | collective-permute-start | bytes 786440 | tf_op jit(solution)/shard_map/ppermute | solution.py:26
  13.5 1.0 %copy-start.1 = (bf16[1,128,1024]{2,1,0:T(8,128)(2,1)S(1)}, bf16[1,128,1024]{2,1,0:T(8,128)(2,1)}, u32[]{:S(2)}) copy-start(bf16[1,128,1024]{2,1,0:T(8,128)(2,1)} %tokens.3) | copy-start | bytes 786436
  14.4 1.2 %copy-start.3 = (bf16[1024,2,256]{2,1,0:T(2,128)(2,1)S(1)}, bf16[1024,2,256]{2,1,0:T(2,128)(2,1)}, u32[]{:S(2)}) copy-start(bf16[1024,2,256]{2,1,0:T(2,128)(2,1)} %w_keyvalue.1) | copy-start | bytes 3145732
  15.7 1.0 %copy-start.4 = (bf16[1024,256]{1,0:T(8,128)(2,1)S(1)}, bf16[1024,256]{1,0:T(8,128)(2,1)}, u32[]{:S(2)}) copy-start(bf16[1024,256]{1,0:T(8,128)(2,1)} %w_query.1) | copy-start | bytes 1572868
  17.7 1.5 %collective-permute-start = (bf16[128,512]{1,0:T(8,128)(2,1)S(1)}, bf16[128,512]{1,0:T(8,128)(2,1)S(1)}, u32[]{:S(2)}, u32[]{:S(2)}) collective-permute-start(bf16[128,512]{1,0:T(8,128)(2,1)S(1)} %get-tuple-element.24.refs_0_), channel_id=1, source_target_pairs={{0,4},{4,0},{1,5},{5,1},{2,6},{6,2},{3,7},{7,3},{8,12},{12,8},{9,1... | collective-permute-start | bytes 393224 | tf_op jit(solution)/shard_map/ppermute | solution.py:31
  19.2 1.0 %copy-start.7 = (bf16[256,1024]{1,0:T(8,128)(2,1)S(1)}, bf16[256,1024]{1,0:T(8,128)(2,1)}, u32[]{:S(2)}) copy-start(bf16[256,1024]{1,0:T(8,128)(2,1)} %w_out.1) | copy-start | bytes 1572868
  20.2 0.7 copy-start.9
  20.9 0.7 copy-start.10
  23.8 5.7 %collective-permute-start.5 = (bf16[32,1024]{1,0:T(8,128)(2,1)S(1)}, bf16[32,1024]{1,0:T(8,128)(2,1)S(1)}, u32[]{:S(2)}, u32[]{:S(2)}) collective-permute-start(bf16[32,1024]{1,0:T(8,128)(2,1)S(1)} %get-tuple-element.26), channel_id=1, source_target_pairs={{0,1},{1,0},{2,3},{3,2},{4,5},{5,4},{6,7},{7,6},{8,9},{9,8},{10,11... | collective-permute-start | bytes 196616 | tf_op jit(solution)/shard_map/ppermute | solution.py:26
  23.8 7.7 %collective-permute-start.6 = (bf16[32,1024]{1,0:T(8,128)(2,1)S(1)}, bf16[32,1024]{1,0:T(8,128)(2,1)S(1)}, u32[]{:S(2)}, u32[]{:S(2)}) collective-permute-start(bf16[32,1024]{1,0:T(8,128)(2,1)S(1)} %get-tuple-element.27), channel_id=1, source_target_pairs={{0,2},{1,3},{2,0},{3,1},{4,6},{5,7},{6,4},{7,5},{8,10},{9,11},{10,... | collective-permute-start | bytes 196616 | tf_op jit(solution)/shard_map/ppermute | solution.py:26
  26.2 6.1 %collective-permute-start.7 = (bf16[32,1024]{1,0:T(8,128)(2,1)S(1)}, bf16[32,1024]{1,0:T(8,128)(2,1)S(1)}, u32[]{:S(2)}, u32[]{:S(2)}) collective-permute-start(bf16[32,1024]{1,0:T(8,128)(2,1)S(1)} %get-tuple-element.28), channel_id=1, source_target_pairs={{0,3},{1,2},{2,1},{3,0},{4,7},{5,6},{6,5},{7,4},{8,11},{9,10},{10,... | collective-permute-start | bytes 196616 | tf_op jit(solution)/shard_map/ppermute | solution.py:26
  33.1 6.7 %collective-permute-start.10 = (bf16[32,1024]{1,0:T(8,128)(2,1)S(1)}, bf16[32,1024]{1,0:T(8,128)(2,1)S(1)}, u32[]{:S(2)}, u32[]{:S(2)}) collective-permute-start(bf16[32,1024]{1,0:T(8,128)(2,1)S(1)} %get-tuple-element.30.refs_0_), channel_id=1, source_target_pairs={{0,3},{1,2},{2,1},{3,0},{4,7},{5,6},{6,5},{7,4},{8,11},{9,10},{10,... | collective-permute-start | bytes 196616 | tf_op jit(solution)/shard_map/ppermute | solution.py:26
  35.8 5.2 %collective-permute-start.8 = (bf16[32,1024]{1,0:T(8,128)(2,1)S(1)}, bf16[32,1024]{1,0:T(8,128)(2,1)S(1)}, u32[]{:S(2)}, u32[]{:S(2)}) collective-permute-start(bf16[32,1024]{1,0:T(8,128)(2,1)S(1)} %get-tuple-element.30.refs_0_), channel_id=1, source_target_pairs={{0,1},{1,0},{2,3},{3,2},{4,5},{5,4},{6,7},{7,6},{8,9},{9,8},{10,11... | collective-permute-start | bytes 196616 | tf_op jit(solution)/shard_map/ppermute | solution.py:26
  36.5 5.2 %collective-permute-start.9 = (bf16[32,1024]{1,0:T(8,128)(2,1)S(1)}, bf16[32,1024]{1,0:T(8,128)(2,1)S(1)}, u32[]{:S(2)}, u32[]{:S(2)}) collective-permute-start(bf16[32,1024]{1,0:T(8,128)(2,1)S(1)} %get-tuple-element.30.refs_0_), channel_id=1, source_target_pairs={{0,2},{1,3},{2,0},{3,1},{4,6},{5,7},{6,4},{7,5},{8,10},{9,11},{10,... | collective-permute-start | bytes 196616 | tf_op jit(solution)/shard_map/ppermute | solution.py:26
  41.7 1.0 %copy-start.6 = (bf16[256,1024]{1,0:T(8,128)(2,1)S(1)}, bf16[256,1024]{1,0:T(8,128)(2,1)}, u32[]{:S(2)}) copy-start(bf16[256,1024]{1,0:T(8,128)(2,1)} %w_cross_out.1) | copy-start | bytes 1572868
  43.7 4.5 %collective-permute-start.11 = (bf16[32,1024]{1,0:T(8,128)(2,1)S(1)}, bf16[32,1024]{1,0:T(8,128)(2,1)S(1)}, u32[]{:S(2)}, u32[]{:S(2)}) collective-permute-start(bf16[32,1024]{1,0:T(8,128)(2,1)S(1)} %get-tuple-element.32), channel_id=1, source_target_pairs={{0,1},{1,0},{2,3},{3,2},{4,5},{5,4},{6,7},{7,6},{8,9},{9,8},{10,11... | collective-permute-start | bytes 196616 | tf_op jit(solution)/shard_map/ppermute | solution.py:26
  45.0 6.6 %collective-permute-start.12 = (bf16[32,1024]{1,0:T(8,128)(2,1)S(1)}, bf16[32,1024]{1,0:T(8,128)(2,1)S(1)}, u32[]{:S(2)}, u32[]{:S(2)}) collective-permute-start(bf16[32,1024]{1,0:T(8,128)(2,1)S(1)} %get-tuple-element.33), channel_id=1, source_target_pairs={{0,2},{1,3},{2,0},{3,1},{4,6},{5,7},{6,4},{7,5},{8,10},{9,11},{10,... | collective-permute-start | bytes 196616 | tf_op jit(solution)/shard_map/ppermute | solution.py:26
  47.3 6.1 %collective-permute-start.13 = (bf16[32,1024]{1,0:T(8,128)(2,1)S(1)}, bf16[32,1024]{1,0:T(8,128)(2,1)S(1)}, u32[]{:S(2)}, u32[]{:S(2)}) collective-permute-start(bf16[32,1024]{1,0:T(8,128)(2,1)S(1)} %get-tuple-element.34), channel_id=1, source_target_pairs={{0,3},{1,2},{2,1},{3,0},{4,7},{5,6},{6,5},{7,4},{8,11},{9,10},{10,... | collective-permute-start | bytes 196616 | tf_op jit(solution)/shard_map/ppermute | solution.py:26
  53.6 5.1 %collective-permute-start.14 = (bf16[32,1024]{1,0:T(8,128)(2,1)S(1)}, bf16[32,1024]{1,0:T(8,128)(2,1)S(1)}, u32[]{:S(2)}, u32[]{:S(2)}) collective-permute-start(bf16[32,1024]{1,0:T(8,128)(2,1)S(1)} %get-tuple-element.36.refs_0_), channel_id=1, source_target_pairs={{0,1},{1,0},{2,3},{3,2},{4,5},{5,4},{6,7},{7,6},{8,9},{9,8},{10,11... | collective-permute-start | bytes 196616 | tf_op jit(solution)/shard_map/ppermute | solution.py:26
  53.7 5.3 %collective-permute-start.15 = (bf16[32,1024]{1,0:T(8,128)(2,1)S(1)}, bf16[32,1024]{1,0:T(8,128)(2,1)S(1)}, u32[]{:S(2)}, u32[]{:S(2)}) collective-permute-start(bf16[32,1024]{1,0:T(8,128)(2,1)S(1)} %get-tuple-element.36.refs_0_), channel_id=1, source_target_pairs={{0,2},{1,3},{2,0},{3,1},{4,6},{5,7},{6,4},{7,5},{8,10},{9,11},{10,... | collective-permute-start | bytes 196616 | tf_op jit(solution)/shard_map/ppermute | solution.py:26
  55.1 6.1 %collective-permute-start.16 = (bf16[32,1024]{1,0:T(8,128)(2,1)S(1)}, bf16[32,1024]{1,0:T(8,128)(2,1)S(1)}, u32[]{:S(2)}, u32[]{:S(2)}) collective-permute-start(bf16[32,1024]{1,0:T(8,128)(2,1)S(1)} %get-tuple-element.36.refs_0_), channel_id=1, source_target_pairs={{0,3},{1,2},{2,1},{3,0},{4,7},{5,6},{6,5},{7,4},{8,11},{9,10},{10,... | collective-permute-start | bytes 196616 | tf_op jit(solution)/shard_map/ppermute | solution.py:26
  61.2 2.2 %copy-start = (bf16[1024,2048]{1,0:T(8,128)(2,1)S(1)}, bf16[1024,2048]{1,0:T(8,128)(2,1)}, u32[]{:S(2)}) copy-start(bf16[1024,2048]{1,0:T(8,128)(2,1)} %w_up.1) | copy-start | bytes 12582916
  66.9 4.9 %collective-permute-start.17 = (bf16[32,1024]{1,0:T(8,128)(2,1)S(1)}, bf16[32,1024]{1,0:T(8,128)(2,1)S(1)}, u32[]{:S(2)}, u32[]{:S(2)}) collective-permute-start(bf16[32,1024]{1,0:T(8,128)(2,1)S(1)} %get-tuple-element.38), channel_id=1, source_target_pairs={{0,1},{1,0},{2,3},{3,2},{4,5},{5,4},{6,7},{7,6},{8,9},{9,8},{10,11... | collective-permute-start | bytes 196616 | tf_op jit(solution)/shard_map/ppermute | solution.py:26
  67.7 5.2 %collective-permute-start.18 = (bf16[32,1024]{1,0:T(8,128)(2,1)S(1)}, bf16[32,1024]{1,0:T(8,128)(2,1)S(1)}, u32[]{:S(2)}, u32[]{:S(2)}) collective-permute-start(bf16[32,1024]{1,0:T(8,128)(2,1)S(1)} %get-tuple-element.39), channel_id=1, source_target_pairs={{0,2},{1,3},{2,0},{3,1},{4,6},{5,7},{6,4},{7,5},{8,10},{9,11},{10,... | collective-permute-start | bytes 196616 | tf_op jit(solution)/shard_map/ppermute | solution.py:26
  70.4 6.1 %collective-permute-start.19 = (bf16[32,1024]{1,0:T(8,128)(2,1)S(1)}, bf16[32,1024]{1,0:T(8,128)(2,1)S(1)}, u32[]{:S(2)}, u32[]{:S(2)}) collective-permute-start(bf16[32,1024]{1,0:T(8,128)(2,1)S(1)} %get-tuple-element.40), channel_id=1, source_target_pairs={{0,3},{1,2},{2,1},{3,0},{4,7},{5,6},{6,5},{7,4},{8,11},{9,10},{10,... | collective-permute-start | bytes 196616 | tf_op jit(solution)/shard_map/ppermute | solution.py:26

commit v3 on v2

v3 whole, which is shorter than its diff:
```python
import functools

import jax
import jax.numpy as jnp
from jax import lax
from jax.experimental import pallas as pl
from jax.experimental.pallas import tpu as pltpu
from jax.sharding import PartitionSpec as P

HEAD_DIM = 64
SPAN = 8
SINK = 4
WINDOW = 1024
SCALE = HEAD_DIM ** (-0.5)
EPS = 1e-05
SMALL_VMEM = 12 << 20
KERNEL_FLOPS = 4 * 10**9
WIDE_SCORES = 8 << 20

bf16 = jnp.bfloat16
f32 = jnp.float32
i32 = jnp.int32


def swap(array, axis, by):
    count = lax.axis_size(axis)
    return lax.ppermute(array, axis, [(i, i ^ by) for i in range(count)])


def from_behind(array, axis, by):
    count = lax.axis_size(axis)
    return lax.ppermute(array, axis, [(i, (i + by) % count) for i in range(count)])


def gather_heads(array):
    return [array] + [swap(array, "head", by) for by in range(1, lax.axis_size("head"))]


def scatter_heads(pieces):
    return [pieces[0]] + [swap(piece, "head", by) for by, piece in enumerate(pieces) if by]


def kernel_call(body, outs, vmem_bytes, scratch, specs, out_specs, *args):
    return pl.pallas_call(
        body,
        out_shape=outs,
        in_specs=list(specs) + [pl.BlockSpec()] * (len(args) - len(specs)),
        out_specs=out_specs or [pl.BlockSpec()] * len(outs),
        scratch_shapes=scratch,
        compiler_params=pltpu.CompilerParams(vmem_limit_bytes=vmem_bytes),
        cost_estimate=pl.CostEstimate(
            flops=KERNEL_FLOPS, bytes_accessed=sum(a.nbytes for a in args), transcendentals=0
        ),
    )(*args)


scalars = pl.BlockSpec(memory_space=pltpu.SMEM)
in_hbm = pl.BlockSpec(memory_space=pltpu.HBM)


def layer_norm(values):
    center = values - jnp.mean(values, axis=-1, keepdims=True)
    spread = jnp.mean(center * center, axis=-1, keepdims=True)
    return center * lax.rsqrt(spread + EPS)


def dot(left, right):
    return jnp.dot(left, right, preferred_element_type=f32)


def split_pair(pairs):
    rows, _, width = pairs.shape
    flat = pairs.astype(f32).reshape(rows, 2 * width).astype(bf16)
    return flat[:, :width], flat[:, width:]


def head_lanes(shape):
    return lax.broadcasted_iota(i32, shape, len(shape) - 1) // HEAD_DIM


def attend_heads(queries, keys, values, bias, heads):
    rows, width = queries.shape
    lanes = head_lanes((rows, width))
    stacked = jnp.concatenate(
        [jnp.where(lanes == h, queries, jnp.zeros_like(queries)) for h in heads], axis=0
    )
    scores = lax.dot_general(
        stacked, keys, (((1,), (1,)), ((), ())), preferred_element_type=f32
    ).reshape(len(heads), rows, keys.shape[0])
    scores = scores * SCALE
    if bias is not None:
        scores = scores + bias[None]
    row_max = jnp.max(scores, axis=-1, keepdims=True)
    weights = jnp.exp(scores - row_max)
    row_sum = jnp.sum(weights, axis=-1, keepdims=True)
    summed = dot(weights.astype(bf16).reshape(len(heads) * rows, -1), values)
    summed = summed.reshape(len(heads), rows, width) / row_sum
    result = jnp.zeros((rows, width), f32)
    for i, h in enumerate(heads):
        result = jnp.where(lanes == h, summed[i], result)
    return result


def attend(queries, keys, values, bias):
    rows, width = queries.shape
    heads = list(range(width // HEAD_DIM))
    if len(heads) * rows * keys.shape[0] * 4 <= WIDE_SCORES:
        return attend_heads(queries, keys, values, bias, heads).astype(bf16)
    result = attend_heads(queries, keys, values, bias, heads[:1])
    for h in heads[1:]:
        result = result + attend_heads(queries, keys, values, bias, [h])
    return result.astype(bf16)


def request_info(token_ids, length_of, requests):
    request = jnp.zeros_like(token_ids)
    first_token = jnp.zeros_like(token_ids)
    end = jnp.int32(0)
    for i in range(requests):
        end = end + length_of(i)
        before = end <= token_ids
        request = request + before.astype(i32)
        first_token = jnp.where(before, first_token + length_of(i), first_token)
    return request, token_ids - first_token


def columns_body(place, pool, *outs):
    width = outs[0].shape[-1]
    for by, out in enumerate(outs):
        first = pl.multiple_of((place[1] ^ by) * width, width)
        out[...] = pool[0, :, :, :, pl.ds(first, width)]


def project_body(
    sizes, place, lengths_in, table_in, tokens, w_query, w_keyvalue, queries, keyvalue, bias, residual,
    lengths, table, sems,
):
    near, tok_count, head_count, shard_blocks, block_len = sizes
    requests = lengths.shape[1]
    copies = [
        pltpu.make_async_copy(lengths_in, lengths, sems.at[0]),
        pltpu.make_async_copy(table_in, table, sems.at[1]),
    ]
    for copy in copies:
        copy.start()
    normed = layer_norm(tokens[0].astype(f32)).astype(bf16)
    queries[...] = dot(normed, w_query[...]).astype(bf16)
    w_key, w_value = split_pair(w_keyvalue[...])
    rows, width = queries.shape
    keyvalue[:, :width] = dot(normed, w_key).astype(bf16)
    keyvalue[:, width:] = dot(normed, w_value).astype(bf16)

    for copy in copies:
        copy.wait()
    tok_index, head_index = place[0], place[1]
    share = residual.shape[0]
    start = pl.multiple_of(head_index * share, share)
    residual[...] = tokens[0, pl.ds(start, share), :].astype(f32)

    def length_of(i):
        return lengths[0, i]

    own_ids = tok_index * rows + lax.broadcasted_iota(i32, (rows, 1), 0)
    own_request, own_offset = request_info(own_ids, length_of, requests)
    for distance in range(near):
        ids = (tok_index - distance) * rows + lax.broadcasted_iota(i32, (1, rows), 1)
        allowed = (
            (ids >= 0)
            & (request_info(ids, length_of, requests)[0] == own_request)
            & (ids <= own_ids)
            & (own_ids - ids < WINDOW)
        )
        bias[:, distance * rows : (distance + 1) * rows] = jnp.where(allowed, 0.0, -jnp.inf)
    shard = head_count * shard_blocks * block_len
    prefix_len = tok_count * shard
    slot = lax.broadcasted_iota(i32, (1, shard), 1)
    for far in range(tok_count):
        places = slot % block_len
        for block in range(head_count * shard_blocks):
            owner = (tok_index ^ far) * head_count + (head_index ^ (block // shard_blocks))
            logical = table[0, owner * shard_blocks + block % shard_blocks]
            places = places + jnp.where(slot // block_len == block, logical * block_len, 0)
        allowed = (places < SINK) | (places > prefix_len + own_offset - WINDOW)
        first = near * rows + far * shard
        bias[:, first : first + shard] = jnp.where(allowed, 0.0, -jnp.inf)


def self_body(near, head_count, place, queries, bias, w_out, *refs):
    term, refs = refs[-1], refs[:-1]
    near_refs, refs = refs[:near], refs[near:]
    slot_refs, outs = refs[:-head_count], refs[-head_count:]
    rows, width = queries.shape
    keys = [ref[:, :width] for ref in near_refs]
    values = [ref[:, width:] for ref in near_refs]
    for ref in slot_refs:
        key, value = split_pair(ref[...].reshape(ref.shape[0] * ref.shape[1], 2, width))
        keys.append(key)
        values.append(value)
    attended = attend(
        queries[...], jnp.concatenate(keys, axis=0), jnp.concatenate(values, axis=0), bias[...]
    )
    share = rows // head_count
    term[...] = dot(attended, w_out[...]).astype(bf16)
    for by, out in enumerate(outs):
        start = pl.multiple_of((place[1] ^ by) * share, share)
        out[...] = term[pl.ds(start, share), :]


def cross_body(head_count, w_cross_query, cross_cache, w_cross_out, *refs):
    rows_in, outs = refs[:head_count], refs[head_count:]
    normed = jnp.concatenate([ref[...] for ref in rows_in], axis=0)
    queries = dot(normed, w_cross_query[...]).astype(bf16)
    keys, values = split_pair(cross_cache[0])
    cross_out = attend(queries, keys, values, None)
    term = dot(cross_out, w_cross_out[...]).astype(bf16)
    share = rows_in[0].shape[0]
    for by, out in enumerate(outs):
        out[...] = term[by * share : (by + 1) * share]


def after_body(before, *refs):
    terms, (after, normed) = refs[:-2], refs[-2:]
    total = before[...] + sum(term[...].astype(f32) for term in terms)
    after[...] = total
    normed[...] = layer_norm(total).astype(bf16)


def hidden_body(head_count, w_up, w_down, *refs):
    rows_in, outs = refs[:head_count], refs[head_count:]
    normed = jnp.concatenate([ref[...] for ref in rows_in], axis=0)
    hidden = jax.nn.relu(dot(normed, w_up[...])).astype(bf16)
    term = dot(hidden, w_down[...]).astype(bf16)
    share = rows_in[0].shape[0]
    for by, out in enumerate(outs):
        out[...] = term[by * share : (by + 1) * share]


def on_device(
    tokens,
    lengths,
    block_position,
    prefix_pool,
    cross_cache,
    w_query,
    w_keyvalue,
    w_out,
    w_cross_query,
    w_cross_out,
    w_up,
    w_down,
):
    rows, model_width = tokens.shape[1:]
    width = w_query.shape[1]
    tok_index, head_index = lax.axis_index("tok"), lax.axis_index("head")
    tok_count, head_count = lax.axis_size("tok"), lax.axis_size("head")
    share = rows // head_count
    place = jnp.stack([tok_index, head_index]).astype(i32)
    shard_blocks, block_len = prefix_pool.shape[1:3]
    near_count = 1 + min(SPAN, tok_count - 1)
    key_count = near_count * rows + block_position.shape[1] * block_len
    sizes = (near_count, tok_count, head_count, shard_blocks, block_len)
    shape = jax.ShapeDtypeStruct
    row_pieces = [shape((share, model_width), bf16)] * head_count
    stats = [shape((share, model_width), f32), shape((share, model_width), bf16)]

    pool_columns = kernel_call(
        columns_body,
        [shape((shard_blocks, block_len, 2, width), bf16)] * head_count,
        SMALL_VMEM,
        [],
        [scalars],
        None,
        place,
        prefix_pool,
    )
    slots = scatter_heads(pool_columns)
    queries, keyvalue, bias, residual = kernel_call(
        functools.partial(project_body, sizes),
        [
            shape((rows, width), bf16),
            shape((rows, 2 * width), bf16),
            shape((rows, key_count), f32),
            shape((share, model_width), f32),
        ],
        2 * SMALL_VMEM,
        [
            pltpu.SMEM(lengths.shape, i32),
            pltpu.SMEM(block_position.shape, i32),
            pltpu.SemaphoreType.DMA((2,)),
        ],
        [scalars, in_hbm, in_hbm],
        None,
        place,
        lengths,
        block_position,
        tokens,
        w_query,
        w_keyvalue,
    )
    near = [keyvalue] + [
        from_behind(keyvalue, "tok", distance) for distance in range(1, near_count)
    ]
    all_slots = list(slots)
    for by in range(1, tok_count):
        for piece in slots:
            all_slots.append(swap(lax.optimization_barrier((piece, keyvalue))[0], "tok", by))
    terms = kernel_call(
        functools.partial(self_body, near_count, head_count),
        row_pieces,
        SMALL_VMEM + 36 * rows * key_count,
        [pltpu.VMEM((rows, model_width), bf16)],
        [scalars],
        None,
        place,
        queries,
        bias,
        w_out,
        *near,
        *all_slots,
    )
    after_self, normed = kernel_call(
        after_body, stats, SMALL_VMEM, [], [], None, residual, *scatter_heads(terms)
    )
    terms = kernel_call(
        functools.partial(cross_body, head_count),
        row_pieces,
        SMALL_VMEM,
        [],
        [],
        None,
        w_cross_query,
        cross_cache,
        w_cross_out,
        *gather_heads(normed),
    )
    after_cross, normed = kernel_call(
        after_body, stats, SMALL_VMEM, [], [], None, after_self, *scatter_heads(terms)
    )
    terms = kernel_call(
        functools.partial(hidden_body, head_count),
        row_pieces,
        2 * SMALL_VMEM,
        [],
        [],
        None,
        w_up,
        w_down,
        *gather_heads(normed),
    )
    result = after_cross + sum(term.astype(f32) for term in scatter_heads(terms))
    return result.astype(bf16)[None]


def solution(mesh):
    return jax.shard_map(
        on_device,
        mesh=mesh,
        in_specs=(
            P("grp", "tok", None),
            P("grp", None),
            P("grp", None),
            P("grp", ("tok", "head"), None, None, None),
            P("grp", None, None, "head"),
            P(None, "head"),
            P(None, None, "head"),
            P("head", None),
            P(None, "head"),
            P("head", None),
            P(None, "head"),
            P("head", None),
        ),
        out_specs=P("grp", ("tok", "head"), None),
        check_vma=False,
    )
```

time: 77.6 us -> 63.1 us (0.81)
  local copies, waits for them, and re-layouts: 10 us -> 0.99 us
  waiting for transfers between devices: 28.8 us -> 25.1 us
  Pallas kernels: 8.49 us -> 6.94 us
    unnamed x22 -> x24, local copies, waits for them, and re-layouts: 8.8 us -> 0.99 us
    ppermute x19 -> x22, waiting for transfers between devices: 27.9 us -> 25.1 us  [swap(): return lax.ppermute(array, axis, [(i, i ^ by) for i in range(count)])]
    pallas_call x6 -> x7, Pallas kernels: 8.49 us -> 6.94 us  [kernel_call(): pl.pallas_call(body, out_shape=outs, in_specs=list(specs) + [pl.BlockSpec...]
    dynamic_slice x1 -> x0, local copies, waits for them, and re-layouts: 1.22 us -> none  [on_device(): lax.dynamic_slice_in_dim(prefix_pool[0], (head_index ^ by) * width, width...]
    ppermute x19 -> x22, starting transfers between devices: 28 us -> 29 us  [swap(): return lax.ppermute(array, axis, [(i, i ^ by) for i in range(count)])]
    ppermute x1, waiting for transfers between devices: 0.91 us -> 0.01 us  [from_behind(): lax.ppermute(array, axis, [(i, (i + by) % count) for i in range(count)])]
  transfers between devices with their start and end apart: 20 -> 23, of which waited for: 17 -> 17; matrix products, arithmetic and copies ran while one was open for 0% -> 0% of each run, Pallas kernels for 1% -> 3%
where the time goes in v3:
time: 63.1 us; the launch traced here: 63 us
  starting transfers between devices  29.1 us (46%)
  waiting for transfers between devices  25.1 us (40%)
  Pallas kernels  6.94 us (11%)
  local copies, waits for them, and re-layouts  0.99 us (2%)
  other arithmetic  0.75 us (1%)
    ppermute x22, starting transfers between devices, swap(): return lax.ppermute(array, axis, [(i, i ^ by) for i in range(count)])  29 us
    ppermute x22, waiting for transfers between devices, swap(): return lax.ppermute(array, axis, [(i, i ^ by) for i in range(count)])  25.1 us
    pallas_call x7, Pallas kernels, kernel_call(): pl.pallas_call(body, out_shape=outs, in_specs=list(specs) + [pl.BlockSpec...  6.94 us
  transfers between devices with their start and end apart: 23, of which 17 were waited for; matrix products, arithmetic and copies ran while one was open for 0% of the time, Pallas kernels for 3%

profile of v3, /device:TPU:0, one launch (start us, length us, event | category | flops | bytes accessed | tf_op | source)
XLA Modules:
  0.0 63.0 jit_solution(195581678652932290)
XLA Ops:
  0.1 0.9 %copy-done.7 = bf16[1,4,16,2,1024]{4,3,2,1,0:T(2,128)(2,1)S(1)} copy-done((bf16[1,4,16,2,1024]{4,3,2,1,0:T(2,128)(2,1)S(1)}, bf16[1,4,16,2,1024]{4,3,2,1,0:T(2,128)(2,1)}, u32[]{:S(2)}) %copy-start.7) | copy-done | bytes 262168
  1.7 3.1 %collective-permute-start.1 = (bf16[4,16,2,256]{3,2,1,0:T(2,128)(2,1)S(1)}, bf16[4,16,2,256]{3,2,1,0:T(2,128)(2,1)S(1)}, u32[]{:S(2)}, u32[]{:S(2)}) collective-permute-start(bf16[4,16,2,256]{3,2,1,0:T(2,128)(2,1)S(1)} %get-tuple-element.38), channel_id=1, source_target_pairs={{0,1},{1,0},{2,3},{3,2},{4,5},{5,4},{6,7},{7,6},{8,9},{9,8},{10,11... | collective-permute-start | bytes 196616 | tf_op jit(solution)/shard_map/ppermute | solution.py:27
  4.8 2.6 %collective-permute-start.2 = (bf16[4,16,2,256]{3,2,1,0:T(2,128)(2,1)S(1)}, bf16[4,16,2,256]{3,2,1,0:T(2,128)(2,1)S(1)}, u32[]{:S(2)}, u32[]{:S(2)}) collective-permute-start(bf16[4,16,2,256]{3,2,1,0:T(2,128)(2,1)S(1)} %get-tuple-element.39), channel_id=1, source_target_pairs={{0,2},{1,3},{2,0},{3,1},{4,6},{5,7},{6,4},{7,5},{8,10},{9,11},{10,... | collective-permute-start | bytes 196616 | tf_op jit(solution)/shard_map/ppermute | solution.py:27
  7.4 1.7 %shard_map.118 = (bf16[128,256]{1,0:T(8,128)(2,1)S(1)}, bf16[128,512]{1,0:T(8,128)(2,1)S(1)}, f32[128,768]{1,0:T(8,128)S(1)}, f32[32,1024]{1,0:T(8,128)S(1)}) custom-call(s32[2]{0:T(128)S(1)} %pad_add_fusion.place, s32[1,8]{1,0:T(1,128)S(1)} %copy-done.10, s32[1,32]{1,0:T(1,128)S(1)} %copy-done.11, bf16[1,128,1024]{2,1,0:T(8,128)(2,1)S(1)} %copy-done.8, ...), custom_call_target="tpu_custom_call" | custom-call | flops 4000000000 | bytes 1835176 | tf_op jit(solution)/shard_map/pallas_call | solution.py:44
  9.7 3.7 %collective-permute-done.3.refs_5_ = bf16[4,16,2,256]{3,2,1,0:T(2,128)(2,1)S(1)} collective-permute-done((bf16[4,16,2,256]{3,2,1,0:T(2,128)(2,1)S(1)}, bf16[4,16,2,256]{3,2,1,0:T(2,128)(2,1)S(1)}, u32[]{:S(2)}, u32[]{:S(2)}) %collective-permute-start.3) | collective-permute-done | bytes 65568 | tf_op jit(solution)/shard_map/ppermute | solution.py:27
  14.0 0.7 %collective-permute-done.5.refs_7_ = bf16[4,16,2,256]{3,2,1,0:T(2,128)(2,1)S(1)} collective-permute-done((bf16[4,16,2,256]{3,2,1,0:T(2,128)(2,1)S(1)}, bf16[4,16,2,256]{3,2,1,0:T(2,128)(2,1)S(1)}, u32[]{:S(2)}, u32[]{:S(2)}) %collective-permute-start.5) | collective-permute-done | bytes 65568 | tf_op jit(solution)/shard_map/ppermute | solution.py:27
  15.2 1.9 %shard_map.120 = (bf16[32,1024]{1,0:T(8,128)(2,1)S(1)}, bf16[32,1024]{1,0:T(8,128)(2,1)S(1)}, bf16[32,1024]{1,0:T(8,128)(2,1)S(1)}, bf16[32,1024]{1,0:T(8,128)(2,1)S(1)}) custom-call(s32[2]{0:T(128)S(1)} %pad_add_fusion.place, bf16[128,256]{1,0:T(8,128)(2,1)S(1)} %get-tuple-element.34.queries, f32[128,768]{1,0:T(8,128)S(1)} %get-tuple-element.35.bias, ...), custom_call_target="tpu_custom_call" | custom-call | flops 4000000000 | bytes 1769480 | tf_op jit(solution)/shard_map/pallas_call | solution.py:44
  17.3 2.3 %collective-permute-start.9 = (bf16[32,1024]{1,0:T(8,128)(2,1)S(1)}, bf16[32,1024]{1,0:T(8,128)(2,1)S(1)}, u32[]{:S(2)}, u32[]{:S(2)}) collective-permute-start(bf16[32,1024]{1,0:T(8,128)(2,1)S(1)} %get-tuple-element.47), channel_id=1, source_target_pairs={{0,2},{1,3},{2,0},{3,1},{4,6},{5,7},{6,4},{7,5},{8,10},{9,11},{10,... | collective-permute-start | bytes 196616 | tf_op jit(solution)/shard_map/ppermute | solution.py:27
  19.6 2.1 %collective-permute-start.10 = (bf16[32,1024]{1,0:T(8,128)(2,1)S(1)}, bf16[32,1024]{1,0:T(8,128)(2,1)S(1)}, u32[]{:S(2)}, u32[]{:S(2)}) collective-permute-start(bf16[32,1024]{1,0:T(8,128)(2,1)S(1)} %get-tuple-element.48), channel_id=1, source_target_pairs={{0,3},{1,2},{2,1},{3,0},{4,7},{5,6},{6,5},{7,4},{8,11},{9,10},{10,... | collective-permute-start | bytes 196616 | tf_op jit(solution)/shard_map/ppermute | solution.py:27
  21.6 1.1 %collective-permute-done.8.refs_1_ = bf16[32,1024]{1,0:T(8,128)(2,1)S(1)} collective-permute-done((bf16[32,1024]{1,0:T(8,128)(2,1)S(1)}, bf16[32,1024]{1,0:T(8,128)(2,1)S(1)}, u32[]{:S(2)}, u32[]{:S(2)}) %collective-permute-start.8) | collective-permute-done | bytes 65568 | tf_op jit(solution)/shard_map/ppermute | solution.py:27
  22.7 2.1 %collective-permute-done.9.refs_2_ = bf16[32,1024]{1,0:T(8,128)(2,1)S(1)} collective-permute-done((bf16[32,1024]{1,0:T(8,128)(2,1)S(1)}, bf16[32,1024]{1,0:T(8,128)(2,1)S(1)}, u32[]{:S(2)}, u32[]{:S(2)}) %collective-permute-start.9) | collective-permute-done | bytes 65568 | tf_op jit(solution)/shard_map/ppermute | solution.py:27
  24.8 0.8 %collective-permute-done.10.refs_3_ = bf16[32,1024]{1,0:T(8,128)(2,1)S(1)} collective-permute-done((bf16[32,1024]{1,0:T(8,128)(2,1)S(1)}, bf16[32,1024]{1,0:T(8,128)(2,1)S(1)}, u32[]{:S(2)}, u32[]{:S(2)}) %collective-permute-start.10) | collective-permute-done | bytes 65568 | tf_op jit(solution)/shard_map/ppermute | solution.py:27
  25.9 2.6 %collective-permute-start.13 = (bf16[32,1024]{1,0:T(8,128)(2,1)S(1)}, bf16[32,1024]{1,0:T(8,128)(2,1)S(1)}, u32[]{:S(2)}, u32[]{:S(2)}) collective-permute-start(bf16[32,1024]{1,0:T(8,128)(2,1)S(1)} %get-tuple-element.50.refs_0_), channel_id=1, source_target_pairs={{0,3},{1,2},{2,1},{3,0},{4,7},{5,6},{6,5},{7,4},{8,11},{9,10},{10,... | collective-permute-start | bytes 196616 | tf_op jit(solution)/shard_map/ppermute | solution.py:27
  29.0 1.4 %collective-permute-start.11 = (bf16[32,1024]{1,0:T(8,128)(2,1)S(1)}, bf16[32,1024]{1,0:T(8,128)(2,1)S(1)}, u32[]{:S(2)}, u32[]{:S(2)}) collective-permute-start(bf16[32,1024]{1,0:T(8,128)(2,1)S(1)} %get-tuple-element.50.refs_0_), channel_id=1, source_target_pairs={{0,1},{1,0},{2,3},{3,2},{4,5},{5,4},{6,7},{7,6},{8,9},{9,8},{10,11... | collective-permute-start | bytes 196616 | tf_op jit(solution)/shard_map/ppermute | solution.py:27
  30.4 2.2 %collective-permute-done.13.refs_3_ = bf16[32,1024]{1,0:T(8,128)(2,1)S(1)} collective-permute-done((bf16[32,1024]{1,0:T(8,128)(2,1)S(1)}, bf16[32,1024]{1,0:T(8,128)(2,1)S(1)}, u32[]{:S(2)}, u32[]{:S(2)}) %collective-permute-start.13) | collective-permute-done | bytes 65568 | tf_op jit(solution)/shard_map/ppermute | solution.py:27
  32.6 2.2 %collective-permute-done.12.refs_2_ = bf16[32,1024]{1,0:T(8,128)(2,1)S(1)} collective-permute-done((bf16[32,1024]{1,0:T(8,128)(2,1)S(1)}, bf16[32,1024]{1,0:T(8,128)(2,1)S(1)}, u32[]{:S(2)}, u32[]{:S(2)}) %collective-permute-start.12) | collective-permute-done | bytes 65568 | tf_op jit(solution)/shard_map/ppermute | solution.py:27
  34.9 0.9 %shard_map.122 = (bf16[32,1024]{1,0:T(8,128)(2,1)S(1)}, bf16[32,1024]{1,0:T(8,128)(2,1)S(1)}, bf16[32,1024]{1,0:T(8,128)(2,1)S(1)}, bf16[32,1024]{1,0:T(8,128)(2,1)S(1)}) custom-call(bf16[1024,256]{1,0:T(8,128)(2,1)S(1)} %copy-done.5, bf16[1,256,2,256]{3,2,1,0:T(2,128)(2,1)S(1)} %copy-done.9, bf16[256,1024]{1,0:T(8,128)(2,1)S(1)} %copy-done.6, ...), custom_call_target="tpu_custom_call" | custom-call | flops 4000000000 | bytes 1572864 | tf_op jit(solution)/shard_map/pallas_call | solution.py:44
  35.9 2.9 %collective-permute-start.15 = (bf16[32,1024]{1,0:T(8,128)(2,1)S(1)}, bf16[32,1024]{1,0:T(8,128)(2,1)S(1)}, u32[]{:S(2)}, u32[]{:S(2)}) collective-permute-start(bf16[32,1024]{1,0:T(8,128)(2,1)S(1)} %get-tuple-element.53), channel_id=1, source_target_pairs={{0,2},{1,3},{2,0},{3,1},{4,6},{5,7},{6,4},{7,5},{8,10},{9,11},{10,... | collective-permute-start | bytes 196616 | tf_op jit(solution)/shard_map/ppermute | solution.py:27
  38.8 1.5 %collective-permute-start.16 = (bf16[32,1024]{1,0:T(8,128)(2,1)S(1)}, bf16[32,1024]{1,0:T(8,128)(2,1)S(1)}, u32[]{:S(2)}, u32[]{:S(2)}) collective-permute-start(bf16[32,1024]{1,0:T(8,128)(2,1)S(1)} %get-tuple-element.54), channel_id=1, source_target_pairs={{0,3},{1,2},{2,1},{3,0},{4,7},{5,6},{6,5},{7,4},{8,11},{9,10},{10,... | collective-permute-start | bytes 196616 | tf_op jit(solution)/shard_map/ppermute | solution.py:27
  40.3 2.8 %collective-permute-done.15.refs_2_ = bf16[32,1024]{1,0:T(8,128)(2,1)S(1)} collective-permute-done((bf16[32,1024]{1,0:T(8,128)(2,1)S(1)}, bf16[32,1024]{1,0:T(8,128)(2,1)S(1)}, u32[]{:S(2)}, u32[]{:S(2)}) %collective-permute-start.15) | collective-permute-done | bytes 65568 | tf_op jit(solution)/shard_map/ppermute | solution.py:27
  43.1 1.8 %collective-permute-done.16.refs_3_ = bf16[32,1024]{1,0:T(8,128)(2,1)S(1)} collective-permute-done((bf16[32,1024]{1,0:T(8,128)(2,1)S(1)}, bf16[32,1024]{1,0:T(8,128)(2,1)S(1)}, u32[]{:S(2)}, u32[]{:S(2)}) %collective-permute-start.16) | collective-permute-done | bytes 65568 | tf_op jit(solution)/shard_map/ppermute | solution.py:27
  45.2 1.6 %collective-permute-start.19 = (bf16[32,1024]{1,0:T(8,128)(2,1)S(1)}, bf16[32,1024]{1,0:T(8,128)(2,1)S(1)}, u32[]{:S(2)}, u32[]{:S(2)}) collective-permute-start(bf16[32,1024]{1,0:T(8,128)(2,1)S(1)} %get-tuple-element.56.refs_0_), channel_id=1, source_target_pairs={{0,3},{1,2},{2,1},{3,0},{4,7},{5,6},{6,5},{7,4},{8,11},{9,10},{10,... | collective-permute-start | bytes 196616 | tf_op jit(solution)/shard_map/ppermute | solution.py:27
  46.7 2.9 %collective-permute-start.17 = (bf16[32,1024]{1,0:T(8,128)(2,1)S(1)}, bf16[32,1024]{1,0:T(8,128)(2,1)S(1)}, u32[]{:S(2)}, u32[]{:S(2)}) collective-permute-start(bf16[32,1024]{1,0:T(8,128)(2,1)S(1)} %get-tuple-element.56.refs_0_), channel_id=1, source_target_pairs={{0,1},{1,0},{2,3},{3,2},{4,5},{5,4},{6,7},{7,6},{8,9},{9,8},{10,11... | collective-permute-start | bytes 196616 | tf_op jit(solution)/shard_map/ppermute | solution.py:27
  49.6 1.7 %collective-permute-done.19.refs_3_ = bf16[32,1024]{1,0:T(8,128)(2,1)S(1)} collective-permute-done((bf16[32,1024]{1,0:T(8,128)(2,1)S(1)}, bf16[32,1024]{1,0:T(8,128)(2,1)S(1)}, u32[]{:S(2)}, u32[]{:S(2)}) %collective-permute-start.19) | collective-permute-done | bytes 65568 | tf_op jit(solution)/shard_map/ppermute | solution.py:27
  51.3 1.4 %collective-permute-done.18.refs_2_ = bf16[32,1024]{1,0:T(8,128)(2,1)S(1)} collective-permute-done((bf16[32,1024]{1,0:T(8,128)(2,1)S(1)}, bf16[32,1024]{1,0:T(8,128)(2,1)S(1)}, u32[]{:S(2)}, u32[]{:S(2)}) %collective-permute-start.18) | collective-permute-done | bytes 65568 | tf_op jit(solution)/shard_map/ppermute | solution.py:27
  52.7 1.3 %shard_map.124 = (bf16[32,1024]{1,0:T(8,128)(2,1)S(1)}, bf16[32,1024]{1,0:T(8,128)(2,1)S(1)}, bf16[32,1024]{1,0:T(8,128)(2,1)S(1)}, bf16[32,1024]{1,0:T(8,128)(2,1)S(1)}) custom-call(bf16[1024,2048]{1,0:T(8,128)(2,1)S(1)} %copy-done, bf16[2048,1024]{1,0:T(8,128)(2,1)S(1)} %copy-done.1, bf16[32,1024]{1,0:T(8,128)(2,1)S(1)} %get-tuple-element.56.refs_0_, ...), custom_call_target="tpu_custom_call" | custom-call | flops 4000000000 | bytes 8650752 | tf_op jit(solution)/shard_map/pallas_call | solution.py:44
  54.0 1.2 %collective-permute-start.20 = (bf16[32,1024]{1,0:T(8,128)(2,1)S(1)}, bf16[32,1024]{1,0:T(8,128)(2,1)S(1)}, u32[]{:S(2)}, u32[]{:S(2)}) collective-permute-start(bf16[32,1024]{1,0:T(8,128)(2,1)S(1)} %get-tuple-element.58), channel_id=1, source_target_pairs={{0,1},{1,0},{2,3},{3,2},{4,5},{5,4},{6,7},{7,6},{8,9},{9,8},{10,11... | collective-permute-start | bytes 196616 | tf_op jit(solution)/shard_map/ppermute | solution.py:27
  55.2 0.9 %collective-permute-start.21 = (bf16[32,1024]{1,0:T(8,128)(2,1)S(1)}, bf16[32,1024]{1,0:T(8,128)(2,1)S(1)}, u32[]{:S(2)}, u32[]{:S(2)}) collective-permute-start(bf16[32,1024]{1,0:T(8,128)(2,1)S(1)} %get-tuple-element.59), channel_id=1, source_target_pairs={{0,2},{1,3},{2,0},{3,1},{4,6},{5,7},{6,4},{7,5},{8,10},{9,11},{10,... | collective-permute-start | bytes 196616 | tf_op jit(solution)/shard_map/ppermute | solution.py:27
  56.1 2.3 %collective-permute-start.22 = (bf16[32,1024]{1,0:T(8,128)(2,1)S(1)}, bf16[32,1024]{1,0:T(8,128)(2,1)S(1)}, u32[]{:S(2)}, u32[]{:S(2)}) collective-permute-start(bf16[32,1024]{1,0:T(8,128)(2,1)S(1)} %get-tuple-element.60), channel_id=1, source_target_pairs={{0,3},{1,2},{2,1},{3,0},{4,7},{5,6},{6,5},{7,4},{8,11},{9,10},{10,... | collective-permute-start | bytes 196616 | tf_op jit(solution)/shard_map/ppermute | solution.py:27
  58.8 2.3 %collective-permute-done.21 = bf16[32,1024]{1,0:T(8,128)(2,1)S(1)} collective-permute-done((bf16[32,1024]{1,0:T(8,128)(2,1)S(1)}, bf16[32,1024]{1,0:T(8,128)(2,1)S(1)}, u32[]{:S(2)}, u32[]{:S(2)}) %collective-permute-start.21) | collective-permute-done | bytes 65568 | tf_op jit(solution)/shard_map/ppermute | solution.py:27
  61.1 1.2 %collective-permute-done.22 = bf16[32,1024]{1,0:T(8,128)(2,1)S(1)} collective-permute-done((bf16[32,1024]{1,0:T(8,128)(2,1)S(1)}, bf16[32,1024]{1,0:T(8,128)(2,1)S(1)}, u32[]{:S(2)}, u32[]{:S(2)}) %collective-permute-start.22) | collective-permute-done | bytes 65568 | tf_op jit(solution)/shard_map/ppermute | solution.py:27
  62.3 0.7 %fusion = bf16[1,32,1024]{2,1,0:T(8,128)(2,1)} fusion(f32[32,1024]{1,0:T(8,128)S(1)} %get-tuple-element.55, bf16[32,1024]{1,0:T(8,128)(2,1)S(1)} %collective-permute-done.22, bf16[32,1024]{1,0:T(8,128)(2,1)S(1)} %collective-permute-done.21, bf16[32,1024]{1,0:T(8,128)(2,1)S(1)} %collective-permute-done.20, bf16[32,1024]{1,0:T(8,128)(2,1)S(1)} %get-tuple-element.57), kind=kLoop, calls=%fused_computation.1 | loop fusion | flops 294912 | bytes 458752 | tf_op jit(solution)/shard_map/broadcast_in_dim | solution.py:351
  (47 shorter events, 3.9 us)
Async XLA Ops:
  1.0 6.4 %copy-start.8 = (bf16[1,128,1024]{2,1,0:T(8,128)(2,1)S(1)}, bf16[1,128,1024]{2,1,0:T(8,128)(2,1)}, u32[]{:S(2)}) copy-start(bf16[1,128,1024]{2,1,0:T(8,128)(2,1)} %tokens.1) | copy-start | bytes 786436
  1.0 6.4 %copy-start.10 = (s32[1,8]{1,0:T(1,128)S(1)}, s32[1,8]{1,0:T(1,128)}, u32[]{:S(2)}) copy-start(s32[1,8]{1,0:T(1,128)} %lengths_in.1) | copy-start | bytes 100
  1.0 6.4 %copy-start.11 = (s32[1,32]{1,0:T(1,128)S(1)}, s32[1,32]{1,0:T(1,128)}, u32[]{:S(2)}) copy-start(s32[1,32]{1,0:T(1,128)} %table_in.1) | copy-start | bytes 388
  1.7 11.8 %collective-permute-start.1 = (bf16[4,16,2,256]{3,2,1,0:T(2,128)(2,1)S(1)}, bf16[4,16,2,256]{3,2,1,0:T(2,128)(2,1)S(1)}, u32[]{:S(2)}, u32[]{:S(2)}) collective-permute-start(bf16[4,16,2,256]{3,2,1,0:T(2,128)(2,1)S(1)} %get-tuple-element.38), channel_id=1, source_target_pairs={{0,1},{1,0},{2,3},{3,2},{4,5},{5,4},{6,7},{7,6},{8,9},{9,8},{10,11... | collective-permute-start | bytes 196616 | tf_op jit(solution)/shard_map/ppermute | solution.py:27
  4.8 8.7 %collective-permute-start.2 = (bf16[4,16,2,256]{3,2,1,0:T(2,128)(2,1)S(1)}, bf16[4,16,2,256]{3,2,1,0:T(2,128)(2,1)S(1)}, u32[]{:S(2)}, u32[]{:S(2)}) collective-permute-start(bf16[4,16,2,256]{3,2,1,0:T(2,128)(2,1)S(1)} %get-tuple-element.39), channel_id=1, source_target_pairs={{0,2},{1,3},{2,0},{3,1},{4,6},{5,7},{6,4},{7,5},{8,10},{9,11},{10,... | collective-permute-start | bytes 196616 | tf_op jit(solution)/shard_map/ppermute | solution.py:27
  7.4 7.9 %copy-start.4 = (bf16[256,1024]{1,0:T(8,128)(2,1)S(1)}, bf16[256,1024]{1,0:T(8,128)(2,1)}, u32[]{:S(2)}) copy-start(bf16[256,1024]{1,0:T(8,128)(2,1)} %w_out.1) | copy-start | bytes 1572868
  7.4 6.1 %collective-permute-start.3 = (bf16[4,16,2,256]{3,2,1,0:T(2,128)(2,1)S(1)}, bf16[4,16,2,256]{3,2,1,0:T(2,128)(2,1)S(1)}, u32[]{:S(2)}, u32[]{:S(2)}) collective-permute-start(bf16[4,16,2,256]{3,2,1,0:T(2,128)(2,1)S(1)} %get-tuple-element.40), channel_id=1, source_target_pairs={{0,3},{1,2},{2,1},{3,0},{4,7},{5,6},{6,5},{7,4},{8,11},{9,10},{10,... | collective-permute-start | bytes 196616 | tf_op jit(solution)/shard_map/ppermute | solution.py:27
  9.2 6.1 %collective-permute-start = (bf16[128,512]{1,0:T(8,128)(2,1)S(1)}, bf16[128,512]{1,0:T(8,128)(2,1)S(1)}, u32[]{:S(2)}, u32[]{:S(2)}) collective-permute-start(bf16[128,512]{1,0:T(8,128)(2,1)S(1)} %get-tuple-element.36.refs_0_), channel_id=1, source_target_pairs={{0,4},{4,0},{1,5},{5,1},{2,6},{6,2},{3,7},{7,3},{8,12},{12,8},{9,1... | collective-permute-start | bytes 393224 | tf_op jit(solution)/shard_map/ppermute | solution.py:32
  9.2 4.8 %collective-permute-start.4 = (bf16[4,16,2,256]{3,2,1,0:T(2,128)(2,1)S(1)}, bf16[4,16,2,256]{3,2,1,0:T(2,128)(2,1)S(1)}, u32[]{:S(2)}, u32[]{:S(2)}) collective-permute-start(bf16[4,16,2,256]{3,2,1,0:T(2,128)(2,1)S(1)} %get-tuple-element.41.refs_2_), channel_id=1, source_target_pairs={{0,4},{4,0},{1,5},{5,1},{2,6},{6,2},{3,7},{7,3},{8,12},{12,8},{9,1... | collective-permute-start | bytes 196616 | tf_op jit(solution)/shard_map/ppermute | solution.py:27
  13.5 1.3 %collective-permute-start.5 = (bf16[4,16,2,256]{3,2,1,0:T(2,128)(2,1)S(1)}, bf16[4,16,2,256]{3,2,1,0:T(2,128)(2,1)S(1)}, u32[]{:S(2)}, u32[]{:S(2)}) collective-permute-start(bf16[4,16,2,256]{3,2,1,0:T(2,128)(2,1)S(1)} %collective-permute-done.1.refs_3_), channel_id=1, source_target_pairs={{0,4},{4,0},{1,5},{5,1},{2,6},{6,2},{3,7},{7,3},{8,12},{12,8},{9,1... | collective-permute-start | bytes 196616 | tf_op jit(solution)/shard_map/ppermute | solution.py:27
  13.5 1.4 %collective-permute-start.6 = (bf16[4,16,2,256]{3,2,1,0:T(2,128)(2,1)S(1)}, bf16[4,16,2,256]{3,2,1,0:T(2,128)(2,1)S(1)}, u32[]{:S(2)}, u32[]{:S(2)}) collective-permute-start(bf16[4,16,2,256]{3,2,1,0:T(2,128)(2,1)S(1)} %collective-permute-done.2.refs_4_), channel_id=1, source_target_pairs={{0,4},{4,0},{1,5},{5,1},{2,6},{6,2},{3,7},{7,3},{8,12},{12,8},{9,1... | collective-permute-start | bytes 196616 | tf_op jit(solution)/shard_map/ppermute | solution.py:27
  14.0 1.3 %collective-permute-start.7 = (bf16[4,16,2,256]{3,2,1,0:T(2,128)(2,1)S(1)}, bf16[4,16,2,256]{3,2,1,0:T(2,128)(2,1)S(1)}, u32[]{:S(2)}, u32[]{:S(2)}) collective-permute-start(bf16[4,16,2,256]{3,2,1,0:T(2,128)(2,1)S(1)} %collective-permute-done.3.refs_5_), channel_id=1, source_target_pairs={{0,4},{4,0},{1,5},{5,1},{2,6},{6,2},{3,7},{7,3},{8,12},{12,8},{9,1... | collective-permute-start | bytes 196616 | tf_op jit(solution)/shard_map/ppermute | solution.py:27
  17.2 5.6 %collective-permute-start.8 = (bf16[32,1024]{1,0:T(8,128)(2,1)S(1)}, bf16[32,1024]{1,0:T(8,128)(2,1)S(1)}, u32[]{:S(2)}, u32[]{:S(2)}) collective-permute-start(bf16[32,1024]{1,0:T(8,128)(2,1)S(1)} %get-tuple-element.46), channel_id=1, source_target_pairs={{0,1},{1,0},{2,3},{3,2},{4,5},{5,4},{6,7},{7,6},{8,9},{9,8},{10,11... | collective-permute-start | bytes 196616 | tf_op jit(solution)/shard_map/ppermute | solution.py:27
  17.3 7.6 %collective-permute-start.9 = (bf16[32,1024]{1,0:T(8,128)(2,1)S(1)}, bf16[32,1024]{1,0:T(8,128)(2,1)S(1)}, u32[]{:S(2)}, u32[]{:S(2)}) collective-permute-start(bf16[32,1024]{1,0:T(8,128)(2,1)S(1)} %get-tuple-element.47), channel_id=1, source_target_pairs={{0,2},{1,3},{2,0},{3,1},{4,6},{5,7},{6,4},{7,5},{8,10},{9,11},{10,... | collective-permute-start | bytes 196616 | tf_op jit(solution)/shard_map/ppermute | solution.py:27
  19.6 6.1 %collective-permute-start.10 = (bf16[32,1024]{1,0:T(8,128)(2,1)S(1)}, bf16[32,1024]{1,0:T(8,128)(2,1)S(1)}, u32[]{:S(2)}, u32[]{:S(2)}) collective-permute-start(bf16[32,1024]{1,0:T(8,128)(2,1)S(1)} %get-tuple-element.48), channel_id=1, source_target_pairs={{0,3},{1,2},{2,1},{3,0},{4,7},{5,6},{6,5},{7,4},{8,11},{9,10},{10,... | collective-permute-start | bytes 196616 | tf_op jit(solution)/shard_map/ppermute | solution.py:27
  25.7 9.2 %copy-start.5 = (bf16[1024,256]{1,0:T(8,128)(2,1)S(1)}, bf16[1024,256]{1,0:T(8,128)(2,1)}, u32[]{:S(2)}) copy-start(bf16[1024,256]{1,0:T(8,128)(2,1)} %w_cross_query.1) | copy-start | bytes 1572868
  25.7 9.2 %copy-start.6 = (bf16[256,1024]{1,0:T(8,128)(2,1)S(1)}, bf16[256,1024]{1,0:T(8,128)(2,1)}, u32[]{:S(2)}) copy-start(bf16[256,1024]{1,0:T(8,128)(2,1)} %w_cross_out.1) | copy-start | bytes 1572868
  25.7 9.2 %copy-start.9 = (bf16[1,256,2,256]{3,2,1,0:T(2,128)(2,1)S(1)}, bf16[1,256,2,256]{3,2,1,0:T(2,128)(2,1)}, u32[]{:S(2)}) copy-start(bf16[1,256,2,256]{3,2,1,0:T(2,128)(2,1)} %cross_cache.1) | copy-start | bytes 786436
  25.9 6.7 %collective-permute-start.13 = (bf16[32,1024]{1,0:T(8,128)(2,1)S(1)}, bf16[32,1024]{1,0:T(8,128)(2,1)S(1)}, u32[]{:S(2)}, u32[]{:S(2)}) collective-permute-start(bf16[32,1024]{1,0:T(8,128)(2,1)S(1)} %get-tuple-element.50.refs_0_), channel_id=1, source_target_pairs={{0,3},{1,2},{2,1},{3,0},{4,7},{5,6},{6,5},{7,4},{8,11},{9,10},{10,... | collective-permute-start | bytes 196616 | tf_op jit(solution)/shard_map/ppermute | solution.py:27
  28.6 6.3 %collective-permute-start.12 = (bf16[32,1024]{1,0:T(8,128)(2,1)S(1)}, bf16[32,1024]{1,0:T(8,128)(2,1)S(1)}, u32[]{:S(2)}, u32[]{:S(2)}) collective-permute-start(bf16[32,1024]{1,0:T(8,128)(2,1)S(1)} %get-tuple-element.50.refs_0_), channel_id=1, source_target_pairs={{0,2},{1,3},{2,0},{3,1},{4,6},{5,7},{6,4},{7,5},{8,10},{9,11},{10,... | collective-permute-start | bytes 196616 | tf_op jit(solution)/shard_map/ppermute | solution.py:27
  29.0 5.8 %collective-permute-start.11 = (bf16[32,1024]{1,0:T(8,128)(2,1)S(1)}, bf16[32,1024]{1,0:T(8,128)(2,1)S(1)}, u32[]{:S(2)}, u32[]{:S(2)}) collective-permute-start(bf16[32,1024]{1,0:T(8,128)(2,1)S(1)} %get-tuple-element.50.refs_0_), channel_id=1, source_target_pairs={{0,1},{1,0},{2,3},{3,2},{4,5},{5,4},{6,7},{7,6},{8,9},{9,8},{10,11... | collective-permute-start | bytes 196616 | tf_op jit(solution)/shard_map/ppermute | solution.py:27
  35.8 4.5 %collective-permute-start.14 = (bf16[32,1024]{1,0:T(8,128)(2,1)S(1)}, bf16[32,1024]{1,0:T(8,128)(2,1)S(1)}, u32[]{:S(2)}, u32[]{:S(2)}) collective-permute-start(bf16[32,1024]{1,0:T(8,128)(2,1)S(1)} %get-tuple-element.52), channel_id=1, source_target_pairs={{0,1},{1,0},{2,3},{3,2},{4,5},{5,4},{6,7},{7,6},{8,9},{9,8},{10,11... | collective-permute-start | bytes 196616 | tf_op jit(solution)/shard_map/ppermute | solution.py:27
  35.9 7.3 %collective-permute-start.15 = (bf16[32,1024]{1,0:T(8,128)(2,1)S(1)}, bf16[32,1024]{1,0:T(8,128)(2,1)S(1)}, u32[]{:S(2)}, u32[]{:S(2)}) collective-permute-start(bf16[32,1024]{1,0:T(8,128)(2,1)S(1)} %get-tuple-element.53), channel_id=1, source_target_pairs={{0,2},{1,3},{2,0},{3,1},{4,6},{5,7},{6,4},{7,5},{8,10},{9,11},{10,... | collective-permute-start | bytes 196616 | tf_op jit(solution)/shard_map/ppermute | solution.py:27
  38.8 6.2 %collective-permute-start.16 = (bf16[32,1024]{1,0:T(8,128)(2,1)S(1)}, bf16[32,1024]{1,0:T(8,128)(2,1)S(1)}, u32[]{:S(2)}, u32[]{:S(2)}) collective-permute-start(bf16[32,1024]{1,0:T(8,128)(2,1)S(1)} %get-tuple-element.54), channel_id=1, source_target_pairs={{0,3},{1,2},{2,1},{3,0},{4,7},{5,6},{6,5},{7,4},{8,11},{9,10},{10,... | collective-permute-start | bytes 196616 | tf_op jit(solution)/shard_map/ppermute | solution.py:27
  44.9 7.8 %copy-start = (bf16[1024,2048]{1,0:T(8,128)(2,1)S(1)}, bf16[1024,2048]{1,0:T(8,128)(2,1)}, u32[]{:S(2)}) copy-start(bf16[1024,2048]{1,0:T(8,128)(2,1)} %w_up.1) | copy-start | bytes 12582916
  44.9 7.8 %copy-start.1 = (bf16[2048,1024]{1,0:T(8,128)(2,1)S(1)}, bf16[2048,1024]{1,0:T(8,128)(2,1)}, u32[]{:S(2)}) copy-start(bf16[2048,1024]{1,0:T(8,128)(2,1)} %w_down.1) | copy-start | bytes 12582916
  45.2 6.1 %collective-permute-start.19 = (bf16[32,1024]{1,0:T(8,128)(2,1)S(1)}, bf16[32,1024]{1,0:T(8,128)(2,1)S(1)}, u32[]{:S(2)}, u32[]{:S(2)}) collective-permute-start(bf16[32,1024]{1,0:T(8,128)(2,1)S(1)} %get-tuple-element.56.refs_0_), channel_id=1, source_target_pairs={{0,3},{1,2},{2,1},{3,0},{4,7},{5,6},{6,5},{7,4},{8,11},{9,10},{10,... | collective-permute-start | bytes 196616 | tf_op jit(solution)/shard_map/ppermute | solution.py:27
  46.7 6.0 %collective-permute-start.18 = (bf16[32,1024]{1,0:T(8,128)(2,1)S(1)}, bf16[32,1024]{1,0:T(8,128)(2,1)S(1)}, u32[]{:S(2)}, u32[]{:S(2)}) collective-permute-start(bf16[32,1024]{1,0:T(8,128)(2,1)S(1)} %get-tuple-element.56.refs_0_), channel_id=1, source_target_pairs={{0,2},{1,3},{2,0},{3,1},{4,6},{5,7},{6,4},{7,5},{8,10},{9,11},{10,... | collective-permute-start | bytes 196616 | tf_op jit(solution)/shard_map/ppermute | solution.py:27
  46.7 6.0 %collective-permute-start.17 = (bf16[32,1024]{1,0:T(8,128)(2,1)S(1)}, bf16[32,1024]{1,0:T(8,128)(2,1)S(1)}, u32[]{:S(2)}, u32[]{:S(2)}) collective-permute-start(bf16[32,1024]{1,0:T(8,128)(2,1)S(1)} %get-tuple-element.56.refs_0_), channel_id=1, source_target_pairs={{0,1},{1,0},{2,3},{3,2},{4,5},{5,4},{6,7},{7,6},{8,9},{9,8},{10,11... | collective-permute-start | bytes 196616 | tf_op jit(solution)/shard_map/ppermute | solution.py:27
  54.0 4.9 %collective-permute-start.20 = (bf16[32,1024]{1,0:T(8,128)(2,1)S(1)}, bf16[32,1024]{1,0:T(8,128)(2,1)S(1)}, u32[]{:S(2)}, u32[]{:S(2)}) collective-permute-start(bf16[32,1024]{1,0:T(8,128)(2,1)S(1)} %get-tuple-element.58), channel_id=1, source_target_pairs={{0,1},{1,0},{2,3},{3,2},{4,5},{5,4},{6,7},{7,6},{8,9},{9,8},{10,11... | collective-permute-start | bytes 196616 | tf_op jit(solution)/shard_map/ppermute | solution.py:27
  55.2 5.9 %collective-permute-start.21 = (bf16[32,1024]{1,0:T(8,128)(2,1)S(1)}, bf16[32,1024]{1,0:T(8,128)(2,1)S(1)}, u32[]{:S(2)}, u32[]{:S(2)}) collective-permute-start(bf16[32,1024]{1,0:T(8,128)(2,1)S(1)} %get-tuple-element.59), channel_id=1, source_target_pairs={{0,2},{1,3},{2,0},{3,1},{4,6},{5,7},{6,4},{7,5},{8,10},{9,11},{10,... | collective-permute-start | bytes 196616 | tf_op jit(solution)/shard_map/ppermute | solution.py:27
  56.1 6.2 %collective-permute-start.22 = (bf16[32,1024]{1,0:T(8,128)(2,1)S(1)}, bf16[32,1024]{1,0:T(8,128)(2,1)S(1)}, u32[]{:S(2)}, u32[]{:S(2)}) collective-permute-start(bf16[32,1024]{1,0:T(8,128)(2,1)S(1)} %get-tuple-element.60), channel_id=1, source_target_pairs={{0,3},{1,2},{2,1},{3,0},{4,7},{5,6},{6,5},{7,4},{8,11},{9,10},{10,... | collective-permute-start | bytes 196616 | tf_op jit(solution)/shard_map/ppermute | solution.py:27
  (3 other events, 13.7 us)

commit v4 on v3

--- a/solution.py
+++ b/solution.py
@@ -32,12 +32,29 @@
     return lax.ppermute(array, axis, [(i, (i + by) % count) for i in range(count)])
 
 
+def rounds(count):
+    return [0, count // 2] + [by for by in range(1, count) if by != count // 2]
+
+
+def arrivals(count):
+    own, *others = rounds(count)
+    return [own] + others[::-1]
+
+
+def rotate(array, by):
+    return array if by == 0 else from_behind(array, "head", by)
+
+
 def gather_heads(array):
-    return [array] + [swap(array, "head", by) for by in range(1, lax.axis_size("head"))]
+    return [rotate(array, by) for by in arrivals(lax.axis_size("head"))]
 
 
 def scatter_heads(pieces):
-    return [pieces[0]] + [swap(piece, "head", by) for by, piece in enumerate(pieces) if by]
+    return [rotate(piece, by) for piece, by in zip(pieces, rounds(len(pieces)))]
+
+
+def ahead(head_index, by, count):
+    return lax.rem(head_index + by + count, count)
 
 
 def kernel_call(body, outs, vmem_bytes, scratch, specs, out_specs, *args):
@@ -126,8 +143,8 @@
 
 def columns_body(place, pool, *outs):
     width = outs[0].shape[-1]
-    for by, out in enumerate(outs):
-        first = pl.multiple_of((place[1] ^ by) * width, width)
+    for by, out in zip(rounds(len(outs)), outs):
+        first = pl.multiple_of(ahead(place[1], by, len(outs)) * width, width)
         out[...] = pool[0, :, :, :, pl.ds(first, width)]
 
 
@@ -177,7 +194,9 @@
     for far in range(tok_count):
         places = slot % block_len
         for block in range(head_count * shard_blocks):
-            owner = (tok_index ^ far) * head_count + (head_index ^ (block // shard_blocks))
+            owner = (tok_index ^ far) * head_count + ahead(
+                head_index, -rounds(head_count)[block // shard_blocks], head_count
+            )
             logical = table[0, owner * shard_blocks + block % shard_blocks]
             places = places + jnp.where(slot // block_len == block, logical * block_len, 0)
         allowed = (places < SINK) | (places > prefix_len + own_offset - WINDOW)
@@ -201,8 +220,8 @@
     )
     share = rows // head_count
     term[...] = dot(attended, w_out[...]).astype(bf16)
-    for by, out in enumerate(outs):
-        start = pl.multiple_of((place[1] ^ by) * share, share)
+    for by, out in zip(rounds(head_count), outs):
+        start = pl.multiple_of(ahead(place[1], by, head_count) * share, share)
         out[...] = term[pl.ds(start, share), :]
 
 
@@ -214,8 +233,9 @@
     cross_out = attend(queries, keys, values, None)
     term = dot(cross_out, w_cross_out[...]).astype(bf16)
     share = rows_in[0].shape[0]
-    for by, out in enumerate(outs):
-        out[...] = term[by * share : (by + 1) * share]
+    for by, out in zip(rounds(head_count), outs):
+        row = arrivals(head_count).index(-by % head_count)
+        out[...] = term[row * share : (row + 1) * share]
 
 
 def after_body(before, *refs):
@@ -231,8 +251,9 @@
     hidden = jax.nn.relu(dot(normed, w_up[...])).astype(bf16)
     term = dot(hidden, w_down[...]).astype(bf16)
     share = rows_in[0].shape[0]
-    for by, out in enumerate(outs):
-        out[...] = term[by * share : (by + 1) * share]
+    for by, out in zip(rounds(head_count), outs):
+        row = arrivals(head_count).index(-by % head_count)
+        out[...] = term[row * share : (row + 1) * share]
 
 
 def on_device(

time: 63.1 us -> 61.7 us (0.978)
  waiting for transfers between devices: 25.1 us -> 18.8 us
  starting transfers between devices: 29.1 us -> 34 us
    ppermute x1 -> x19, starting transfers between devices: 0.07 us -> 32.9 us  [from_behind(): lax.ppermute(array, axis, [(i, (i + by) % count) for i in range(count)])]
    ppermute x22 -> x4, starting transfers between devices: 29 us -> 1.07 us  [swap(): return lax.ppermute(array, axis, [(i, i ^ by) for i in range(count)])]
    ppermute x22 -> x4, waiting for transfers between devices: 25.1 us -> 1.18 us  [swap(): return lax.ppermute(array, axis, [(i, i ^ by) for i in range(count)])]
    ppermute x1 -> x19, waiting for transfers between devices: 0.01 us -> 17.6 us  [from_behind(): lax.ppermute(array, axis, [(i, (i + by) % count) for i in range(count)])]
where the time goes in v4:
time: 61.7 us; the launch traced here: 61.6 us
  starting transfers between devices  34 us (55%)
  waiting for transfers between devices  18.8 us (30%)
  Pallas kernels  6.97 us (11%)
  local copies, waits for them, and re-layouts  0.99 us (2%)
  other arithmetic  0.75 us (1%)
    ppermute x19, starting transfers between devices, from_behind(): lax.ppermute(array, axis, [(i, (i + by) % count) for i in range(count)])  32.9 us
    ppermute x19, waiting for transfers between devices, from_behind(): lax.ppermute(array, axis, [(i, (i + by) % count) for i in range(count)])  17.6 us
    pallas_call x7, Pallas kernels, kernel_call(): pl.pallas_call(body, out_shape=outs, in_specs=list(specs) + [pl.BlockSpec...  6.97 us
  transfers between devices with their start and end apart: 23, of which 17 were waited for; matrix products, arithmetic and copies ran while one was open for 0% of the time, Pallas kernels for 3%

profile of v4, /device:TPU:0, one launch (start us, length us, event | category | flops | bytes accessed | tf_op | source)
XLA Modules:
  0.0 61.6 jit_solution(3481903513498245623)
XLA Ops:
  0.1 0.9 %copy-done.7 = bf16[1,4,16,2,1024]{4,3,2,1,0:T(2,128)(2,1)S(1)} copy-done((bf16[1,4,16,2,1024]{4,3,2,1,0:T(2,128)(2,1)S(1)}, bf16[1,4,16,2,1024]{4,3,2,1,0:T(2,128)(2,1)}, u32[]{:S(2)}) %copy-start.7) | copy-done | bytes 262168
  1.7 4.1 %collective-permute-start.1 = (bf16[4,16,2,256]{3,2,1,0:T(2,128)(2,1)S(1)}, bf16[4,16,2,256]{3,2,1,0:T(2,128)(2,1)S(1)}, u32[]{:S(2)}, u32[]{:S(2)}) collective-permute-start(bf16[4,16,2,256]{3,2,1,0:T(2,128)(2,1)S(1)} %get-tuple-element.38), channel_id=1, source_target_pairs={{0,2},{1,3},{2,0},{3,1},{4,6},{5,7},{6,4},{7,5},{8,10},{9,11},{10,... | collective-permute-start | bytes 196616 | tf_op jit(solution)/shard_map/ppermute | solution.py:32
  5.8 1.6 %collective-permute-start.2 = (bf16[4,16,2,256]{3,2,1,0:T(2,128)(2,1)S(1)}, bf16[4,16,2,256]{3,2,1,0:T(2,128)(2,1)S(1)}, u32[]{:S(2)}, u32[]{:S(2)}) collective-permute-start(bf16[4,16,2,256]{3,2,1,0:T(2,128)(2,1)S(1)} %get-tuple-element.39), channel_id=1, source_target_pairs={{0,1},{1,2},{2,3},{3,0},{4,5},{5,6},{6,7},{7,4},{8,9},{9,10},{10,1... | collective-permute-start | bytes 196616 | tf_op jit(solution)/shard_map/ppermute | solution.py:32
  7.4 2.2 %collective-permute-start.3 = (bf16[4,16,2,256]{3,2,1,0:T(2,128)(2,1)S(1)}, bf16[4,16,2,256]{3,2,1,0:T(2,128)(2,1)S(1)}, u32[]{:S(2)}, u32[]{:S(2)}) collective-permute-start(bf16[4,16,2,256]{3,2,1,0:T(2,128)(2,1)S(1)} %get-tuple-element.40), channel_id=1, source_target_pairs={{0,3},{1,0},{2,1},{3,2},{4,7},{5,4},{6,5},{7,6},{8,11},{9,8},{10,9... | collective-permute-start | bytes 196616 | tf_op jit(solution)/shard_map/ppermute | solution.py:32
  9.7 1.8 %shard_map.118 = (bf16[128,256]{1,0:T(8,128)(2,1)S(1)}, bf16[128,512]{1,0:T(8,128)(2,1)S(1)}, f32[128,768]{1,0:T(8,128)S(1)}, f32[32,1024]{1,0:T(8,128)S(1)}) custom-call(s32[2]{0:T(128)S(1)} %pad_add_fusion.place, s32[1,8]{1,0:T(1,128)S(1)} %copy-done.10, s32[1,32]{1,0:T(1,128)S(1)} %copy-done.11, bf16[1,128,1024]{2,1,0:T(8,128)(2,1)S(1)} %copy-done.8, ...), custom_call_target="tpu_custom_call" | custom-call | flops 4000000000 | bytes 1835176 | tf_op jit(solution)/shard_map/pallas_call | solution.py:61
  14.1 1.9 %shard_map.120 = (bf16[32,1024]{1,0:T(8,128)(2,1)S(1)}, bf16[32,1024]{1,0:T(8,128)(2,1)S(1)}, bf16[32,1024]{1,0:T(8,128)(2,1)S(1)}, bf16[32,1024]{1,0:T(8,128)(2,1)S(1)}) custom-call(s32[2]{0:T(128)S(1)} %pad_add_fusion.place, bf16[128,256]{1,0:T(8,128)(2,1)S(1)} %get-tuple-element.34.queries, f32[128,768]{1,0:T(8,128)S(1)} %get-tuple-element.35.bias, ...), custom_call_target="tpu_custom_call" | custom-call | flops 4000000000 | bytes 1769480 | tf_op jit(solution)/shard_map/pallas_call | solution.py:61
  16.1 1.8 %collective-permute-start.8 = (bf16[32,1024]{1,0:T(8,128)(2,1)S(1)}, bf16[32,1024]{1,0:T(8,128)(2,1)S(1)}, u32[]{:S(2)}, u32[]{:S(2)}) collective-permute-start(bf16[32,1024]{1,0:T(8,128)(2,1)S(1)} %get-tuple-element.46), channel_id=1, source_target_pairs={{0,2},{1,3},{2,0},{3,1},{4,6},{5,7},{6,4},{7,5},{8,10},{9,11},{10,... | collective-permute-start | bytes 196616 | tf_op jit(solution)/shard_map/ppermute | solution.py:32
  17.8 2.2 %collective-permute-start.9 = (bf16[32,1024]{1,0:T(8,128)(2,1)S(1)}, bf16[32,1024]{1,0:T(8,128)(2,1)S(1)}, u32[]{:S(2)}, u32[]{:S(2)}) collective-permute-start(bf16[32,1024]{1,0:T(8,128)(2,1)S(1)} %get-tuple-element.47), channel_id=1, source_target_pairs={{0,1},{1,2},{2,3},{3,0},{4,5},{5,6},{6,7},{7,4},{8,9},{9,10},{10,1... | collective-permute-start | bytes 196616 | tf_op jit(solution)/shard_map/ppermute | solution.py:32
  20.0 1.6 %collective-permute-start.10 = (bf16[32,1024]{1,0:T(8,128)(2,1)S(1)}, bf16[32,1024]{1,0:T(8,128)(2,1)S(1)}, u32[]{:S(2)}, u32[]{:S(2)}) collective-permute-start(bf16[32,1024]{1,0:T(8,128)(2,1)S(1)} %get-tuple-element.48), channel_id=1, source_target_pairs={{0,3},{1,0},{2,1},{3,2},{4,7},{5,4},{6,5},{7,6},{8,11},{9,8},{10,9... | collective-permute-start | bytes 196616 | tf_op jit(solution)/shard_map/ppermute | solution.py:32
  21.6 3.0 %collective-permute-done.8.refs_1_ = bf16[32,1024]{1,0:T(8,128)(2,1)S(1)} collective-permute-done((bf16[32,1024]{1,0:T(8,128)(2,1)S(1)}, bf16[32,1024]{1,0:T(8,128)(2,1)S(1)}, u32[]{:S(2)}, u32[]{:S(2)}) %collective-permute-start.8) | collective-permute-done | bytes 65568 | tf_op jit(solution)/shard_map/ppermute | solution.py:32
  24.6 0.9 %collective-permute-done.10.refs_3_ = bf16[32,1024]{1,0:T(8,128)(2,1)S(1)} collective-permute-done((bf16[32,1024]{1,0:T(8,128)(2,1)S(1)}, bf16[32,1024]{1,0:T(8,128)(2,1)S(1)}, u32[]{:S(2)}, u32[]{:S(2)}) %collective-permute-start.10) | collective-permute-done | bytes 65568 | tf_op jit(solution)/shard_map/ppermute | solution.py:32
  25.7 1.8 %collective-permute-start.13 = (bf16[32,1024]{1,0:T(8,128)(2,1)S(1)}, bf16[32,1024]{1,0:T(8,128)(2,1)S(1)}, u32[]{:S(2)}, u32[]{:S(2)}) collective-permute-start(bf16[32,1024]{1,0:T(8,128)(2,1)S(1)} %get-tuple-element.50.refs_0_), channel_id=1, source_target_pairs={{0,2},{1,3},{2,0},{3,1},{4,6},{5,7},{6,4},{7,5},{8,10},{9,11},{10,... | collective-permute-start | bytes 196616 | tf_op jit(solution)/shard_map/ppermute | solution.py:32
  27.4 1.2 %collective-permute-start.12 = (bf16[32,1024]{1,0:T(8,128)(2,1)S(1)}, bf16[32,1024]{1,0:T(8,128)(2,1)S(1)}, u32[]{:S(2)}, u32[]{:S(2)}) collective-permute-start(bf16[32,1024]{1,0:T(8,128)(2,1)S(1)} %get-tuple-element.50.refs_0_), channel_id=1, source_target_pairs={{0,1},{1,2},{2,3},{3,0},{4,5},{5,6},{6,7},{7,4},{8,9},{9,10},{10,1... | collective-permute-start | bytes 196616 | tf_op jit(solution)/shard_map/ppermute | solution.py:32
  28.6 2.6 %collective-permute-start.11 = (bf16[32,1024]{1,0:T(8,128)(2,1)S(1)}, bf16[32,1024]{1,0:T(8,128)(2,1)S(1)}, u32[]{:S(2)}, u32[]{:S(2)}) collective-permute-start(bf16[32,1024]{1,0:T(8,128)(2,1)S(1)} %get-tuple-element.50.refs_0_), channel_id=1, source_target_pairs={{0,3},{1,0},{2,1},{3,2},{4,7},{5,4},{6,5},{7,6},{8,11},{9,8},{10,9... | collective-permute-start | bytes 196616 | tf_op jit(solution)/shard_map/ppermute | solution.py:32
  31.3 1.8 %collective-permute-done.13.refs_3_ = bf16[32,1024]{1,0:T(8,128)(2,1)S(1)} collective-permute-done((bf16[32,1024]{1,0:T(8,128)(2,1)S(1)}, bf16[32,1024]{1,0:T(8,128)(2,1)S(1)}, u32[]{:S(2)}, u32[]{:S(2)}) %collective-permute-start.13) | collective-permute-done | bytes 65568 | tf_op jit(solution)/shard_map/ppermute | solution.py:32
  34.0 0.9 %shard_map.122 = (bf16[32,1024]{1,0:T(8,128)(2,1)S(1)}, bf16[32,1024]{1,0:T(8,128)(2,1)S(1)}, bf16[32,1024]{1,0:T(8,128)(2,1)S(1)}, bf16[32,1024]{1,0:T(8,128)(2,1)S(1)}) custom-call(bf16[1024,256]{1,0:T(8,128)(2,1)S(1)} %copy-done.5, bf16[1,256,2,256]{3,2,1,0:T(2,128)(2,1)S(1)} %copy-done.9, bf16[256,1024]{1,0:T(8,128)(2,1)S(1)} %copy-done.6, ...), custom_call_target="tpu_custom_call" | custom-call | flops 4000000000 | bytes 1572864 | tf_op jit(solution)/shard_map/pallas_call | solution.py:61
  35.0 1.1 %collective-permute-start.14 = (bf16[32,1024]{1,0:T(8,128)(2,1)S(1)}, bf16[32,1024]{1,0:T(8,128)(2,1)S(1)}, u32[]{:S(2)}, u32[]{:S(2)}) collective-permute-start(bf16[32,1024]{1,0:T(8,128)(2,1)S(1)} %get-tuple-element.52), channel_id=1, source_target_pairs={{0,2},{1,3},{2,0},{3,1},{4,6},{5,7},{6,4},{7,5},{8,10},{9,11},{10,... | collective-permute-start | bytes 196616 | tf_op jit(solution)/shard_map/ppermute | solution.py:32
  36.0 2.9 %collective-permute-start.15 = (bf16[32,1024]{1,0:T(8,128)(2,1)S(1)}, bf16[32,1024]{1,0:T(8,128)(2,1)S(1)}, u32[]{:S(2)}, u32[]{:S(2)}) collective-permute-start(bf16[32,1024]{1,0:T(8,128)(2,1)S(1)} %get-tuple-element.53), channel_id=1, source_target_pairs={{0,1},{1,2},{2,3},{3,0},{4,5},{5,6},{6,7},{7,4},{8,9},{9,10},{10,1... | collective-permute-start | bytes 196616 | tf_op jit(solution)/shard_map/ppermute | solution.py:32
  38.9 1.0 %collective-permute-start.16 = (bf16[32,1024]{1,0:T(8,128)(2,1)S(1)}, bf16[32,1024]{1,0:T(8,128)(2,1)S(1)}, u32[]{:S(2)}, u32[]{:S(2)}) collective-permute-start(bf16[32,1024]{1,0:T(8,128)(2,1)S(1)} %get-tuple-element.54), channel_id=1, source_target_pairs={{0,3},{1,0},{2,1},{3,2},{4,7},{5,4},{6,5},{7,6},{8,11},{9,8},{10,9... | collective-permute-start | bytes 196616 | tf_op jit(solution)/shard_map/ppermute | solution.py:32
  39.9 1.4 %collective-permute-done.14.refs_1_ = bf16[32,1024]{1,0:T(8,128)(2,1)S(1)} collective-permute-done((bf16[32,1024]{1,0:T(8,128)(2,1)S(1)}, bf16[32,1024]{1,0:T(8,128)(2,1)S(1)}, u32[]{:S(2)}, u32[]{:S(2)}) %collective-permute-start.14) | collective-permute-done | bytes 65568 | tf_op jit(solution)/shard_map/ppermute | solution.py:32
  41.3 0.8 %collective-permute-done.15.refs_2_ = bf16[32,1024]{1,0:T(8,128)(2,1)S(1)} collective-permute-done((bf16[32,1024]{1,0:T(8,128)(2,1)S(1)}, bf16[32,1024]{1,0:T(8,128)(2,1)S(1)}, u32[]{:S(2)}, u32[]{:S(2)}) %collective-permute-start.15) | collective-permute-done | bytes 65568 | tf_op jit(solution)/shard_map/ppermute | solution.py:32
  42.1 1.1 %collective-permute-done.16.refs_3_ = bf16[32,1024]{1,0:T(8,128)(2,1)S(1)} collective-permute-done((bf16[32,1024]{1,0:T(8,128)(2,1)S(1)}, bf16[32,1024]{1,0:T(8,128)(2,1)S(1)}, u32[]{:S(2)}, u32[]{:S(2)}) %collective-permute-start.16) | collective-permute-done | bytes 65568 | tf_op jit(solution)/shard_map/ppermute | solution.py:32
  43.4 0.9 %collective-permute-start.19 = (bf16[32,1024]{1,0:T(8,128)(2,1)S(1)}, bf16[32,1024]{1,0:T(8,128)(2,1)S(1)}, u32[]{:S(2)}, u32[]{:S(2)}) collective-permute-start(bf16[32,1024]{1,0:T(8,128)(2,1)S(1)} %get-tuple-element.56.refs_0_), channel_id=1, source_target_pairs={{0,2},{1,3},{2,0},{3,1},{4,6},{5,7},{6,4},{7,5},{8,10},{9,11},{10,... | collective-permute-start | bytes 196616 | tf_op jit(solution)/shard_map/ppermute | solution.py:32
  44.3 2.8 %collective-permute-start.18 = (bf16[32,1024]{1,0:T(8,128)(2,1)S(1)}, bf16[32,1024]{1,0:T(8,128)(2,1)S(1)}, u32[]{:S(2)}, u32[]{:S(2)}) collective-permute-start(bf16[32,1024]{1,0:T(8,128)(2,1)S(1)} %get-tuple-element.56.refs_0_), channel_id=1, source_target_pairs={{0,1},{1,2},{2,3},{3,0},{4,5},{5,6},{6,7},{7,4},{8,9},{9,10},{10,1... | collective-permute-start | bytes 196616 | tf_op jit(solution)/shard_map/ppermute | solution.py:32
  47.1 1.0 %collective-permute-start.17 = (bf16[32,1024]{1,0:T(8,128)(2,1)S(1)}, bf16[32,1024]{1,0:T(8,128)(2,1)S(1)}, u32[]{:S(2)}, u32[]{:S(2)}) collective-permute-start(bf16[32,1024]{1,0:T(8,128)(2,1)S(1)} %get-tuple-element.56.refs_0_), channel_id=1, source_target_pairs={{0,3},{1,0},{2,1},{3,2},{4,7},{5,4},{6,5},{7,6},{8,11},{9,8},{10,9... | collective-permute-start | bytes 196616 | tf_op jit(solution)/shard_map/ppermute | solution.py:32
  48.1 1.2 %collective-permute-done.19.refs_3_ = bf16[32,1024]{1,0:T(8,128)(2,1)S(1)} collective-permute-done((bf16[32,1024]{1,0:T(8,128)(2,1)S(1)}, bf16[32,1024]{1,0:T(8,128)(2,1)S(1)}, u32[]{:S(2)}, u32[]{:S(2)}) %collective-permute-start.19) | collective-permute-done | bytes 65568 | tf_op jit(solution)/shard_map/ppermute | solution.py:32
  49.3 1.0 %collective-permute-done.18.refs_2_ = bf16[32,1024]{1,0:T(8,128)(2,1)S(1)} collective-permute-done((bf16[32,1024]{1,0:T(8,128)(2,1)S(1)}, bf16[32,1024]{1,0:T(8,128)(2,1)S(1)}, u32[]{:S(2)}, u32[]{:S(2)}) %collective-permute-start.18) | collective-permute-done | bytes 65568 | tf_op jit(solution)/shard_map/ppermute | solution.py:32
  50.4 1.0 %collective-permute-done.17.refs_1_ = bf16[32,1024]{1,0:T(8,128)(2,1)S(1)} collective-permute-done((bf16[32,1024]{1,0:T(8,128)(2,1)S(1)}, bf16[32,1024]{1,0:T(8,128)(2,1)S(1)}, u32[]{:S(2)}, u32[]{:S(2)}) %collective-permute-start.17) | collective-permute-done | bytes 65568 | tf_op jit(solution)/shard_map/ppermute | solution.py:32
  51.4 1.3 %shard_map.124 = (bf16[32,1024]{1,0:T(8,128)(2,1)S(1)}, bf16[32,1024]{1,0:T(8,128)(2,1)S(1)}, bf16[32,1024]{1,0:T(8,128)(2,1)S(1)}, bf16[32,1024]{1,0:T(8,128)(2,1)S(1)}) custom-call(bf16[1024,2048]{1,0:T(8,128)(2,1)S(1)} %copy-done, bf16[2048,1024]{1,0:T(8,128)(2,1)S(1)} %copy-done.1, bf16[32,1024]{1,0:T(8,128)(2,1)S(1)} %get-tuple-element.56.refs_0_, ...), custom_call_target="tpu_custom_call" | custom-call | flops 4000000000 | bytes 8650752 | tf_op jit(solution)/shard_map/pallas_call | solution.py:61
  53.0 3.7 %collective-permute-start.21 = (bf16[32,1024]{1,0:T(8,128)(2,1)S(1)}, bf16[32,1024]{1,0:T(8,128)(2,1)S(1)}, u32[]{:S(2)}, u32[]{:S(2)}) collective-permute-start(bf16[32,1024]{1,0:T(8,128)(2,1)S(1)} %get-tuple-element.59), channel_id=1, source_target_pairs={{0,1},{1,2},{2,3},{3,0},{4,5},{5,6},{6,7},{7,4},{8,9},{9,10},{10,1... | collective-permute-start | bytes 196616 | tf_op jit(solution)/shard_map/ppermute | solution.py:32
  56.8 2.5 %collective-permute-done.20 = bf16[32,1024]{1,0:T(8,128)(2,1)S(1)} collective-permute-done((bf16[32,1024]{1,0:T(8,128)(2,1)S(1)}, bf16[32,1024]{1,0:T(8,128)(2,1)S(1)}, u32[]{:S(2)}, u32[]{:S(2)}) %collective-permute-start.20) | collective-permute-done | bytes 65568 | tf_op jit(solution)/shard_map/ppermute | solution.py:32
  59.3 1.7 %collective-permute-done.22 = bf16[32,1024]{1,0:T(8,128)(2,1)S(1)} collective-permute-done((bf16[32,1024]{1,0:T(8,128)(2,1)S(1)}, bf16[32,1024]{1,0:T(8,128)(2,1)S(1)}, u32[]{:S(2)}, u32[]{:S(2)}) %collective-permute-start.22) | collective-permute-done | bytes 65568 | tf_op jit(solution)/shard_map/ppermute | solution.py:32
  (47 shorter events, 6.0 us)
Async XLA Ops:
  1.0 8.6 %copy-start.2 = (bf16[1024,2,256]{2,1,0:T(2,128)(2,1)S(1)}, bf16[1024,2,256]{2,1,0:T(2,128)(2,1)}, u32[]{:S(2)}) copy-start(bf16[1024,2,256]{2,1,0:T(2,128)(2,1)} %w_keyvalue.1) | copy-start | bytes 3145732
  1.0 8.6 %copy-start.3 = (bf16[1024,256]{1,0:T(8,128)(2,1)S(1)}, bf16[1024,256]{1,0:T(8,128)(2,1)}, u32[]{:S(2)}) copy-start(bf16[1024,256]{1,0:T(8,128)(2,1)} %w_query.1) | copy-start | bytes 1572868
  1.0 8.6 %copy-start.8 = (bf16[1,128,1024]{2,1,0:T(8,128)(2,1)S(1)}, bf16[1,128,1024]{2,1,0:T(8,128)(2,1)}, u32[]{:S(2)}) copy-start(bf16[1,128,1024]{2,1,0:T(8,128)(2,1)} %tokens.1) | copy-start | bytes 786436
  1.0 8.6 %copy-start.10 = (s32[1,8]{1,0:T(1,128)S(1)}, s32[1,8]{1,0:T(1,128)}, u32[]{:S(2)}) copy-start(s32[1,8]{1,0:T(1,128)} %lengths_in.1) | copy-start | bytes 100
  1.0 8.6 %copy-start.11 = (s32[1,32]{1,0:T(1,128)S(1)}, s32[1,32]{1,0:T(1,128)}, u32[]{:S(2)}) copy-start(s32[1,32]{1,0:T(1,128)} %table_in.1) | copy-start | bytes 388
  1.7 10.7 %collective-permute-start.1 = (bf16[4,16,2,256]{3,2,1,0:T(2,128)(2,1)S(1)}, bf16[4,16,2,256]{3,2,1,0:T(2,128)(2,1)S(1)}, u32[]{:S(2)}, u32[]{:S(2)}) collective-permute-start(bf16[4,16,2,256]{3,2,1,0:T(2,128)(2,1)S(1)} %get-tuple-element.38), channel_id=1, source_target_pairs={{0,2},{1,3},{2,0},{3,1},{4,6},{5,7},{6,4},{7,5},{8,10},{9,11},{10,... | collective-permute-start | bytes 196616 | tf_op jit(solution)/shard_map/ppermute | solution.py:32
  5.8 6.5 %collective-permute-start.2 = (bf16[4,16,2,256]{3,2,1,0:T(2,128)(2,1)S(1)}, bf16[4,16,2,256]{3,2,1,0:T(2,128)(2,1)S(1)}, u32[]{:S(2)}, u32[]{:S(2)}) collective-permute-start(bf16[4,16,2,256]{3,2,1,0:T(2,128)(2,1)S(1)} %get-tuple-element.39), channel_id=1, source_target_pairs={{0,1},{1,2},{2,3},{3,0},{4,5},{5,6},{6,7},{7,4},{8,9},{9,10},{10,1... | collective-permute-start | bytes 196616 | tf_op jit(solution)/shard_map/ppermute | solution.py:32
  7.4 5.0 %collective-permute-start.3 = (bf16[4,16,2,256]{3,2,1,0:T(2,128)(2,1)S(1)}, bf16[4,16,2,256]{3,2,1,0:T(2,128)(2,1)S(1)}, u32[]{:S(2)}, u32[]{:S(2)}) collective-permute-start(bf16[4,16,2,256]{3,2,1,0:T(2,128)(2,1)S(1)} %get-tuple-element.40), channel_id=1, source_target_pairs={{0,3},{1,0},{2,1},{3,2},{4,7},{5,4},{6,5},{7,6},{8,11},{9,8},{10,9... | collective-permute-start | bytes 196616 | tf_op jit(solution)/shard_map/ppermute | solution.py:32
  11.4 2.7 %collective-permute-start = (bf16[128,512]{1,0:T(8,128)(2,1)S(1)}, bf16[128,512]{1,0:T(8,128)(2,1)S(1)}, u32[]{:S(2)}, u32[]{:S(2)}) collective-permute-start(bf16[128,512]{1,0:T(8,128)(2,1)S(1)} %get-tuple-element.36.refs_0_), channel_id=1, source_target_pairs={{0,4},{4,0},{1,5},{5,1},{2,6},{6,2},{3,7},{7,3},{8,12},{12,8},{9,1... | collective-permute-start | bytes 393224 | tf_op jit(solution)/shard_map/ppermute | solution.py:32
  11.5 1.4 %collective-permute-start.4 = (bf16[4,16,2,256]{3,2,1,0:T(2,128)(2,1)S(1)}, bf16[4,16,2,256]{3,2,1,0:T(2,128)(2,1)S(1)}, u32[]{:S(2)}, u32[]{:S(2)}) collective-permute-start(bf16[4,16,2,256]{3,2,1,0:T(2,128)(2,1)S(1)} %get-tuple-element.41.refs_2_), channel_id=1, source_target_pairs={{0,4},{4,0},{1,5},{5,1},{2,6},{6,2},{3,7},{7,3},{8,12},{12,8},{9,1... | collective-permute-start | bytes 196616 | tf_op jit(solution)/shard_map/ppermute | solution.py:27
  12.4 1.3 %collective-permute-start.5 = (bf16[4,16,2,256]{3,2,1,0:T(2,128)(2,1)S(1)}, bf16[4,16,2,256]{3,2,1,0:T(2,128)(2,1)S(1)}, u32[]{:S(2)}, u32[]{:S(2)}) collective-permute-start(bf16[4,16,2,256]{3,2,1,0:T(2,128)(2,1)S(1)} %collective-permute-done.1.refs_3_), channel_id=1, source_target_pairs={{0,4},{4,0},{1,5},{5,1},{2,6},{6,2},{3,7},{7,3},{8,12},{12,8},{9,1... | collective-permute-start | bytes 196616 | tf_op jit(solution)/shard_map/ppermute | solution.py:27
  12.4 1.4 %collective-permute-start.6 = (bf16[4,16,2,256]{3,2,1,0:T(2,128)(2,1)S(1)}, bf16[4,16,2,256]{3,2,1,0:T(2,128)(2,1)S(1)}, u32[]{:S(2)}, u32[]{:S(2)}) collective-permute-start(bf16[4,16,2,256]{3,2,1,0:T(2,128)(2,1)S(1)} %collective-permute-done.2.refs_4_), channel_id=1, source_target_pairs={{0,4},{4,0},{1,5},{5,1},{2,6},{6,2},{3,7},{7,3},{8,12},{12,8},{9,1... | collective-permute-start | bytes 196616 | tf_op jit(solution)/shard_map/ppermute | solution.py:27
  12.9 1.3 %collective-permute-start.7 = (bf16[4,16,2,256]{3,2,1,0:T(2,128)(2,1)S(1)}, bf16[4,16,2,256]{3,2,1,0:T(2,128)(2,1)S(1)}, u32[]{:S(2)}, u32[]{:S(2)}) collective-permute-start(bf16[4,16,2,256]{3,2,1,0:T(2,128)(2,1)S(1)} %collective-permute-done.3.refs_5_), channel_id=1, source_target_pairs={{0,4},{4,0},{1,5},{5,1},{2,6},{6,2},{3,7},{7,3},{8,12},{12,8},{9,1... | collective-permute-start | bytes 196616 | tf_op jit(solution)/shard_map/ppermute | solution.py:27
  16.1 8.5 %collective-permute-start.8 = (bf16[32,1024]{1,0:T(8,128)(2,1)S(1)}, bf16[32,1024]{1,0:T(8,128)(2,1)S(1)}, u32[]{:S(2)}, u32[]{:S(2)}) collective-permute-start(bf16[32,1024]{1,0:T(8,128)(2,1)S(1)} %get-tuple-element.46), channel_id=1, source_target_pairs={{0,2},{1,3},{2,0},{3,1},{4,6},{5,7},{6,4},{7,5},{8,10},{9,11},{10,... | collective-permute-start | bytes 196616 | tf_op jit(solution)/shard_map/ppermute | solution.py:32
  17.8 6.8 %collective-permute-start.9 = (bf16[32,1024]{1,0:T(8,128)(2,1)S(1)}, bf16[32,1024]{1,0:T(8,128)(2,1)S(1)}, u32[]{:S(2)}, u32[]{:S(2)}) collective-permute-start(bf16[32,1024]{1,0:T(8,128)(2,1)S(1)} %get-tuple-element.47), channel_id=1, source_target_pairs={{0,1},{1,2},{2,3},{3,0},{4,5},{5,6},{6,7},{7,4},{8,9},{9,10},{10,1... | collective-permute-start | bytes 196616 | tf_op jit(solution)/shard_map/ppermute | solution.py:32
  20.0 5.4 %collective-permute-start.10 = (bf16[32,1024]{1,0:T(8,128)(2,1)S(1)}, bf16[32,1024]{1,0:T(8,128)(2,1)S(1)}, u32[]{:S(2)}, u32[]{:S(2)}) collective-permute-start(bf16[32,1024]{1,0:T(8,128)(2,1)S(1)} %get-tuple-element.48), channel_id=1, source_target_pairs={{0,3},{1,0},{2,1},{3,2},{4,7},{5,4},{6,5},{7,6},{8,11},{9,8},{10,9... | collective-permute-start | bytes 196616 | tf_op jit(solution)/shard_map/ppermute | solution.py:32
  25.5 8.6 %copy-start.5 = (bf16[1024,256]{1,0:T(8,128)(2,1)S(1)}, bf16[1024,256]{1,0:T(8,128)(2,1)}, u32[]{:S(2)}) copy-start(bf16[1024,256]{1,0:T(8,128)(2,1)} %w_cross_query.1) | copy-start | bytes 1572868
  25.5 8.6 %copy-start.6 = (bf16[256,1024]{1,0:T(8,128)(2,1)S(1)}, bf16[256,1024]{1,0:T(8,128)(2,1)}, u32[]{:S(2)}) copy-start(bf16[256,1024]{1,0:T(8,128)(2,1)} %w_cross_out.1) | copy-start | bytes 1572868
  25.5 8.6 %copy-start.9 = (bf16[1,256,2,256]{3,2,1,0:T(2,128)(2,1)S(1)}, bf16[1,256,2,256]{3,2,1,0:T(2,128)(2,1)}, u32[]{:S(2)}) copy-start(bf16[1,256,2,256]{3,2,1,0:T(2,128)(2,1)} %cross_cache.1) | copy-start | bytes 786436
  25.7 7.3 %collective-permute-start.13 = (bf16[32,1024]{1,0:T(8,128)(2,1)S(1)}, bf16[32,1024]{1,0:T(8,128)(2,1)S(1)}, u32[]{:S(2)}, u32[]{:S(2)}) collective-permute-start(bf16[32,1024]{1,0:T(8,128)(2,1)S(1)} %get-tuple-element.50.refs_0_), channel_id=1, source_target_pairs={{0,2},{1,3},{2,0},{3,1},{4,6},{5,7},{6,4},{7,5},{8,10},{9,11},{10,... | collective-permute-start | bytes 196616 | tf_op jit(solution)/shard_map/ppermute | solution.py:32
  27.4 6.3 %collective-permute-start.12 = (bf16[32,1024]{1,0:T(8,128)(2,1)S(1)}, bf16[32,1024]{1,0:T(8,128)(2,1)S(1)}, u32[]{:S(2)}, u32[]{:S(2)}) collective-permute-start(bf16[32,1024]{1,0:T(8,128)(2,1)S(1)} %get-tuple-element.50.refs_0_), channel_id=1, source_target_pairs={{0,1},{1,2},{2,3},{3,0},{4,5},{5,6},{6,7},{7,4},{8,9},{9,10},{10,1... | collective-permute-start | bytes 196616 | tf_op jit(solution)/shard_map/ppermute | solution.py:32
  28.6 5.4 %collective-permute-start.11 = (bf16[32,1024]{1,0:T(8,128)(2,1)S(1)}, bf16[32,1024]{1,0:T(8,128)(2,1)S(1)}, u32[]{:S(2)}, u32[]{:S(2)}) collective-permute-start(bf16[32,1024]{1,0:T(8,128)(2,1)S(1)} %get-tuple-element.50.refs_0_), channel_id=1, source_target_pairs={{0,3},{1,0},{2,1},{3,2},{4,7},{5,4},{6,5},{7,6},{8,11},{9,8},{10,9... | collective-permute-start | bytes 196616 | tf_op jit(solution)/shard_map/ppermute | solution.py:32
  35.0 6.3 %collective-permute-start.14 = (bf16[32,1024]{1,0:T(8,128)(2,1)S(1)}, bf16[32,1024]{1,0:T(8,128)(2,1)S(1)}, u32[]{:S(2)}, u32[]{:S(2)}) collective-permute-start(bf16[32,1024]{1,0:T(8,128)(2,1)S(1)} %get-tuple-element.52), channel_id=1, source_target_pairs={{0,2},{1,3},{2,0},{3,1},{4,6},{5,7},{6,4},{7,5},{8,10},{9,11},{10,... | collective-permute-start | bytes 196616 | tf_op jit(solution)/shard_map/ppermute | solution.py:32
  36.0 6.1 %collective-permute-start.15 = (bf16[32,1024]{1,0:T(8,128)(2,1)S(1)}, bf16[32,1024]{1,0:T(8,128)(2,1)S(1)}, u32[]{:S(2)}, u32[]{:S(2)}) collective-permute-start(bf16[32,1024]{1,0:T(8,128)(2,1)S(1)} %get-tuple-element.53), channel_id=1, source_target_pairs={{0,1},{1,2},{2,3},{3,0},{4,5},{5,6},{6,7},{7,4},{8,9},{9,10},{10,1... | collective-permute-start | bytes 196616 | tf_op jit(solution)/shard_map/ppermute | solution.py:32
  38.9 4.3 %collective-permute-start.16 = (bf16[32,1024]{1,0:T(8,128)(2,1)S(1)}, bf16[32,1024]{1,0:T(8,128)(2,1)S(1)}, u32[]{:S(2)}, u32[]{:S(2)}) collective-permute-start(bf16[32,1024]{1,0:T(8,128)(2,1)S(1)} %get-tuple-element.54), channel_id=1, source_target_pairs={{0,3},{1,0},{2,1},{3,2},{4,7},{5,4},{6,5},{7,6},{8,11},{9,8},{10,9... | collective-permute-start | bytes 196616 | tf_op jit(solution)/shard_map/ppermute | solution.py:32
  43.2 8.2 %copy-start.1 = (bf16[2048,1024]{1,0:T(8,128)(2,1)S(1)}, bf16[2048,1024]{1,0:T(8,128)(2,1)}, u32[]{:S(2)}) copy-start(bf16[2048,1024]{1,0:T(8,128)(2,1)} %w_down.1) | copy-start | bytes 12582916
  43.4 5.9 %collective-permute-start.19 = (bf16[32,1024]{1,0:T(8,128)(2,1)S(1)}, bf16[32,1024]{1,0:T(8,128)(2,1)S(1)}, u32[]{:S(2)}, u32[]{:S(2)}) collective-permute-start(bf16[32,1024]{1,0:T(8,128)(2,1)S(1)} %get-tuple-element.56.refs_0_), channel_id=1, source_target_pairs={{0,2},{1,3},{2,0},{3,1},{4,6},{5,7},{6,4},{7,5},{8,10},{9,11},{10,... | collective-permute-start | bytes 196616 | tf_op jit(solution)/shard_map/ppermute | solution.py:32
  44.3 6.1 %collective-permute-start.18 = (bf16[32,1024]{1,0:T(8,128)(2,1)S(1)}, bf16[32,1024]{1,0:T(8,128)(2,1)S(1)}, u32[]{:S(2)}, u32[]{:S(2)}) collective-permute-start(bf16[32,1024]{1,0:T(8,128)(2,1)S(1)} %get-tuple-element.56.refs_0_), channel_id=1, source_target_pairs={{0,1},{1,2},{2,3},{3,0},{4,5},{5,6},{6,7},{7,4},{8,9},{9,10},{10,1... | collective-permute-start | bytes 196616 | tf_op jit(solution)/shard_map/ppermute | solution.py:32
  47.1 4.3 %collective-permute-start.17 = (bf16[32,1024]{1,0:T(8,128)(2,1)S(1)}, bf16[32,1024]{1,0:T(8,128)(2,1)S(1)}, u32[]{:S(2)}, u32[]{:S(2)}) collective-permute-start(bf16[32,1024]{1,0:T(8,128)(2,1)S(1)} %get-tuple-element.56.refs_0_), channel_id=1, source_target_pairs={{0,3},{1,0},{2,1},{3,2},{4,7},{5,4},{6,5},{7,6},{8,11},{9,8},{10,9... | collective-permute-start | bytes 196616 | tf_op jit(solution)/shard_map/ppermute | solution.py:32
  52.6 6.6 %collective-permute-start.20 = (bf16[32,1024]{1,0:T(8,128)(2,1)S(1)}, bf16[32,1024]{1,0:T(8,128)(2,1)S(1)}, u32[]{:S(2)}, u32[]{:S(2)}) collective-permute-start(bf16[32,1024]{1,0:T(8,128)(2,1)S(1)} %get-tuple-element.58), channel_id=1, source_target_pairs={{0,2},{1,3},{2,0},{3,1},{4,6},{5,7},{6,4},{7,5},{8,10},{9,11},{10,... | collective-permute-start | bytes 196616 | tf_op jit(solution)/shard_map/ppermute | solution.py:32
  53.0 6.3 %collective-permute-start.21 = (bf16[32,1024]{1,0:T(8,128)(2,1)S(1)}, bf16[32,1024]{1,0:T(8,128)(2,1)S(1)}, u32[]{:S(2)}, u32[]{:S(2)}) collective-permute-start(bf16[32,1024]{1,0:T(8,128)(2,1)S(1)} %get-tuple-element.59), channel_id=1, source_target_pairs={{0,1},{1,2},{2,3},{3,0},{4,5},{5,6},{6,7},{7,4},{8,9},{9,10},{10,1... | collective-permute-start | bytes 196616 | tf_op jit(solution)/shard_map/ppermute | solution.py:32
  56.7 4.3 %collective-permute-start.22 = (bf16[32,1024]{1,0:T(8,128)(2,1)S(1)}, bf16[32,1024]{1,0:T(8,128)(2,1)S(1)}, u32[]{:S(2)}, u32[]{:S(2)}) collective-permute-start(bf16[32,1024]{1,0:T(8,128)(2,1)S(1)} %get-tuple-element.60), channel_id=1, source_target_pairs={{0,3},{1,0},{2,1},{3,2},{4,7},{5,4},{6,5},{7,6},{8,11},{9,8},{10,9... | collective-permute-start | bytes 196616 | tf_op jit(solution)/shard_map/ppermute | solution.py:32
  (3 other events, 15.9 us)

commit v5 on v4

--- a/solution.py
+++ b/solution.py
@@ -36,25 +36,16 @@
     return [0, count // 2] + [by for by in range(1, count) if by != count // 2]
 
 
-def arrivals(count):
-    own, *others = rounds(count)
-    return [own] + others[::-1]
-
-
 def rotate(array, by):
     return array if by == 0 else from_behind(array, "head", by)
 
 
-def gather_heads(array):
-    return [rotate(array, by) for by in arrivals(lax.axis_size("head"))]
-
-
-def scatter_heads(pieces):
+def exchange_heads(pieces):
     return [rotate(piece, by) for piece, by in zip(pieces, rounds(len(pieces)))]
 
 
-def ahead(head_index, by, count):
-    return lax.rem(head_index + by + count, count)
+def ahead(by, count):
+    return lax.rem(lax.axis_index("head") + by + count, count)
 
 
 def kernel_call(body, outs, vmem_bytes, scratch, specs, out_specs, *args):
@@ -71,7 +62,6 @@
     )(*args)
 
 
-scalars = pl.BlockSpec(memory_space=pltpu.SMEM)
 in_hbm = pl.BlockSpec(memory_space=pltpu.HBM)
 
 
@@ -141,15 +131,15 @@
     return request, token_ids - first_token
 
 
-def columns_body(place, pool, *outs):
+def columns_body(pool, *outs):
     width = outs[0].shape[-1]
     for by, out in zip(rounds(len(outs)), outs):
-        first = pl.multiple_of(ahead(place[1], by, len(outs)) * width, width)
+        first = pl.multiple_of(ahead(by, len(outs)) * width, width)
         out[...] = pool[0, :, :, :, pl.ds(first, width)]
 
 
 def project_body(
-    sizes, place, lengths_in, table_in, tokens, w_query, w_keyvalue, queries, keyvalue, bias, residual,
+    sizes, lengths_in, table_in, tokens, w_query, w_keyvalue, queries, keyvalue, bias, residual,
     lengths, table, sems,
 ):
     near, tok_count, head_count, shard_blocks, block_len = sizes
@@ -169,7 +159,7 @@
 
     for copy in copies:
         copy.wait()
-    tok_index, head_index = place[0], place[1]
+    tok_index, head_index = lax.axis_index("tok"), lax.axis_index("head")
     share = residual.shape[0]
     start = pl.multiple_of(head_index * share, share)
     residual[...] = tokens[0, pl.ds(start, share), :].astype(f32)
@@ -195,7 +185,7 @@
         places = slot % block_len
         for block in range(head_count * shard_blocks):
             owner = (tok_index ^ far) * head_count + ahead(
-                head_index, -rounds(head_count)[block // shard_blocks], head_count
+                -rounds(head_count)[block // shard_blocks], head_count
             )
             logical = table[0, owner * shard_blocks + block % shard_blocks]
             places = places + jnp.where(slot // block_len == block, logical * block_len, 0)
@@ -204,7 +194,7 @@
         bias[:, first : first + shard] = jnp.where(allowed, 0.0, -jnp.inf)
 
 
-def self_body(near, head_count, place, queries, bias, w_out, *refs):
+def self_body(near, head_count, queries, bias, w_out, *refs):
     term, refs = refs[-1], refs[:-1]
     near_refs, refs = refs[:near], refs[near:]
     slot_refs, outs = refs[:-head_count], refs[-head_count:]
@@ -221,7 +211,7 @@
     share = rows // head_count
     term[...] = dot(attended, w_out[...]).astype(bf16)
     for by, out in zip(rounds(head_count), outs):
-        start = pl.multiple_of(ahead(place[1], by, head_count) * share, share)
+        start = pl.multiple_of(ahead(by, head_count) * share, share)
         out[...] = term[pl.ds(start, share), :]
 
 
@@ -234,15 +224,17 @@
     term = dot(cross_out, w_cross_out[...]).astype(bf16)
     share = rows_in[0].shape[0]
     for by, out in zip(rounds(head_count), outs):
-        row = arrivals(head_count).index(-by % head_count)
+        row = rounds(head_count).index(-by % head_count)
         out[...] = term[row * share : (row + 1) * share]
 
 
-def after_body(before, *refs):
-    terms, (after, normed) = refs[:-2], refs[-2:]
+def after_body(head_count, before, *refs):
+    terms, (after, *outs) = refs[:head_count], refs[head_count:]
     total = before[...] + sum(term[...].astype(f32) for term in terms)
     after[...] = total
-    normed[...] = layer_norm(total).astype(bf16)
+    normed = layer_norm(total).astype(bf16)
+    for out in outs:
+        out[...] = normed
 
 
 def hidden_body(head_count, w_up, w_down, *refs):
@@ -252,7 +244,7 @@
     term = dot(hidden, w_down[...]).astype(bf16)
     share = rows_in[0].shape[0]
     for by, out in zip(rounds(head_count), outs):
-        row = arrivals(head_count).index(-by % head_count)
+        row = rounds(head_count).index(-by % head_count)
         out[...] = term[row * share : (row + 1) * share]
 
 
@@ -272,29 +264,26 @@
 ):
     rows, model_width = tokens.shape[1:]
     width = w_query.shape[1]
-    tok_index, head_index = lax.axis_index("tok"), lax.axis_index("head")
     tok_count, head_count = lax.axis_size("tok"), lax.axis_size("head")
     share = rows // head_count
-    place = jnp.stack([tok_index, head_index]).astype(i32)
     shard_blocks, block_len = prefix_pool.shape[1:3]
     near_count = 1 + min(SPAN, tok_count - 1)
     key_count = near_count * rows + block_position.shape[1] * block_len
     sizes = (near_count, tok_count, head_count, shard_blocks, block_len)
     shape = jax.ShapeDtypeStruct
     row_pieces = [shape((share, model_width), bf16)] * head_count
-    stats = [shape((share, model_width), f32), shape((share, model_width), bf16)]
+    stats = [shape((share, model_width), f32)] + row_pieces
 
     pool_columns = kernel_call(
         columns_body,
         [shape((shard_blocks, block_len, 2, width), bf16)] * head_count,
         SMALL_VMEM,
         [],
-        [scalars],
-        None,
-        place,
+        [],
+        None,
         prefix_pool,
     )
-    slots = scatter_heads(pool_columns)
+    slots = exchange_heads(pool_columns)
     queries, keyvalue, bias, residual = kernel_call(
         functools.partial(project_body, sizes),
         [
@@ -309,9 +298,8 @@
             pltpu.SMEM(block_position.shape, i32),
             pltpu.SemaphoreType.DMA((2,)),
         ],
-        [scalars, in_hbm, in_hbm],
-        None,
-        place,
+        [in_hbm, in_hbm],
+        None,
         lengths,
         block_position,
         tokens,
@@ -330,17 +318,16 @@
         row_pieces,
         SMALL_VMEM + 36 * rows * key_count,
         [pltpu.VMEM((rows, model_width), bf16)],
-        [scalars],
-        None,
-        place,
+        [],
+        None,
         queries,
         bias,
         w_out,
         *near,
         *all_slots,
     )
-    after_self, normed = kernel_call(
-        after_body, stats, SMALL_VMEM, [], [], None, residual, *scatter_heads(terms)
+    after_self, *normed = kernel_call(
+        functools.partial(after_body, head_count), stats, SMALL_VMEM, [], [], None, residual, *exchange_heads(terms)
     )
     terms = kernel_call(
         functools.partial(cross_body, head_count),
@@ -352,10 +339,10 @@
         w_cross_query,
         cross_cache,
         w_cross_out,
-        *gather_heads(normed),
-    )
-    after_cross, normed = kernel_call(
-        after_body, stats, SMALL_VMEM, [], [], None, after_self, *scatter_heads(terms)
+        *exchange_heads(normed),
+    )
+    after_cross, *normed = kernel_call(
+        functools.partial(after_body, head_count), stats, SMALL_VMEM, [], [], None, after_self, *exchange_heads(terms)
     )
     terms = kernel_call(
         functools.partial(hidden_body, head_count),
@@ -366,9 +353,9 @@
         None,
         w_up,
         w_down,
-        *gather_heads(normed),
-    )
-    result = after_cross + sum(term.astype(f32) for term in scatter_heads(terms))
+        *exchange_heads(normed),
+    )
+    result = after_cross + sum(term.astype(f32) for term in exchange_heads(terms))
     return result.astype(bf16)[None]
 
 

time: 61.7 us -> 60.7 us (0.984)
  Pallas kernels: 6.97 us -> 5.37 us
    pallas_call x7, Pallas kernels: 6.97 us -> 5.37 us  [kernel_call(): pl.pallas_call(body, out_shape=outs, in_specs=list(specs) + [pl.BlockSpec...]
  transfers between devices with their start and end apart: 23 -> 23, of which waited for: 17 -> 17; matrix products, arithmetic and copies ran while one was open for 0% -> 0% of each run, Pallas kernels for 3% -> 2%
where the time goes in v5:
time: 60.7 us; the launch traced here: 60.6 us
  starting transfers between devices  34 us (56%)
  waiting for transfers between devices  19.3 us (32%)
  Pallas kernels  5.37 us (9%)
  local copies, waits for them, and re-layouts  1.11 us (2%)
  other arithmetic  0.67 us (1%)
    ppermute x19, starting transfers between devices, from_behind(): lax.ppermute(array, axis, [(i, (i + by) % count) for i in range(count)])  32.9 us
    ppermute x19, waiting for transfers between devices, from_behind(): lax.ppermute(array, axis, [(i, (i + by) % count) for i in range(count)])  18.2 us
    pallas_call x7, Pallas kernels, kernel_call(): pl.pallas_call(body, out_shape=outs, in_specs=list(specs) + [pl.BlockSpec...  5.37 us
  transfers between devices with their start and end apart: 23, of which 17 were waited for; matrix products, arithmetic and copies ran while one was open for 0% of the time, Pallas kernels for 2%

profile of v5, /device:TPU:0, one launch (start us, length us, event | category | flops | bytes accessed | tf_op | source)
XLA Modules:
  0.0 60.6 jit_solution(14963064918862610694)
XLA Ops:
  0.0 1.1 %copy-done.7 = bf16[1,4,16,2,1024]{4,3,2,1,0:T(2,128)(2,1)S(1)} copy-done((bf16[1,4,16,2,1024]{4,3,2,1,0:T(2,128)(2,1)S(1)}, bf16[1,4,16,2,1024]{4,3,2,1,0:T(2,128)(2,1)}, u32[]{:S(2)}) %copy-start.7) | copy-done | bytes 262168
  1.2 4.1 %collective-permute-start.1 = (bf16[4,16,2,256]{3,2,1,0:T(2,128)(2,1)S(1)}, bf16[4,16,2,256]{3,2,1,0:T(2,128)(2,1)S(1)}, u32[]{:S(2)}, u32[]{:S(2)}) collective-permute-start(bf16[4,16,2,256]{3,2,1,0:T(2,128)(2,1)S(1)} %get-tuple-element.44), channel_id=1, source_target_pairs={{0,2},{1,3},{2,0},{3,1},{4,6},{5,7},{6,4},{7,5},{8,10},{9,11},{10,... | collective-permute-start | bytes 196616 | tf_op jit(solution)/shard_map/ppermute | solution.py:32
  5.3 1.6 %collective-permute-start.2 = (bf16[4,16,2,256]{3,2,1,0:T(2,128)(2,1)S(1)}, bf16[4,16,2,256]{3,2,1,0:T(2,128)(2,1)S(1)}, u32[]{:S(2)}, u32[]{:S(2)}) collective-permute-start(bf16[4,16,2,256]{3,2,1,0:T(2,128)(2,1)S(1)} %get-tuple-element.45), channel_id=1, source_target_pairs={{0,1},{1,2},{2,3},{3,0},{4,5},{5,6},{6,7},{7,4},{8,9},{9,10},{10,1... | collective-permute-start | bytes 196616 | tf_op jit(solution)/shard_map/ppermute | solution.py:32
  6.9 2.2 %collective-permute-start.3 = (bf16[4,16,2,256]{3,2,1,0:T(2,128)(2,1)S(1)}, bf16[4,16,2,256]{3,2,1,0:T(2,128)(2,1)S(1)}, u32[]{:S(2)}, u32[]{:S(2)}) collective-permute-start(bf16[4,16,2,256]{3,2,1,0:T(2,128)(2,1)S(1)} %get-tuple-element.46), channel_id=1, source_target_pairs={{0,3},{1,0},{2,1},{3,2},{4,7},{5,4},{6,5},{7,6},{8,11},{9,8},{10,9... | collective-permute-start | bytes 196616 | tf_op jit(solution)/shard_map/ppermute | solution.py:32
  9.1 1.2 %shard_map.118 = (bf16[128,256]{1,0:T(8,128)(2,1)S(1)}, bf16[128,512]{1,0:T(8,128)(2,1)S(1)}, f32[128,768]{1,0:T(8,128)S(1)}, f32[32,1024]{1,0:T(8,128)S(1)}) custom-call(s32[1,8]{1,0:T(1,128)S(1)} %copy-done.10, s32[1,32]{1,0:T(1,128)S(1)} %copy-done.11, bf16[1,128,1024]{2,1,0:T(8,128)(2,1)S(1)} %copy-done.8, bf16[1024,256]{1,0:T(8,128)(2,1)S(1)} %copy-done.3, ...), custom_call_target="tpu_custom_call" | custom-call | flops 4000000000 | bytes 1835168 | tf_op jit(solution)/shard_map/pallas_call | solution.py:52
  10.9 0.9 %collective-permute-done.3.refs_5_ = bf16[4,16,2,256]{3,2,1,0:T(2,128)(2,1)S(1)} collective-permute-done((bf16[4,16,2,256]{3,2,1,0:T(2,128)(2,1)S(1)}, bf16[4,16,2,256]{3,2,1,0:T(2,128)(2,1)S(1)}, u32[]{:S(2)}, u32[]{:S(2)}) %collective-permute-start.3) | collective-permute-done | bytes 65568 | tf_op jit(solution)/shard_map/ppermute | solution.py:32
  13.6 1.4 %shard_map.120 = (bf16[32,1024]{1,0:T(8,128)(2,1)S(1)}, bf16[32,1024]{1,0:T(8,128)(2,1)S(1)}, bf16[32,1024]{1,0:T(8,128)(2,1)S(1)}, bf16[32,1024]{1,0:T(8,128)(2,1)S(1)}) custom-call(bf16[128,256]{1,0:T(8,128)(2,1)S(1)} %get-tuple-element.40.queries, f32[128,768]{1,0:T(8,128)S(1)} %get-tuple-element.41.bias, bf16[256,1024]{1,0:T(8,128)(2,1)S(1)} %copy-done.4, ...), custom_call_target="tpu_custom_call" | custom-call | flops 4000000000 | bytes 1769472 | tf_op jit(solution)/shard_map/pallas_call | solution.py:52
  15.0 1.8 %collective-permute-start.8 = (bf16[32,1024]{1,0:T(8,128)(2,1)S(1)}, bf16[32,1024]{1,0:T(8,128)(2,1)S(1)}, u32[]{:S(2)}, u32[]{:S(2)}) collective-permute-start(bf16[32,1024]{1,0:T(8,128)(2,1)S(1)} %get-tuple-element.52), channel_id=1, source_target_pairs={{0,2},{1,3},{2,0},{3,1},{4,6},{5,7},{6,4},{7,5},{8,10},{9,11},{10,... | collective-permute-start | bytes 196616 | tf_op jit(solution)/shard_map/ppermute | solution.py:32
  16.8 2.2 %collective-permute-start.9 = (bf16[32,1024]{1,0:T(8,128)(2,1)S(1)}, bf16[32,1024]{1,0:T(8,128)(2,1)S(1)}, u32[]{:S(2)}, u32[]{:S(2)}) collective-permute-start(bf16[32,1024]{1,0:T(8,128)(2,1)S(1)} %get-tuple-element.53), channel_id=1, source_target_pairs={{0,1},{1,2},{2,3},{3,0},{4,5},{5,6},{6,7},{7,4},{8,9},{9,10},{10,1... | collective-permute-start | bytes 196616 | tf_op jit(solution)/shard_map/ppermute | solution.py:32
  19.0 1.6 %collective-permute-start.10 = (bf16[32,1024]{1,0:T(8,128)(2,1)S(1)}, bf16[32,1024]{1,0:T(8,128)(2,1)S(1)}, u32[]{:S(2)}, u32[]{:S(2)}) collective-permute-start(bf16[32,1024]{1,0:T(8,128)(2,1)S(1)} %get-tuple-element.54), channel_id=1, source_target_pairs={{0,3},{1,0},{2,1},{3,2},{4,7},{5,4},{6,5},{7,6},{8,11},{9,8},{10,9... | collective-permute-start | bytes 196616 | tf_op jit(solution)/shard_map/ppermute | solution.py:32
  20.6 3.0 %collective-permute-done.8.refs_1_ = bf16[32,1024]{1,0:T(8,128)(2,1)S(1)} collective-permute-done((bf16[32,1024]{1,0:T(8,128)(2,1)S(1)}, bf16[32,1024]{1,0:T(8,128)(2,1)S(1)}, u32[]{:S(2)}, u32[]{:S(2)}) %collective-permute-start.8) | collective-permute-done | bytes 65568 | tf_op jit(solution)/shard_map/ppermute | solution.py:32
  23.6 0.9 %collective-permute-done.10.refs_3_ = bf16[32,1024]{1,0:T(8,128)(2,1)S(1)} collective-permute-done((bf16[32,1024]{1,0:T(8,128)(2,1)S(1)}, bf16[32,1024]{1,0:T(8,128)(2,1)S(1)}, u32[]{:S(2)}, u32[]{:S(2)}) %collective-permute-start.10) | collective-permute-done | bytes 65568 | tf_op jit(solution)/shard_map/ppermute | solution.py:32
  24.6 1.8 %collective-permute-start.11 = (bf16[32,1024]{1,0:T(8,128)(2,1)S(1)}, bf16[32,1024]{1,0:T(8,128)(2,1)S(1)}, u32[]{:S(2)}, u32[]{:S(2)}) collective-permute-start(bf16[32,1024]{1,0:T(8,128)(2,1)S(1)} %get-tuple-element.57), channel_id=1, source_target_pairs={{0,2},{1,3},{2,0},{3,1},{4,6},{5,7},{6,4},{7,5},{8,10},{9,11},{10,... | collective-permute-start | bytes 196616 | tf_op jit(solution)/shard_map/ppermute | solution.py:32
  26.4 1.2 %collective-permute-start.12 = (bf16[32,1024]{1,0:T(8,128)(2,1)S(1)}, bf16[32,1024]{1,0:T(8,128)(2,1)S(1)}, u32[]{:S(2)}, u32[]{:S(2)}) collective-permute-start(bf16[32,1024]{1,0:T(8,128)(2,1)S(1)} %get-tuple-element.58), channel_id=1, source_target_pairs={{0,1},{1,2},{2,3},{3,0},{4,5},{5,6},{6,7},{7,4},{8,9},{9,10},{10,1... | collective-permute-start | bytes 196616 | tf_op jit(solution)/shard_map/ppermute | solution.py:32
  27.6 2.6 %collective-permute-start.13 = (bf16[32,1024]{1,0:T(8,128)(2,1)S(1)}, bf16[32,1024]{1,0:T(8,128)(2,1)S(1)}, u32[]{:S(2)}, u32[]{:S(2)}) collective-permute-start(bf16[32,1024]{1,0:T(8,128)(2,1)S(1)} %get-tuple-element.59), channel_id=1, source_target_pairs={{0,3},{1,0},{2,1},{3,2},{4,7},{5,4},{6,5},{7,6},{8,11},{9,8},{10,9... | collective-permute-start | bytes 196616 | tf_op jit(solution)/shard_map/ppermute | solution.py:32
  30.2 1.7 %collective-permute-done.11.refs_1_ = bf16[32,1024]{1,0:T(8,128)(2,1)S(1)} collective-permute-done((bf16[32,1024]{1,0:T(8,128)(2,1)S(1)}, bf16[32,1024]{1,0:T(8,128)(2,1)S(1)}, u32[]{:S(2)}, u32[]{:S(2)}) %collective-permute-start.11) | collective-permute-done | bytes 65568 | tf_op jit(solution)/shard_map/ppermute | solution.py:32
  33.0 0.9 %shard_map.122 = (bf16[32,1024]{1,0:T(8,128)(2,1)S(1)}, bf16[32,1024]{1,0:T(8,128)(2,1)S(1)}, bf16[32,1024]{1,0:T(8,128)(2,1)S(1)}, bf16[32,1024]{1,0:T(8,128)(2,1)S(1)}) custom-call(bf16[1024,256]{1,0:T(8,128)(2,1)S(1)} %copy-done.5, bf16[1,256,2,256]{3,2,1,0:T(2,128)(2,1)S(1)} %copy-done.9, bf16[256,1024]{1,0:T(8,128)(2,1)S(1)} %copy-done.6, ...), custom_call_target="tpu_custom_call" | custom-call | flops 4000000000 | bytes 1572864 | tf_op jit(solution)/shard_map/pallas_call | solution.py:52
  33.9 1.1 %collective-permute-start.14 = (bf16[32,1024]{1,0:T(8,128)(2,1)S(1)}, bf16[32,1024]{1,0:T(8,128)(2,1)S(1)}, u32[]{:S(2)}, u32[]{:S(2)}) collective-permute-start(bf16[32,1024]{1,0:T(8,128)(2,1)S(1)} %get-tuple-element.61), channel_id=1, source_target_pairs={{0,2},{1,3},{2,0},{3,1},{4,6},{5,7},{6,4},{7,5},{8,10},{9,11},{10,... | collective-permute-start | bytes 196616 | tf_op jit(solution)/shard_map/ppermute | solution.py:32
  35.0 2.9 %collective-permute-start.15 = (bf16[32,1024]{1,0:T(8,128)(2,1)S(1)}, bf16[32,1024]{1,0:T(8,128)(2,1)S(1)}, u32[]{:S(2)}, u32[]{:S(2)}) collective-permute-start(bf16[32,1024]{1,0:T(8,128)(2,1)S(1)} %get-tuple-element.62), channel_id=1, source_target_pairs={{0,1},{1,2},{2,3},{3,0},{4,5},{5,6},{6,7},{7,4},{8,9},{9,10},{10,1... | collective-permute-start | bytes 196616 | tf_op jit(solution)/shard_map/ppermute | solution.py:32
  37.9 1.0 %collective-permute-start.16 = (bf16[32,1024]{1,0:T(8,128)(2,1)S(1)}, bf16[32,1024]{1,0:T(8,128)(2,1)S(1)}, u32[]{:S(2)}, u32[]{:S(2)}) collective-permute-start(bf16[32,1024]{1,0:T(8,128)(2,1)S(1)} %get-tuple-element.63), channel_id=1, source_target_pairs={{0,3},{1,0},{2,1},{3,2},{4,7},{5,4},{6,5},{7,6},{8,11},{9,8},{10,9... | collective-permute-start | bytes 196616 | tf_op jit(solution)/shard_map/ppermute | solution.py:32
  38.8 1.4 %collective-permute-done.14.refs_1_ = bf16[32,1024]{1,0:T(8,128)(2,1)S(1)} collective-permute-done((bf16[32,1024]{1,0:T(8,128)(2,1)S(1)}, bf16[32,1024]{1,0:T(8,128)(2,1)S(1)}, u32[]{:S(2)}, u32[]{:S(2)}) %collective-permute-start.14) | collective-permute-done | bytes 65568 | tf_op jit(solution)/shard_map/ppermute | solution.py:32
  41.1 1.1 %collective-permute-done.16.refs_3_ = bf16[32,1024]{1,0:T(8,128)(2,1)S(1)} collective-permute-done((bf16[32,1024]{1,0:T(8,128)(2,1)S(1)}, bf16[32,1024]{1,0:T(8,128)(2,1)S(1)}, u32[]{:S(2)}, u32[]{:S(2)}) %collective-permute-start.16) | collective-permute-done | bytes 65568 | tf_op jit(solution)/shard_map/ppermute | solution.py:32
  42.4 0.9 %collective-permute-start.17 = (bf16[32,1024]{1,0:T(8,128)(2,1)S(1)}, bf16[32,1024]{1,0:T(8,128)(2,1)S(1)}, u32[]{:S(2)}, u32[]{:S(2)}) collective-permute-start(bf16[32,1024]{1,0:T(8,128)(2,1)S(1)} %get-tuple-element.66), channel_id=1, source_target_pairs={{0,2},{1,3},{2,0},{3,1},{4,6},{5,7},{6,4},{7,5},{8,10},{9,11},{10,... | collective-permute-start | bytes 196616 | tf_op jit(solution)/shard_map/ppermute | solution.py:32
  43.3 2.8 %collective-permute-start.18 = (bf16[32,1024]{1,0:T(8,128)(2,1)S(1)}, bf16[32,1024]{1,0:T(8,128)(2,1)S(1)}, u32[]{:S(2)}, u32[]{:S(2)}) collective-permute-start(bf16[32,1024]{1,0:T(8,128)(2,1)S(1)} %get-tuple-element.67), channel_id=1, source_target_pairs={{0,1},{1,2},{2,3},{3,0},{4,5},{5,6},{6,7},{7,4},{8,9},{9,10},{10,1... | collective-permute-start | bytes 196616 | tf_op jit(solution)/shard_map/ppermute | solution.py:32
  46.0 1.0 %collective-permute-start.19 = (bf16[32,1024]{1,0:T(8,128)(2,1)S(1)}, bf16[32,1024]{1,0:T(8,128)(2,1)S(1)}, u32[]{:S(2)}, u32[]{:S(2)}) collective-permute-start(bf16[32,1024]{1,0:T(8,128)(2,1)S(1)} %get-tuple-element.68), channel_id=1, source_target_pairs={{0,3},{1,0},{2,1},{3,2},{4,7},{5,4},{6,5},{7,6},{8,11},{9,8},{10,9... | collective-permute-start | bytes 196616 | tf_op jit(solution)/shard_map/ppermute | solution.py:32
  47.1 1.2 %collective-permute-done.17.refs_1_ = bf16[32,1024]{1,0:T(8,128)(2,1)S(1)} collective-permute-done((bf16[32,1024]{1,0:T(8,128)(2,1)S(1)}, bf16[32,1024]{1,0:T(8,128)(2,1)S(1)}, u32[]{:S(2)}, u32[]{:S(2)}) %collective-permute-start.17) | collective-permute-done | bytes 65568 | tf_op jit(solution)/shard_map/ppermute | solution.py:32
  48.3 1.0 %collective-permute-done.18.refs_2_ = bf16[32,1024]{1,0:T(8,128)(2,1)S(1)} collective-permute-done((bf16[32,1024]{1,0:T(8,128)(2,1)S(1)}, bf16[32,1024]{1,0:T(8,128)(2,1)S(1)}, u32[]{:S(2)}, u32[]{:S(2)}) %collective-permute-start.18) | collective-permute-done | bytes 65568 | tf_op jit(solution)/shard_map/ppermute | solution.py:32
  49.3 1.0 %collective-permute-done.19.refs_3_ = bf16[32,1024]{1,0:T(8,128)(2,1)S(1)} collective-permute-done((bf16[32,1024]{1,0:T(8,128)(2,1)S(1)}, bf16[32,1024]{1,0:T(8,128)(2,1)S(1)}, u32[]{:S(2)}, u32[]{:S(2)}) %collective-permute-start.19) | collective-permute-done | bytes 65568 | tf_op jit(solution)/shard_map/ppermute | solution.py:32
  50.3 1.3 %shard_map.124 = (bf16[32,1024]{1,0:T(8,128)(2,1)S(1)}, bf16[32,1024]{1,0:T(8,128)(2,1)S(1)}, bf16[32,1024]{1,0:T(8,128)(2,1)S(1)}, bf16[32,1024]{1,0:T(8,128)(2,1)S(1)}) custom-call(bf16[1024,2048]{1,0:T(8,128)(2,1)S(1)} %copy-done, bf16[2048,1024]{1,0:T(8,128)(2,1)S(1)} %copy-done.1, bf16[32,1024]{1,0:T(8,128)(2,1)S(1)} %get-tuple-element.65.refs_0_, ...), custom_call_target="tpu_custom_call" | custom-call | flops 4000000000 | bytes 8650752 | tf_op jit(solution)/shard_map/pallas_call | solution.py:52
  51.9 3.7 %collective-permute-start.21 = (bf16[32,1024]{1,0:T(8,128)(2,1)S(1)}, bf16[32,1024]{1,0:T(8,128)(2,1)S(1)}, u32[]{:S(2)}, u32[]{:S(2)}) collective-permute-start(bf16[32,1024]{1,0:T(8,128)(2,1)S(1)} %get-tuple-element.71), channel_id=1, source_target_pairs={{0,1},{1,2},{2,3},{3,0},{4,5},{5,6},{6,7},{7,4},{8,9},{9,10},{10,1... | collective-permute-start | bytes 196616 | tf_op jit(solution)/shard_map/ppermute | solution.py:32
  55.8 2.5 %collective-permute-done.20 = bf16[32,1024]{1,0:T(8,128)(2,1)S(1)} collective-permute-done((bf16[32,1024]{1,0:T(8,128)(2,1)S(1)}, bf16[32,1024]{1,0:T(8,128)(2,1)S(1)}, u32[]{:S(2)}, u32[]{:S(2)}) %collective-permute-start.20) | collective-permute-done | bytes 65568 | tf_op jit(solution)/shard_map/ppermute | solution.py:32
  58.2 1.7 %collective-permute-done.22 = bf16[32,1024]{1,0:T(8,128)(2,1)S(1)} collective-permute-done((bf16[32,1024]{1,0:T(8,128)(2,1)S(1)}, bf16[32,1024]{1,0:T(8,128)(2,1)S(1)}, u32[]{:S(2)}, u32[]{:S(2)}) %collective-permute-start.22) | collective-permute-done | bytes 65568 | tf_op jit(solution)/shard_map/ppermute | solution.py:32
  (46 shorter events, 5.9 us)
Async XLA Ops:
  0.0 9.1 %copy-start.2 = (bf16[1024,2,256]{2,1,0:T(2,128)(2,1)S(1)}, bf16[1024,2,256]{2,1,0:T(2,128)(2,1)}, u32[]{:S(2)}) copy-start(bf16[1024,2,256]{2,1,0:T(2,128)(2,1)} %w_keyvalue.1) | copy-start | bytes 3145732
  0.0 9.1 %copy-start.3 = (bf16[1024,256]{1,0:T(8,128)(2,1)S(1)}, bf16[1024,256]{1,0:T(8,128)(2,1)}, u32[]{:S(2)}) copy-start(bf16[1024,256]{1,0:T(8,128)(2,1)} %w_query.1) | copy-start | bytes 1572868
  1.1 8.0 %copy-start.10 = (s32[1,8]{1,0:T(1,128)S(1)}, s32[1,8]{1,0:T(1,128)}, u32[]{:S(2)}) copy-start(s32[1,8]{1,0:T(1,128)} %lengths_in.1) | copy-start | bytes 100
  1.1 8.0 %copy-start.11 = (s32[1,32]{1,0:T(1,128)S(1)}, s32[1,32]{1,0:T(1,128)}, u32[]{:S(2)}) copy-start(s32[1,32]{1,0:T(1,128)} %table_in.1) | copy-start | bytes 388
  1.2 10.7 %collective-permute-start.1 = (bf16[4,16,2,256]{3,2,1,0:T(2,128)(2,1)S(1)}, bf16[4,16,2,256]{3,2,1,0:T(2,128)(2,1)S(1)}, u32[]{:S(2)}, u32[]{:S(2)}) collective-permute-start(bf16[4,16,2,256]{3,2,1,0:T(2,128)(2,1)S(1)} %get-tuple-element.44), channel_id=1, source_target_pairs={{0,2},{1,3},{2,0},{3,1},{4,6},{5,7},{6,4},{7,5},{8,10},{9,11},{10,... | collective-permute-start | bytes 196616 | tf_op jit(solution)/shard_map/ppermute | solution.py:32
  5.3 6.5 %collective-permute-start.2 = (bf16[4,16,2,256]{3,2,1,0:T(2,128)(2,1)S(1)}, bf16[4,16,2,256]{3,2,1,0:T(2,128)(2,1)S(1)}, u32[]{:S(2)}, u32[]{:S(2)}) collective-permute-start(bf16[4,16,2,256]{3,2,1,0:T(2,128)(2,1)S(1)} %get-tuple-element.45), channel_id=1, source_target_pairs={{0,1},{1,2},{2,3},{3,0},{4,5},{5,6},{6,7},{7,4},{8,9},{9,10},{10,1... | collective-permute-start | bytes 196616 | tf_op jit(solution)/shard_map/ppermute | solution.py:32
  6.9 5.0 %collective-permute-start.3 = (bf16[4,16,2,256]{3,2,1,0:T(2,128)(2,1)S(1)}, bf16[4,16,2,256]{3,2,1,0:T(2,128)(2,1)S(1)}, u32[]{:S(2)}, u32[]{:S(2)}) collective-permute-start(bf16[4,16,2,256]{3,2,1,0:T(2,128)(2,1)S(1)} %get-tuple-element.46), channel_id=1, source_target_pairs={{0,3},{1,0},{2,1},{3,2},{4,7},{5,4},{6,5},{7,6},{8,11},{9,8},{10,9... | collective-permute-start | bytes 196616 | tf_op jit(solution)/shard_map/ppermute | solution.py:32
  10.4 3.2 %collective-permute-start = (bf16[128,512]{1,0:T(8,128)(2,1)S(1)}, bf16[128,512]{1,0:T(8,128)(2,1)S(1)}, u32[]{:S(2)}, u32[]{:S(2)}) collective-permute-start(bf16[128,512]{1,0:T(8,128)(2,1)S(1)} %get-tuple-element.42.refs_0_), channel_id=1, source_target_pairs={{0,4},{4,0},{1,5},{5,1},{2,6},{6,2},{3,7},{7,3},{8,12},{12,8},{9,1... | collective-permute-start | bytes 393224 | tf_op jit(solution)/shard_map/ppermute | solution.py:32
  10.4 2.0 %collective-permute-start.4 = (bf16[4,16,2,256]{3,2,1,0:T(2,128)(2,1)S(1)}, bf16[4,16,2,256]{3,2,1,0:T(2,128)(2,1)S(1)}, u32[]{:S(2)}, u32[]{:S(2)}) collective-permute-start(bf16[4,16,2,256]{3,2,1,0:T(2,128)(2,1)S(1)} %get-tuple-element.47.refs_2_), channel_id=1, source_target_pairs={{0,4},{4,0},{1,5},{5,1},{2,6},{6,2},{3,7},{7,3},{8,12},{12,8},{9,1... | collective-permute-start | bytes 196616 | tf_op jit(solution)/shard_map/ppermute | solution.py:27
  11.8 1.3 %collective-permute-start.5 = (bf16[4,16,2,256]{3,2,1,0:T(2,128)(2,1)S(1)}, bf16[4,16,2,256]{3,2,1,0:T(2,128)(2,1)S(1)}, u32[]{:S(2)}, u32[]{:S(2)}) collective-permute-start(bf16[4,16,2,256]{3,2,1,0:T(2,128)(2,1)S(1)} %collective-permute-done.1.refs_3_), channel_id=1, source_target_pairs={{0,4},{4,0},{1,5},{5,1},{2,6},{6,2},{3,7},{7,3},{8,12},{12,8},{9,1... | collective-permute-start | bytes 196616 | tf_op jit(solution)/shard_map/ppermute | solution.py:27
  11.8 1.4 %collective-permute-start.6 = (bf16[4,16,2,256]{3,2,1,0:T(2,128)(2,1)S(1)}, bf16[4,16,2,256]{3,2,1,0:T(2,128)(2,1)S(1)}, u32[]{:S(2)}, u32[]{:S(2)}) collective-permute-start(bf16[4,16,2,256]{3,2,1,0:T(2,128)(2,1)S(1)} %collective-permute-done.2.refs_4_), channel_id=1, source_target_pairs={{0,4},{4,0},{1,5},{5,1},{2,6},{6,2},{3,7},{7,3},{8,12},{12,8},{9,1... | collective-permute-start | bytes 196616 | tf_op jit(solution)/shard_map/ppermute | solution.py:27
  12.3 1.3 %collective-permute-start.7 = (bf16[4,16,2,256]{3,2,1,0:T(2,128)(2,1)S(1)}, bf16[4,16,2,256]{3,2,1,0:T(2,128)(2,1)S(1)}, u32[]{:S(2)}, u32[]{:S(2)}) collective-permute-start(bf16[4,16,2,256]{3,2,1,0:T(2,128)(2,1)S(1)} %collective-permute-done.3.refs_5_), channel_id=1, source_target_pairs={{0,4},{4,0},{1,5},{5,1},{2,6},{6,2},{3,7},{7,3},{8,12},{12,8},{9,1... | collective-permute-start | bytes 196616 | tf_op jit(solution)/shard_map/ppermute | solution.py:27
  15.0 8.5 %collective-permute-start.8 = (bf16[32,1024]{1,0:T(8,128)(2,1)S(1)}, bf16[32,1024]{1,0:T(8,128)(2,1)S(1)}, u32[]{:S(2)}, u32[]{:S(2)}) collective-permute-start(bf16[32,1024]{1,0:T(8,128)(2,1)S(1)} %get-tuple-element.52), channel_id=1, source_target_pairs={{0,2},{1,3},{2,0},{3,1},{4,6},{5,7},{6,4},{7,5},{8,10},{9,11},{10,... | collective-permute-start | bytes 196616 | tf_op jit(solution)/shard_map/ppermute | solution.py:32
  16.8 6.8 %collective-permute-start.9 = (bf16[32,1024]{1,0:T(8,128)(2,1)S(1)}, bf16[32,1024]{1,0:T(8,128)(2,1)S(1)}, u32[]{:S(2)}, u32[]{:S(2)}) collective-permute-start(bf16[32,1024]{1,0:T(8,128)(2,1)S(1)} %get-tuple-element.53), channel_id=1, source_target_pairs={{0,1},{1,2},{2,3},{3,0},{4,5},{5,6},{6,7},{7,4},{8,9},{9,10},{10,1... | collective-permute-start | bytes 196616 | tf_op jit(solution)/shard_map/ppermute | solution.py:32
  19.0 5.4 %collective-permute-start.10 = (bf16[32,1024]{1,0:T(8,128)(2,1)S(1)}, bf16[32,1024]{1,0:T(8,128)(2,1)S(1)}, u32[]{:S(2)}, u32[]{:S(2)}) collective-permute-start(bf16[32,1024]{1,0:T(8,128)(2,1)S(1)} %get-tuple-element.54), channel_id=1, source_target_pairs={{0,3},{1,0},{2,1},{3,2},{4,7},{5,4},{6,5},{7,6},{8,11},{9,8},{10,9... | collective-permute-start | bytes 196616 | tf_op jit(solution)/shard_map/ppermute | solution.py:32
  24.4 8.6 %copy-start.5 = (bf16[1024,256]{1,0:T(8,128)(2,1)S(1)}, bf16[1024,256]{1,0:T(8,128)(2,1)}, u32[]{:S(2)}) copy-start(bf16[1024,256]{1,0:T(8,128)(2,1)} %w_cross_query.1) | copy-start | bytes 1572868
  24.4 8.6 %copy-start.6 = (bf16[256,1024]{1,0:T(8,128)(2,1)S(1)}, bf16[256,1024]{1,0:T(8,128)(2,1)}, u32[]{:S(2)}) copy-start(bf16[256,1024]{1,0:T(8,128)(2,1)} %w_cross_out.1) | copy-start | bytes 1572868
  24.4 8.6 %copy-start.9 = (bf16[1,256,2,256]{3,2,1,0:T(2,128)(2,1)S(1)}, bf16[1,256,2,256]{3,2,1,0:T(2,128)(2,1)}, u32[]{:S(2)}) copy-start(bf16[1,256,2,256]{3,2,1,0:T(2,128)(2,1)} %cross_cache.1) | copy-start | bytes 786436
  24.6 7.3 %collective-permute-start.11 = (bf16[32,1024]{1,0:T(8,128)(2,1)S(1)}, bf16[32,1024]{1,0:T(8,128)(2,1)S(1)}, u32[]{:S(2)}, u32[]{:S(2)}) collective-permute-start(bf16[32,1024]{1,0:T(8,128)(2,1)S(1)} %get-tuple-element.57), channel_id=1, source_target_pairs={{0,2},{1,3},{2,0},{3,1},{4,6},{5,7},{6,4},{7,5},{8,10},{9,11},{10,... | collective-permute-start | bytes 196616 | tf_op jit(solution)/shard_map/ppermute | solution.py:32
  26.4 6.3 %collective-permute-start.12 = (bf16[32,1024]{1,0:T(8,128)(2,1)S(1)}, bf16[32,1024]{1,0:T(8,128)(2,1)S(1)}, u32[]{:S(2)}, u32[]{:S(2)}) collective-permute-start(bf16[32,1024]{1,0:T(8,128)(2,1)S(1)} %get-tuple-element.58), channel_id=1, source_target_pairs={{0,1},{1,2},{2,3},{3,0},{4,5},{5,6},{6,7},{7,4},{8,9},{9,10},{10,1... | collective-permute-start | bytes 196616 | tf_op jit(solution)/shard_map/ppermute | solution.py:32
  27.6 5.4 %collective-permute-start.13 = (bf16[32,1024]{1,0:T(8,128)(2,1)S(1)}, bf16[32,1024]{1,0:T(8,128)(2,1)S(1)}, u32[]{:S(2)}, u32[]{:S(2)}) collective-permute-start(bf16[32,1024]{1,0:T(8,128)(2,1)S(1)} %get-tuple-element.59), channel_id=1, source_target_pairs={{0,3},{1,0},{2,1},{3,2},{4,7},{5,4},{6,5},{7,6},{8,11},{9,8},{10,9... | collective-permute-start | bytes 196616 | tf_op jit(solution)/shard_map/ppermute | solution.py:32
  33.9 6.3 %collective-permute-start.14 = (bf16[32,1024]{1,0:T(8,128)(2,1)S(1)}, bf16[32,1024]{1,0:T(8,128)(2,1)S(1)}, u32[]{:S(2)}, u32[]{:S(2)}) collective-permute-start(bf16[32,1024]{1,0:T(8,128)(2,1)S(1)} %get-tuple-element.61), channel_id=1, source_target_pairs={{0,2},{1,3},{2,0},{3,1},{4,6},{5,7},{6,4},{7,5},{8,10},{9,11},{10,... | collective-permute-start | bytes 196616 | tf_op jit(solution)/shard_map/ppermute | solution.py:32
  35.0 6.1 %collective-permute-start.15 = (bf16[32,1024]{1,0:T(8,128)(2,1)S(1)}, bf16[32,1024]{1,0:T(8,128)(2,1)S(1)}, u32[]{:S(2)}, u32[]{:S(2)}) collective-permute-start(bf16[32,1024]{1,0:T(8,128)(2,1)S(1)} %get-tuple-element.62), channel_id=1, source_target_pairs={{0,1},{1,2},{2,3},{3,0},{4,5},{5,6},{6,7},{7,4},{8,9},{9,10},{10,1... | collective-permute-start | bytes 196616 | tf_op jit(solution)/shard_map/ppermute | solution.py:32
  37.9 4.3 %collective-permute-start.16 = (bf16[32,1024]{1,0:T(8,128)(2,1)S(1)}, bf16[32,1024]{1,0:T(8,128)(2,1)S(1)}, u32[]{:S(2)}, u32[]{:S(2)}) collective-permute-start(bf16[32,1024]{1,0:T(8,128)(2,1)S(1)} %get-tuple-element.63), channel_id=1, source_target_pairs={{0,3},{1,0},{2,1},{3,2},{4,7},{5,4},{6,5},{7,6},{8,11},{9,8},{10,9... | collective-permute-start | bytes 196616 | tf_op jit(solution)/shard_map/ppermute | solution.py:32
  42.1 8.2 %copy-start = (bf16[1024,2048]{1,0:T(8,128)(2,1)S(1)}, bf16[1024,2048]{1,0:T(8,128)(2,1)}, u32[]{:S(2)}) copy-start(bf16[1024,2048]{1,0:T(8,128)(2,1)} %w_up.1) | copy-start | bytes 12582916
  42.1 8.2 %copy-start.1 = (bf16[2048,1024]{1,0:T(8,128)(2,1)S(1)}, bf16[2048,1024]{1,0:T(8,128)(2,1)}, u32[]{:S(2)}) copy-start(bf16[2048,1024]{1,0:T(8,128)(2,1)} %w_down.1) | copy-start | bytes 12582916
  42.4 5.9 %collective-permute-start.17 = (bf16[32,1024]{1,0:T(8,128)(2,1)S(1)}, bf16[32,1024]{1,0:T(8,128)(2,1)S(1)}, u32[]{:S(2)}, u32[]{:S(2)}) collective-permute-start(bf16[32,1024]{1,0:T(8,128)(2,1)S(1)} %get-tuple-element.66), channel_id=1, source_target_pairs={{0,2},{1,3},{2,0},{3,1},{4,6},{5,7},{6,4},{7,5},{8,10},{9,11},{10,... | collective-permute-start | bytes 196616 | tf_op jit(solution)/shard_map/ppermute | solution.py:32
  43.3 6.1 %collective-permute-start.18 = (bf16[32,1024]{1,0:T(8,128)(2,1)S(1)}, bf16[32,1024]{1,0:T(8,128)(2,1)S(1)}, u32[]{:S(2)}, u32[]{:S(2)}) collective-permute-start(bf16[32,1024]{1,0:T(8,128)(2,1)S(1)} %get-tuple-element.67), channel_id=1, source_target_pairs={{0,1},{1,2},{2,3},{3,0},{4,5},{5,6},{6,7},{7,4},{8,9},{9,10},{10,1... | collective-permute-start | bytes 196616 | tf_op jit(solution)/shard_map/ppermute | solution.py:32
  46.0 4.3 %collective-permute-start.19 = (bf16[32,1024]{1,0:T(8,128)(2,1)S(1)}, bf16[32,1024]{1,0:T(8,128)(2,1)S(1)}, u32[]{:S(2)}, u32[]{:S(2)}) collective-permute-start(bf16[32,1024]{1,0:T(8,128)(2,1)S(1)} %get-tuple-element.68), channel_id=1, source_target_pairs={{0,3},{1,0},{2,1},{3,2},{4,7},{5,4},{6,5},{7,6},{8,11},{9,8},{10,9... | collective-permute-start | bytes 196616 | tf_op jit(solution)/shard_map/ppermute | solution.py:32
  51.6 6.6 %collective-permute-start.20 = (bf16[32,1024]{1,0:T(8,128)(2,1)S(1)}, bf16[32,1024]{1,0:T(8,128)(2,1)S(1)}, u32[]{:S(2)}, u32[]{:S(2)}) collective-permute-start(bf16[32,1024]{1,0:T(8,128)(2,1)S(1)} %get-tuple-element.70), channel_id=1, source_target_pairs={{0,2},{1,3},{2,0},{3,1},{4,6},{5,7},{6,4},{7,5},{8,10},{9,11},{10,... | collective-permute-start | bytes 196616 | tf_op jit(solution)/shard_map/ppermute | solution.py:32
  51.9 6.3 %collective-permute-start.21 = (bf16[32,1024]{1,0:T(8,128)(2,1)S(1)}, bf16[32,1024]{1,0:T(8,128)(2,1)S(1)}, u32[]{:S(2)}, u32[]{:S(2)}) collective-permute-start(bf16[32,1024]{1,0:T(8,128)(2,1)S(1)} %get-tuple-element.71), channel_id=1, source_target_pairs={{0,1},{1,2},{2,3},{3,0},{4,5},{5,6},{6,7},{7,4},{8,9},{9,10},{10,1... | collective-permute-start | bytes 196616 | tf_op jit(solution)/shard_map/ppermute | solution.py:32
  55.6 4.3 %collective-permute-start.22 = (bf16[32,1024]{1,0:T(8,128)(2,1)S(1)}, bf16[32,1024]{1,0:T(8,128)(2,1)S(1)}, u32[]{:S(2)}, u32[]{:S(2)}) collective-permute-start(bf16[32,1024]{1,0:T(8,128)(2,1)S(1)} %get-tuple-element.72), channel_id=1, source_target_pairs={{0,3},{1,0},{2,1},{3,2},{4,7},{5,4},{6,5},{7,6},{8,11},{9,8},{10,9... | collective-permute-start | bytes 196616 | tf_op jit(solution)/shard_map/ppermute | solution.py:32
  (3 other events, 15.9 us)

commit v6 on v5

--- a/solution.py
+++ b/solution.py
@@ -16,6 +16,7 @@
 SMALL_VMEM = 12 << 20
 KERNEL_FLOPS = 4 * 10**9
 WIDE_SCORES = 8 << 20
+FULL_ROWS = 128
 
 bf16 = jnp.bfloat16
 f32 = jnp.float32
@@ -33,19 +34,15 @@
 
 
 def rounds(count):
-    return [0, count // 2] + [by for by in range(1, count) if by != count // 2]
-
-
-def rotate(array, by):
-    return array if by == 0 else from_behind(array, "head", by)
+    return [0, count - 1, *range(1, count - 1)]
 
 
 def exchange_heads(pieces):
-    return [rotate(piece, by) for piece, by in zip(pieces, rounds(len(pieces)))]
-
-
-def ahead(by, count):
-    return lax.rem(lax.axis_index("head") + by + count, count)
+    return [pieces[0]] + [swap(p, "head", by) for p, by in zip(pieces[1:], rounds(len(pieces))[1:])]
+
+
+def partner(by):
+    return lax.axis_index("head") ^ by
 
 
 def kernel_call(body, outs, vmem_bytes, scratch, specs, out_specs, *args):
@@ -134,7 +131,7 @@
 def columns_body(pool, *outs):
     width = outs[0].shape[-1]
     for by, out in zip(rounds(len(outs)), outs):
-        first = pl.multiple_of(ahead(by, len(outs)) * width, width)
+        first = pl.multiple_of(partner(by) * width, width)
         out[...] = pool[0, :, :, :, pl.ds(first, width)]
 
 
@@ -184,8 +181,8 @@
     for far in range(tok_count):
         places = slot % block_len
         for block in range(head_count * shard_blocks):
-            owner = (tok_index ^ far) * head_count + ahead(
-                -rounds(head_count)[block // shard_blocks], head_count
+            owner = (tok_index ^ far) * head_count + partner(
+                rounds(head_count)[block // shard_blocks]
             )
             logical = table[0, owner * shard_blocks + block % shard_blocks]
             places = places + jnp.where(slot // block_len == block, logical * block_len, 0)
@@ -211,21 +208,20 @@
     share = rows // head_count
     term[...] = dot(attended, w_out[...]).astype(bf16)
     for by, out in zip(rounds(head_count), outs):
-        start = pl.multiple_of(ahead(by, head_count) * share, share)
+        start = pl.multiple_of(partner(by) * share, share)
         out[...] = term[pl.ds(start, share), :]
 
 
-def cross_body(head_count, w_cross_query, cross_cache, w_cross_out, *refs):
-    rows_in, outs = refs[:head_count], refs[head_count:]
+def cross_body(w_cross_query, cross_cache, w_cross_out, *refs):
+    rows_in, outs = refs[: len(refs) // 2], refs[len(refs) // 2 :]
     normed = jnp.concatenate([ref[...] for ref in rows_in], axis=0)
     queries = dot(normed, w_cross_query[...]).astype(bf16)
     keys, values = split_pair(cross_cache[0])
     cross_out = attend(queries, keys, values, None)
     term = dot(cross_out, w_cross_out[...]).astype(bf16)
     share = rows_in[0].shape[0]
-    for by, out in zip(rounds(head_count), outs):
-        row = rounds(head_count).index(-by % head_count)
-        out[...] = term[row * share : (row + 1) * share]
+    for i, out in enumerate(outs):
+        out[...] = term[i * share : (i + 1) * share]
 
 
 def after_body(head_count, before, *refs):
@@ -237,15 +233,16 @@
         out[...] = normed
 
 
-def hidden_body(head_count, w_up, w_down, *refs):
-    rows_in, outs = refs[:head_count], refs[head_count:]
+def hidden_body(w_up, w_down, *refs):
+    rows_in, outs = refs[: len(refs) // 2], refs[len(refs) // 2 :]
     normed = jnp.concatenate([ref[...] for ref in rows_in], axis=0)
+    if normed.shape[0] < FULL_ROWS:
+        normed = jnp.concatenate([normed] * (FULL_ROWS // normed.shape[0]), axis=0)
     hidden = jax.nn.relu(dot(normed, w_up[...])).astype(bf16)
     term = dot(hidden, w_down[...]).astype(bf16)
     share = rows_in[0].shape[0]
-    for by, out in zip(rounds(head_count), outs):
-        row = rounds(head_count).index(-by % head_count)
-        out[...] = term[row * share : (row + 1) * share]
+    for i, out in enumerate(outs):
+        out[...] = term[i * share : (i + 1) * share]
 
 
 def on_device(
@@ -311,8 +308,10 @@
     ]
     all_slots = list(slots)
     for by in range(1, tok_count):
-        for piece in slots:
-            all_slots.append(swap(lax.optimization_barrier((piece, keyvalue))[0], "tok", by))
+        for i, piece in enumerate(slots):
+            ready = keyvalue if i < 3 else all_slots[-2]
+            piece, _ = lax.optimization_barrier((piece, ready))
+            all_slots.append(swap(piece, "tok", by))
     terms = kernel_call(
         functools.partial(self_body, near_count, head_count),
         row_pieces,
@@ -329,32 +328,38 @@
     after_self, *normed = kernel_call(
         functools.partial(after_body, head_count), stats, SMALL_VMEM, [], [], None, residual, *exchange_heads(terms)
     )
-    terms = kernel_call(
-        functools.partial(cross_body, head_count),
-        row_pieces,
-        SMALL_VMEM,
-        [],
-        [],
-        None,
-        w_cross_query,
-        cross_cache,
-        w_cross_out,
-        *exchange_heads(normed),
-    )
+    arrived = exchange_heads(normed)
+    terms = []
+    for rows_in in (arrived[: head_count // 2], arrived[head_count // 2 :]):
+        terms += kernel_call(
+            cross_body,
+            row_pieces[: len(rows_in)],
+            SMALL_VMEM,
+            [],
+            [],
+            None,
+            w_cross_query,
+            cross_cache,
+            w_cross_out,
+            *rows_in,
+        )
     after_cross, *normed = kernel_call(
         functools.partial(after_body, head_count), stats, SMALL_VMEM, [], [], None, after_self, *exchange_heads(terms)
     )
-    terms = kernel_call(
-        functools.partial(hidden_body, head_count),
-        row_pieces,
-        2 * SMALL_VMEM,
-        [],
-        [],
-        None,
-        w_up,
-        w_down,
-        *exchange_heads(normed),
-    )
+    arrived = exchange_heads(normed)
+    terms = []
+    for rows_in in (arrived[: head_count // 2], arrived[head_count // 2 :]):
+        terms += kernel_call(
+            hidden_body,
+            row_pieces[: len(rows_in)],
+            2 * SMALL_VMEM,
+            [],
+            [],
+            None,
+            w_up,
+            w_down,
+            *rows_in,
+        )
     result = after_cross + sum(term.astype(f32) for term in exchange_heads(terms))
     return result.astype(bf16)[None]
 

time: 60.7 us -> 57.6 us (0.949)
  starting transfers between devices: 34 us -> 28.7 us
  Pallas kernels: 5.37 us -> 7.37 us
    ppermute x19 -> x1, starting transfers between devices: 32.9 us -> 0.51 us  [from_behind(): lax.ppermute(array, axis, [(i, (i + by) % count) for i in range(count)])]
    ppermute x4 -> x22, starting transfers between devices: 1.07 us -> 28.1 us  [swap(): return lax.ppermute(array, axis, [(i, i ^ by) for i in range(count)])]
    ppermute x4 -> x22, waiting for transfers between devices: 1.18 us -> 19.5 us  [swap(): return lax.ppermute(array, axis, [(i, i ^ by) for i in range(count)])]
    ppermute x19 -> x1, waiting for transfers between devices: 18.2 us -> 0.01 us  [from_behind(): lax.ppermute(array, axis, [(i, (i + by) % count) for i in range(count)])]
    pallas_call x7 -> x9, Pallas kernels: 5.37 us -> 7.37 us  [kernel_call(): pl.pallas_call(body, out_shape=outs, in_specs=list(specs) + [pl.BlockSpec...]
  transfers between devices with their start and end apart: 23 -> 23, of which waited for: 17 -> 17; matrix products, arithmetic and copies ran while one was open for 0% -> 0% of each run, Pallas kernels for 2% -> 9%
where the time goes in v6:
time: 57.6 us; the launch traced here: 57.4 us
  starting transfers between devices  28.7 us (50%)
  waiting for transfers between devices  19.5 us (34%)
  Pallas kernels  7.37 us (13%)
  local copies, waits for them, and re-layouts  1.11 us (2%)
  other arithmetic  0.67 us (1%)
    ppermute x22, starting transfers between devices, swap(): return lax.ppermute(array, axis, [(i, i ^ by) for i in range(count)])  28.1 us
    ppermute x22, waiting for transfers between devices, swap(): return lax.ppermute(array, axis, [(i, i ^ by) for i in range(count)])  19.5 us
    pallas_call x9, Pallas kernels, kernel_call(): pl.pallas_call(body, out_shape=outs, in_specs=list(specs) + [pl.BlockSpec...  7.37 us
  transfers between devices with their start and end apart: 23, of which 17 were waited for; matrix products, arithmetic and copies ran while one was open for 0% of the time, Pallas kernels for 9%

profile of v6, /device:TPU:0, one launch (start us, length us, event | category | flops | bytes accessed | tf_op | source)
XLA Modules:
  0.0 57.4 jit_solution(13937655005698212591)
XLA Ops:
  0.0 1.1 %copy-done.7 = bf16[1,4,16,2,1024]{4,3,2,1,0:T(2,128)(2,1)S(1)} copy-done((bf16[1,4,16,2,1024]{4,3,2,1,0:T(2,128)(2,1)S(1)}, bf16[1,4,16,2,1024]{4,3,2,1,0:T(2,128)(2,1)}, u32[]{:S(2)}) %copy-start.7) | copy-done | bytes 262168
  1.2 5.1 %collective-permute-start.1 = (bf16[4,16,2,256]{3,2,1,0:T(2,128)(2,1)S(1)}, bf16[4,16,2,256]{3,2,1,0:T(2,128)(2,1)S(1)}, u32[]{:S(2)}, u32[]{:S(2)}) collective-permute-start(bf16[4,16,2,256]{3,2,1,0:T(2,128)(2,1)S(1)} %get-tuple-element.44), channel_id=1, source_target_pairs={{0,3},{1,2},{2,1},{3,0},{4,7},{5,6},{6,5},{7,4},{8,11},{9,10},{10,... | collective-permute-start | bytes 196616 | tf_op jit(solution)/shard_map/ppermute | solution.py:28
  7.0 1.2 %shard_map.118 = (bf16[128,256]{1,0:T(8,128)(2,1)S(1)}, bf16[128,512]{1,0:T(8,128)(2,1)S(1)}, f32[128,768]{1,0:T(8,128)S(1)}, f32[32,1024]{1,0:T(8,128)S(1)}) custom-call(s32[1,8]{1,0:T(1,128)S(1)} %copy-done.10, s32[1,32]{1,0:T(1,128)S(1)} %copy-done.11, bf16[1,128,1024]{2,1,0:T(8,128)(2,1)S(1)} %copy-done.8, bf16[1024,256]{1,0:T(8,128)(2,1)S(1)} %copy-done.3, ...), custom_call_target="tpu_custom_call" | custom-call | flops 4000000000 | bytes 1835168 | tf_op jit(solution)/shard_map/pallas_call | solution.py:49
  8.2 1.0 %collective-permute-done.1.refs_3_ = bf16[4,16,2,256]{3,2,1,0:T(2,128)(2,1)S(1)} collective-permute-done((bf16[4,16,2,256]{3,2,1,0:T(2,128)(2,1)S(1)}, bf16[4,16,2,256]{3,2,1,0:T(2,128)(2,1)S(1)}, u32[]{:S(2)}, u32[]{:S(2)}) %collective-permute-start.1) | collective-permute-done | bytes 65568 | tf_op jit(solution)/shard_map/ppermute | solution.py:28
  9.7 1.2 %collective-permute-done.2.refs_4_ = bf16[4,16,2,256]{3,2,1,0:T(2,128)(2,1)S(1)} collective-permute-done((bf16[4,16,2,256]{3,2,1,0:T(2,128)(2,1)S(1)}, bf16[4,16,2,256]{3,2,1,0:T(2,128)(2,1)S(1)}, u32[]{:S(2)}, u32[]{:S(2)}) %collective-permute-start.2) | collective-permute-done | bytes 65568 | tf_op jit(solution)/shard_map/ppermute | solution.py:28
  11.0 1.0 %collective-permute-done.3.refs_5_ = bf16[4,16,2,256]{3,2,1,0:T(2,128)(2,1)S(1)} collective-permute-done((bf16[4,16,2,256]{3,2,1,0:T(2,128)(2,1)S(1)}, bf16[4,16,2,256]{3,2,1,0:T(2,128)(2,1)S(1)}, u32[]{:S(2)}, u32[]{:S(2)}) %collective-permute-start.3) | collective-permute-done | bytes 65568 | tf_op jit(solution)/shard_map/ppermute | solution.py:28
  12.2 1.0 %collective-permute-done.7.refs_9_ = bf16[4,16,2,256]{3,2,1,0:T(2,128)(2,1)S(1)} collective-permute-done((bf16[4,16,2,256]{3,2,1,0:T(2,128)(2,1)S(1)}, bf16[4,16,2,256]{3,2,1,0:T(2,128)(2,1)S(1)}, u32[]{:S(2)}, u32[]{:S(2)}) %collective-permute-start.7) | collective-permute-done | bytes 65568 | tf_op jit(solution)/shard_map/ppermute | solution.py:28
  13.2 1.4 %shard_map.120 = (bf16[32,1024]{1,0:T(8,128)(2,1)S(1)}, bf16[32,1024]{1,0:T(8,128)(2,1)S(1)}, bf16[32,1024]{1,0:T(8,128)(2,1)S(1)}, bf16[32,1024]{1,0:T(8,128)(2,1)S(1)}) custom-call(bf16[128,256]{1,0:T(8,128)(2,1)S(1)} %get-tuple-element.40.queries, f32[128,768]{1,0:T(8,128)S(1)} %get-tuple-element.41.bias, bf16[256,1024]{1,0:T(8,128)(2,1)S(1)} %copy-done.4, ...), custom_call_target="tpu_custom_call" | custom-call | flops 4000000000 | bytes 1769472 | tf_op jit(solution)/shard_map/pallas_call | solution.py:49
  14.6 2.5 %collective-permute-start.8 = (bf16[32,1024]{1,0:T(8,128)(2,1)S(1)}, bf16[32,1024]{1,0:T(8,128)(2,1)S(1)}, u32[]{:S(2)}, u32[]{:S(2)}) collective-permute-start(bf16[32,1024]{1,0:T(8,128)(2,1)S(1)} %get-tuple-element.52), channel_id=1, source_target_pairs={{0,3},{1,2},{2,1},{3,0},{4,7},{5,6},{6,5},{7,4},{8,11},{9,10},{10,... | collective-permute-start | bytes 196616 | tf_op jit(solution)/shard_map/ppermute | solution.py:28
  17.2 1.9 %collective-permute-start.10 = (bf16[32,1024]{1,0:T(8,128)(2,1)S(1)}, bf16[32,1024]{1,0:T(8,128)(2,1)S(1)}, u32[]{:S(2)}, u32[]{:S(2)}) collective-permute-start(bf16[32,1024]{1,0:T(8,128)(2,1)S(1)} %get-tuple-element.54), channel_id=1, source_target_pairs={{0,2},{1,3},{2,0},{3,1},{4,6},{5,7},{6,4},{7,5},{8,10},{9,11},{10,... | collective-permute-start | bytes 196616 | tf_op jit(solution)/shard_map/ppermute | solution.py:28
  19.1 2.3 %collective-permute-done.8.refs_1_ = bf16[32,1024]{1,0:T(8,128)(2,1)S(1)} collective-permute-done((bf16[32,1024]{1,0:T(8,128)(2,1)S(1)}, bf16[32,1024]{1,0:T(8,128)(2,1)S(1)}, u32[]{:S(2)}, u32[]{:S(2)}) %collective-permute-start.8) | collective-permute-done | bytes 65568 | tf_op jit(solution)/shard_map/ppermute | solution.py:28
  21.3 1.7 %collective-permute-done.9.refs_2_ = bf16[32,1024]{1,0:T(8,128)(2,1)S(1)} collective-permute-done((bf16[32,1024]{1,0:T(8,128)(2,1)S(1)}, bf16[32,1024]{1,0:T(8,128)(2,1)S(1)}, u32[]{:S(2)}, u32[]{:S(2)}) %collective-permute-start.9) | collective-permute-done | bytes 65568 | tf_op jit(solution)/shard_map/ppermute | solution.py:28
  23.0 1.1 %collective-permute-done.10.refs_3_ = bf16[32,1024]{1,0:T(8,128)(2,1)S(1)} collective-permute-done((bf16[32,1024]{1,0:T(8,128)(2,1)S(1)}, bf16[32,1024]{1,0:T(8,128)(2,1)S(1)}, u32[]{:S(2)}, u32[]{:S(2)}) %collective-permute-start.10) | collective-permute-done | bytes 65568 | tf_op jit(solution)/shard_map/ppermute | solution.py:28
  24.4 1.9 %collective-permute-start.11 = (bf16[32,1024]{1,0:T(8,128)(2,1)S(1)}, bf16[32,1024]{1,0:T(8,128)(2,1)S(1)}, u32[]{:S(2)}, u32[]{:S(2)}) collective-permute-start(bf16[32,1024]{1,0:T(8,128)(2,1)S(1)} %get-tuple-element.57), channel_id=1, source_target_pairs={{0,3},{1,2},{2,1},{3,0},{4,7},{5,6},{6,5},{7,4},{8,11},{9,10},{10,... | collective-permute-start | bytes 196616 | tf_op jit(solution)/shard_map/ppermute | solution.py:28
  26.3 2.5 %collective-permute-start.14 = (bf16[32,1024]{1,0:T(8,128)(2,1)S(1)}, bf16[32,1024]{1,0:T(8,128)(2,1)S(1)}, u32[]{:S(2)}, u32[]{:S(2)}) collective-permute-start(bf16[32,1024]{1,0:T(8,128)(2,1)S(1)} %get-tuple-element.61), channel_id=1, source_target_pairs={{0,2},{1,3},{2,0},{3,1},{4,6},{5,7},{6,4},{7,5},{8,10},{9,11},{10,... | collective-permute-start | bytes 196616 | tf_op jit(solution)/shard_map/ppermute | solution.py:28
  28.8 2.5 %collective-permute-done.11.refs_1_ = bf16[32,1024]{1,0:T(8,128)(2,1)S(1)} collective-permute-done((bf16[32,1024]{1,0:T(8,128)(2,1)S(1)}, bf16[32,1024]{1,0:T(8,128)(2,1)S(1)}, u32[]{:S(2)}, u32[]{:S(2)}) %collective-permute-start.11) | collective-permute-done | bytes 65568 | tf_op jit(solution)/shard_map/ppermute | solution.py:28
  31.3 0.8 %shard_map.122 = (bf16[32,1024]{1,0:T(8,128)(2,1)S(1)}, bf16[32,1024]{1,0:T(8,128)(2,1)S(1)}) custom-call(bf16[1024,256]{1,0:T(8,128)(2,1)S(1)} %copy-done.5, bf16[1,256,2,256]{3,2,1,0:T(2,128)(2,1)S(1)} %copy-done.9, bf16[256,1024]{1,0:T(8,128)(2,1)S(1)} %copy-done.6, bf16[32,1024]{1,0:T(8,128)(2,1)S(1)} %get-tuple-element.56.refs_0_, ...), custom_call_target="tpu_custom_call" | custom-call | flops 4000000000 | bytes 1441792 | tf_op jit(solution)/shard_map/pallas_call | solution.py:49
  32.1 1.3 %collective-permute-start.12 = (bf16[32,1024]{1,0:T(8,128)(2,1)S(1)}, bf16[32,1024]{1,0:T(8,128)(2,1)S(1)}, u32[]{:S(2)}, u32[]{:S(2)}) collective-permute-start(bf16[32,1024]{1,0:T(8,128)(2,1)S(1)} %get-tuple-element.59), channel_id=1, source_target_pairs={{0,3},{1,2},{2,1},{3,0},{4,7},{5,6},{6,5},{7,4},{8,11},{9,10},{10,... | collective-permute-start | bytes 196616 | tf_op jit(solution)/shard_map/ppermute | solution.py:28
  33.4 0.8 %shard_map.123 = (bf16[32,1024]{1,0:T(8,128)(2,1)S(1)}, bf16[32,1024]{1,0:T(8,128)(2,1)S(1)}) custom-call(bf16[1024,256]{1,0:T(8,128)(2,1)S(1)} %copy-done.5, bf16[1,256,2,256]{3,2,1,0:T(2,128)(2,1)S(1)} %copy-done.9, bf16[256,1024]{1,0:T(8,128)(2,1)S(1)} %copy-done.6, bf16[32,1024]{1,0:T(8,128)(2,1)S(1)} %collective-permute-done.13.refs_0_, ...), custom_call_target="tpu_custom_call" | custom-call | flops 4000000000 | bytes 1441792 | tf_op jit(solution)/shard_map/pallas_call | solution.py:49
  34.5 3.1 %collective-permute-start.16 = (bf16[32,1024]{1,0:T(8,128)(2,1)S(1)}, bf16[32,1024]{1,0:T(8,128)(2,1)S(1)}, u32[]{:S(2)}, u32[]{:S(2)}) collective-permute-start(bf16[32,1024]{1,0:T(8,128)(2,1)S(1)} %get-tuple-element.63), channel_id=1, source_target_pairs={{0,2},{1,3},{2,0},{3,1},{4,6},{5,7},{6,4},{7,5},{8,10},{9,11},{10,... | collective-permute-start | bytes 196616 | tf_op jit(solution)/shard_map/ppermute | solution.py:28
  37.6 0.7 %collective-permute-done.12.refs_1_ = bf16[32,1024]{1,0:T(8,128)(2,1)S(1)} collective-permute-done((bf16[32,1024]{1,0:T(8,128)(2,1)S(1)}, bf16[32,1024]{1,0:T(8,128)(2,1)S(1)}, u32[]{:S(2)}, u32[]{:S(2)}) %collective-permute-start.12) | collective-permute-done | bytes 65568 | tf_op jit(solution)/shard_map/ppermute | solution.py:28
  39.0 0.8 %collective-permute-done.16.refs_3_ = bf16[32,1024]{1,0:T(8,128)(2,1)S(1)} collective-permute-done((bf16[32,1024]{1,0:T(8,128)(2,1)S(1)}, bf16[32,1024]{1,0:T(8,128)(2,1)S(1)}, u32[]{:S(2)}, u32[]{:S(2)}) %collective-permute-start.16) | collective-permute-done | bytes 65568 | tf_op jit(solution)/shard_map/ppermute | solution.py:28
  40.0 2.5 %collective-permute-start.17 = (bf16[32,1024]{1,0:T(8,128)(2,1)S(1)}, bf16[32,1024]{1,0:T(8,128)(2,1)S(1)}, u32[]{:S(2)}, u32[]{:S(2)}) collective-permute-start(bf16[32,1024]{1,0:T(8,128)(2,1)S(1)} %get-tuple-element.66), channel_id=1, source_target_pairs={{0,3},{1,2},{2,1},{3,0},{4,7},{5,6},{6,5},{7,4},{8,11},{9,10},{10,... | collective-permute-start | bytes 196616 | tf_op jit(solution)/shard_map/ppermute | solution.py:28
  42.5 1.1 %collective-permute-start.19 = (bf16[32,1024]{1,0:T(8,128)(2,1)S(1)}, bf16[32,1024]{1,0:T(8,128)(2,1)S(1)}, u32[]{:S(2)}, u32[]{:S(2)}) collective-permute-start(bf16[32,1024]{1,0:T(8,128)(2,1)S(1)} %get-tuple-element.69), channel_id=1, source_target_pairs={{0,1},{1,0},{2,3},{3,2},{4,5},{5,4},{6,7},{7,6},{8,9},{9,8},{10,11... | collective-permute-start | bytes 196616 | tf_op jit(solution)/shard_map/ppermute | solution.py:28
  43.6 0.9 %collective-permute-start.20 = (bf16[32,1024]{1,0:T(8,128)(2,1)S(1)}, bf16[32,1024]{1,0:T(8,128)(2,1)S(1)}, u32[]{:S(2)}, u32[]{:S(2)}) collective-permute-start(bf16[32,1024]{1,0:T(8,128)(2,1)S(1)} %get-tuple-element.70), channel_id=1, source_target_pairs={{0,2},{1,3},{2,0},{3,1},{4,6},{5,7},{6,4},{7,5},{8,10},{9,11},{10,... | collective-permute-start | bytes 196616 | tf_op jit(solution)/shard_map/ppermute | solution.py:28
  44.5 1.8 %collective-permute-done.17.refs_1_ = bf16[32,1024]{1,0:T(8,128)(2,1)S(1)} collective-permute-done((bf16[32,1024]{1,0:T(8,128)(2,1)S(1)}, bf16[32,1024]{1,0:T(8,128)(2,1)S(1)}, u32[]{:S(2)}, u32[]{:S(2)}) %collective-permute-start.17) | collective-permute-done | bytes 65568 | tf_op jit(solution)/shard_map/ppermute | solution.py:28
  46.2 1.3 %shard_map.125 = (bf16[32,1024]{1,0:T(8,128)(2,1)S(1)}, bf16[32,1024]{1,0:T(8,128)(2,1)S(1)}) custom-call(bf16[1024,2048]{1,0:T(8,128)(2,1)S(1)} %copy-done, bf16[2048,1024]{1,0:T(8,128)(2,1)S(1)} %copy-done.1, bf16[32,1024]{1,0:T(8,128)(2,1)S(1)} %get-tuple-element.65.refs_0_, bf16[32,1024]{1,0:T(8,128)(2,1)S(1)} %collective-permute-done.17.refs_1_), custom_call_target="tpu_custom_call" | custom-call | flops 4000000000 | bytes 8519680 | tf_op jit(solution)/shard_map/pallas_call | solution.py:49
  47.5 2.6 %collective-permute-start.18 = (bf16[32,1024]{1,0:T(8,128)(2,1)S(1)}, bf16[32,1024]{1,0:T(8,128)(2,1)S(1)}, u32[]{:S(2)}, u32[]{:S(2)}) collective-permute-start(bf16[32,1024]{1,0:T(8,128)(2,1)S(1)} %get-tuple-element.68), channel_id=1, source_target_pairs={{0,3},{1,2},{2,1},{3,0},{4,7},{5,6},{6,5},{7,4},{8,11},{9,10},{10,... | collective-permute-start | bytes 196616 | tf_op jit(solution)/shard_map/ppermute | solution.py:28
  50.2 1.3 %shard_map.126 = (bf16[32,1024]{1,0:T(8,128)(2,1)S(1)}, bf16[32,1024]{1,0:T(8,128)(2,1)S(1)}) custom-call(bf16[1024,2048]{1,0:T(8,128)(2,1)S(1)} %copy-done, bf16[2048,1024]{1,0:T(8,128)(2,1)S(1)} %copy-done.1, bf16[32,1024]{1,0:T(8,128)(2,1)S(1)} %collective-permute-done.19.refs_0_, bf16[32,1024]{1,0:T(8,128)(2,1)S(1)} %collective-permute-done.20.refs_1_), custom_call_target="tpu_custom_call" | custom-call | flops 4000000000 | bytes 8519680 | tf_op jit(solution)/shard_map/pallas_call | solution.py:49
  51.6 1.8 %collective-permute-start.22 = (bf16[32,1024]{1,0:T(8,128)(2,1)S(1)}, bf16[32,1024]{1,0:T(8,128)(2,1)S(1)}, u32[]{:S(2)}, u32[]{:S(2)}) collective-permute-start(bf16[32,1024]{1,0:T(8,128)(2,1)S(1)} %get-tuple-element.72), channel_id=1, source_target_pairs={{0,2},{1,3},{2,0},{3,1},{4,6},{5,7},{6,4},{7,5},{8,10},{9,11},{10,... | collective-permute-start | bytes 196616 | tf_op jit(solution)/shard_map/ppermute | solution.py:28
  53.9 1.9 %collective-permute-done.21 = bf16[32,1024]{1,0:T(8,128)(2,1)S(1)} collective-permute-done((bf16[32,1024]{1,0:T(8,128)(2,1)S(1)}, bf16[32,1024]{1,0:T(8,128)(2,1)S(1)}, u32[]{:S(2)}, u32[]{:S(2)}) %collective-permute-start.21) | collective-permute-done | bytes 65568 | tf_op jit(solution)/shard_map/ppermute | solution.py:28
  55.8 1.0 %collective-permute-done.22 = bf16[32,1024]{1,0:T(8,128)(2,1)S(1)} collective-permute-done((bf16[32,1024]{1,0:T(8,128)(2,1)S(1)}, bf16[32,1024]{1,0:T(8,128)(2,1)S(1)}, u32[]{:S(2)}, u32[]{:S(2)}) %collective-permute-start.22) | collective-permute-done | bytes 65568 | tf_op jit(solution)/shard_map/ppermute | solution.py:28
  (48 shorter events, 4.4 us)
Async XLA Ops:
  0.0 6.9 %copy-start.2 = (bf16[1024,2,256]{2,1,0:T(2,128)(2,1)S(1)}, bf16[1024,2,256]{2,1,0:T(2,128)(2,1)}, u32[]{:S(2)}) copy-start(bf16[1024,2,256]{2,1,0:T(2,128)(2,1)} %w_keyvalue.1) | copy-start | bytes 3145732
  0.0 6.9 %copy-start.3 = (bf16[1024,256]{1,0:T(8,128)(2,1)S(1)}, bf16[1024,256]{1,0:T(8,128)(2,1)}, u32[]{:S(2)}) copy-start(bf16[1024,256]{1,0:T(8,128)(2,1)} %w_query.1) | copy-start | bytes 1572868
  1.1 5.9 %copy-start.11 = (s32[1,32]{1,0:T(1,128)S(1)}, s32[1,32]{1,0:T(1,128)}, u32[]{:S(2)}) copy-start(s32[1,32]{1,0:T(1,128)} %table_in.1) | copy-start | bytes 388
  1.2 8.0 %collective-permute-start.1 = (bf16[4,16,2,256]{3,2,1,0:T(2,128)(2,1)S(1)}, bf16[4,16,2,256]{3,2,1,0:T(2,128)(2,1)S(1)}, u32[]{:S(2)}, u32[]{:S(2)}) collective-permute-start(bf16[4,16,2,256]{3,2,1,0:T(2,128)(2,1)S(1)} %get-tuple-element.44), channel_id=1, source_target_pairs={{0,3},{1,2},{2,1},{3,0},{4,7},{5,6},{6,5},{7,4},{8,11},{9,10},{10,... | collective-permute-start | bytes 196616 | tf_op jit(solution)/shard_map/ppermute | solution.py:28
  6.3 4.7 %collective-permute-start.2 = (bf16[4,16,2,256]{3,2,1,0:T(2,128)(2,1)S(1)}, bf16[4,16,2,256]{3,2,1,0:T(2,128)(2,1)S(1)}, u32[]{:S(2)}, u32[]{:S(2)}) collective-permute-start(bf16[4,16,2,256]{3,2,1,0:T(2,128)(2,1)S(1)} %get-tuple-element.45), channel_id=1, source_target_pairs={{0,1},{1,0},{2,3},{3,2},{4,5},{5,4},{6,7},{7,6},{8,9},{9,8},{10,11... | collective-permute-start | bytes 196616 | tf_op jit(solution)/shard_map/ppermute | solution.py:28
  6.3 6.9 %copy-start.4 = (bf16[256,1024]{1,0:T(8,128)(2,1)S(1)}, bf16[256,1024]{1,0:T(8,128)(2,1)}, u32[]{:S(2)}) copy-start(bf16[256,1024]{1,0:T(8,128)(2,1)} %w_out.1) | copy-start | bytes 1572868
  6.3 5.6 %collective-permute-start.3 = (bf16[4,16,2,256]{3,2,1,0:T(2,128)(2,1)S(1)}, bf16[4,16,2,256]{3,2,1,0:T(2,128)(2,1)S(1)}, u32[]{:S(2)}, u32[]{:S(2)}) collective-permute-start(bf16[4,16,2,256]{3,2,1,0:T(2,128)(2,1)S(1)} %get-tuple-element.46), channel_id=1, source_target_pairs={{0,2},{1,3},{2,0},{3,1},{4,6},{5,7},{6,4},{7,5},{8,10},{9,11},{10,... | collective-permute-start | bytes 196616 | tf_op jit(solution)/shard_map/ppermute | solution.py:28
  9.2 2.7 %collective-permute-start.5 = (bf16[4,16,2,256]{3,2,1,0:T(2,128)(2,1)S(1)}, bf16[4,16,2,256]{3,2,1,0:T(2,128)(2,1)S(1)}, u32[]{:S(2)}, u32[]{:S(2)}) collective-permute-start(bf16[4,16,2,256]{3,2,1,0:T(2,128)(2,1)S(1)} %collective-permute-done.1.refs_3_), channel_id=1, source_target_pairs={{0,4},{4,0},{1,5},{5,1},{2,6},{6,2},{3,7},{7,3},{8,12},{12,8},{9,1... | collective-permute-start | bytes 196616 | tf_op jit(solution)/shard_map/ppermute | solution.py:28
  9.2 3.0 %collective-permute-start = (bf16[128,512]{1,0:T(8,128)(2,1)S(1)}, bf16[128,512]{1,0:T(8,128)(2,1)S(1)}, u32[]{:S(2)}, u32[]{:S(2)}) collective-permute-start(bf16[128,512]{1,0:T(8,128)(2,1)S(1)} %get-tuple-element.42.refs_0_), channel_id=1, source_target_pairs={{0,4},{4,0},{1,5},{5,1},{2,6},{6,2},{3,7},{7,3},{8,12},{12,8},{9,1... | collective-permute-start | bytes 393224 | tf_op jit(solution)/shard_map/ppermute | solution.py:33
  9.7 2.2 %collective-permute-start.4 = (bf16[4,16,2,256]{3,2,1,0:T(2,128)(2,1)S(1)}, bf16[4,16,2,256]{3,2,1,0:T(2,128)(2,1)S(1)}, u32[]{:S(2)}, u32[]{:S(2)}) collective-permute-start(bf16[4,16,2,256]{3,2,1,0:T(2,128)(2,1)S(1)} %get-tuple-element.47.refs_2_), channel_id=1, source_target_pairs={{0,4},{4,0},{1,5},{5,1},{2,6},{6,2},{3,7},{7,3},{8,12},{12,8},{9,1... | collective-permute-start | bytes 196616 | tf_op jit(solution)/shard_map/ppermute | solution.py:28
  11.0 1.3 %collective-permute-start.6 = (bf16[4,16,2,256]{3,2,1,0:T(2,128)(2,1)S(1)}, bf16[4,16,2,256]{3,2,1,0:T(2,128)(2,1)S(1)}, u32[]{:S(2)}, u32[]{:S(2)}) collective-permute-start(bf16[4,16,2,256]{3,2,1,0:T(2,128)(2,1)S(1)} %collective-permute-done.2.refs_4_), channel_id=1, source_target_pairs={{0,4},{4,0},{1,5},{5,1},{2,6},{6,2},{3,7},{7,3},{8,12},{12,8},{9,1... | collective-permute-start | bytes 196616 | tf_op jit(solution)/shard_map/ppermute | solution.py:28
  11.9 1.3 %collective-permute-start.7 = (bf16[4,16,2,256]{3,2,1,0:T(2,128)(2,1)S(1)}, bf16[4,16,2,256]{3,2,1,0:T(2,128)(2,1)S(1)}, u32[]{:S(2)}, u32[]{:S(2)}) collective-permute-start(bf16[4,16,2,256]{3,2,1,0:T(2,128)(2,1)S(1)} %collective-permute-done.3.refs_5_), channel_id=1, source_target_pairs={{0,4},{4,0},{1,5},{5,1},{2,6},{6,2},{3,7},{7,3},{8,12},{12,8},{9,1... | collective-permute-start | bytes 196616 | tf_op jit(solution)/shard_map/ppermute | solution.py:28
  14.6 6.7 %collective-permute-start.8 = (bf16[32,1024]{1,0:T(8,128)(2,1)S(1)}, bf16[32,1024]{1,0:T(8,128)(2,1)S(1)}, u32[]{:S(2)}, u32[]{:S(2)}) collective-permute-start(bf16[32,1024]{1,0:T(8,128)(2,1)S(1)} %get-tuple-element.52), channel_id=1, source_target_pairs={{0,3},{1,2},{2,1},{3,0},{4,7},{5,6},{6,5},{7,4},{8,11},{9,10},{10,... | collective-permute-start | bytes 196616 | tf_op jit(solution)/shard_map/ppermute | solution.py:28
  17.1 5.9 %collective-permute-start.9 = (bf16[32,1024]{1,0:T(8,128)(2,1)S(1)}, bf16[32,1024]{1,0:T(8,128)(2,1)S(1)}, u32[]{:S(2)}, u32[]{:S(2)}) collective-permute-start(bf16[32,1024]{1,0:T(8,128)(2,1)S(1)} %get-tuple-element.53), channel_id=1, source_target_pairs={{0,1},{1,0},{2,3},{3,2},{4,5},{5,4},{6,7},{7,6},{8,9},{9,8},{10,11... | collective-permute-start | bytes 196616 | tf_op jit(solution)/shard_map/ppermute | solution.py:28
  17.2 7.0 %collective-permute-start.10 = (bf16[32,1024]{1,0:T(8,128)(2,1)S(1)}, bf16[32,1024]{1,0:T(8,128)(2,1)S(1)}, u32[]{:S(2)}, u32[]{:S(2)}) collective-permute-start(bf16[32,1024]{1,0:T(8,128)(2,1)S(1)} %get-tuple-element.54), channel_id=1, source_target_pairs={{0,2},{1,3},{2,0},{3,1},{4,6},{5,7},{6,4},{7,5},{8,10},{9,11},{10,... | collective-permute-start | bytes 196616 | tf_op jit(solution)/shard_map/ppermute | solution.py:28
  24.1 7.1 %copy-start.5 = (bf16[1024,256]{1,0:T(8,128)(2,1)S(1)}, bf16[1024,256]{1,0:T(8,128)(2,1)}, u32[]{:S(2)}) copy-start(bf16[1024,256]{1,0:T(8,128)(2,1)} %w_cross_query.3) | copy-start | bytes 1572868
  24.1 7.1 %copy-start.6 = (bf16[256,1024]{1,0:T(8,128)(2,1)S(1)}, bf16[256,1024]{1,0:T(8,128)(2,1)}, u32[]{:S(2)}) copy-start(bf16[256,1024]{1,0:T(8,128)(2,1)} %w_cross_out.3) | copy-start | bytes 1572868
  24.1 7.1 %copy-start.9 = (bf16[1,256,2,256]{3,2,1,0:T(2,128)(2,1)S(1)}, bf16[1,256,2,256]{3,2,1,0:T(2,128)(2,1)}, u32[]{:S(2)}) copy-start(bf16[1,256,2,256]{3,2,1,0:T(2,128)(2,1)} %cross_cache.3) | copy-start | bytes 786436
  24.4 6.9 %collective-permute-start.11 = (bf16[32,1024]{1,0:T(8,128)(2,1)S(1)}, bf16[32,1024]{1,0:T(8,128)(2,1)S(1)}, u32[]{:S(2)}, u32[]{:S(2)}) collective-permute-start(bf16[32,1024]{1,0:T(8,128)(2,1)S(1)} %get-tuple-element.57), channel_id=1, source_target_pairs={{0,3},{1,2},{2,1},{3,0},{4,7},{5,6},{6,5},{7,4},{8,11},{9,10},{10,... | collective-permute-start | bytes 196616 | tf_op jit(solution)/shard_map/ppermute | solution.py:28
  26.3 7.1 %collective-permute-start.13 = (bf16[32,1024]{1,0:T(8,128)(2,1)S(1)}, bf16[32,1024]{1,0:T(8,128)(2,1)S(1)}, u32[]{:S(2)}, u32[]{:S(2)}) collective-permute-start(bf16[32,1024]{1,0:T(8,128)(2,1)S(1)} %get-tuple-element.60), channel_id=1, source_target_pairs={{0,1},{1,0},{2,3},{3,2},{4,5},{5,4},{6,7},{7,6},{8,9},{9,8},{10,11... | collective-permute-start | bytes 196616 | tf_op jit(solution)/shard_map/ppermute | solution.py:28
  26.3 7.1 %collective-permute-start.14 = (bf16[32,1024]{1,0:T(8,128)(2,1)S(1)}, bf16[32,1024]{1,0:T(8,128)(2,1)S(1)}, u32[]{:S(2)}, u32[]{:S(2)}) collective-permute-start(bf16[32,1024]{1,0:T(8,128)(2,1)S(1)} %get-tuple-element.61), channel_id=1, source_target_pairs={{0,2},{1,3},{2,0},{3,1},{4,6},{5,7},{6,4},{7,5},{8,10},{9,11},{10,... | collective-permute-start | bytes 196616 | tf_op jit(solution)/shard_map/ppermute | solution.py:28
  32.1 6.2 %collective-permute-start.12 = (bf16[32,1024]{1,0:T(8,128)(2,1)S(1)}, bf16[32,1024]{1,0:T(8,128)(2,1)S(1)}, u32[]{:S(2)}, u32[]{:S(2)}) collective-permute-start(bf16[32,1024]{1,0:T(8,128)(2,1)S(1)} %get-tuple-element.59), channel_id=1, source_target_pairs={{0,3},{1,2},{2,1},{3,0},{4,7},{5,6},{6,5},{7,4},{8,11},{9,10},{10,... | collective-permute-start | bytes 196616 | tf_op jit(solution)/shard_map/ppermute | solution.py:28
  34.3 4.7 %collective-permute-start.15 = (bf16[32,1024]{1,0:T(8,128)(2,1)S(1)}, bf16[32,1024]{1,0:T(8,128)(2,1)S(1)}, u32[]{:S(2)}, u32[]{:S(2)}) collective-permute-start(bf16[32,1024]{1,0:T(8,128)(2,1)S(1)} %get-tuple-element.62), channel_id=1, source_target_pairs={{0,1},{1,0},{2,3},{3,2},{4,5},{5,4},{6,7},{7,6},{8,9},{9,8},{10,11... | collective-permute-start | bytes 196616 | tf_op jit(solution)/shard_map/ppermute | solution.py:28
  34.5 5.3 %collective-permute-start.16 = (bf16[32,1024]{1,0:T(8,128)(2,1)S(1)}, bf16[32,1024]{1,0:T(8,128)(2,1)S(1)}, u32[]{:S(2)}, u32[]{:S(2)}) collective-permute-start(bf16[32,1024]{1,0:T(8,128)(2,1)S(1)} %get-tuple-element.63), channel_id=1, source_target_pairs={{0,2},{1,3},{2,0},{3,1},{4,6},{5,7},{6,4},{7,5},{8,10},{9,11},{10,... | collective-permute-start | bytes 196616 | tf_op jit(solution)/shard_map/ppermute | solution.py:28
  39.8 6.4 %copy-start = (bf16[1024,2048]{1,0:T(8,128)(2,1)S(1)}, bf16[1024,2048]{1,0:T(8,128)(2,1)}, u32[]{:S(2)}) copy-start(bf16[1024,2048]{1,0:T(8,128)(2,1)} %w_up.3) | copy-start | bytes 12582916
  39.8 6.4 %copy-start.1 = (bf16[2048,1024]{1,0:T(8,128)(2,1)S(1)}, bf16[2048,1024]{1,0:T(8,128)(2,1)}, u32[]{:S(2)}) copy-start(bf16[2048,1024]{1,0:T(8,128)(2,1)} %w_down.3) | copy-start | bytes 12582916
  40.0 6.2 %collective-permute-start.17 = (bf16[32,1024]{1,0:T(8,128)(2,1)S(1)}, bf16[32,1024]{1,0:T(8,128)(2,1)S(1)}, u32[]{:S(2)}, u32[]{:S(2)}) collective-permute-start(bf16[32,1024]{1,0:T(8,128)(2,1)S(1)} %get-tuple-element.66), channel_id=1, source_target_pairs={{0,3},{1,2},{2,1},{3,0},{4,7},{5,6},{6,5},{7,4},{8,11},{9,10},{10,... | collective-permute-start | bytes 196616 | tf_op jit(solution)/shard_map/ppermute | solution.py:28
  42.5 7.6 %collective-permute-start.19 = (bf16[32,1024]{1,0:T(8,128)(2,1)S(1)}, bf16[32,1024]{1,0:T(8,128)(2,1)S(1)}, u32[]{:S(2)}, u32[]{:S(2)}) collective-permute-start(bf16[32,1024]{1,0:T(8,128)(2,1)S(1)} %get-tuple-element.69), channel_id=1, source_target_pairs={{0,1},{1,0},{2,3},{3,2},{4,5},{5,4},{6,7},{7,6},{8,9},{9,8},{10,11... | collective-permute-start | bytes 196616 | tf_op jit(solution)/shard_map/ppermute | solution.py:28
  43.6 6.6 %collective-permute-start.20 = (bf16[32,1024]{1,0:T(8,128)(2,1)S(1)}, bf16[32,1024]{1,0:T(8,128)(2,1)S(1)}, u32[]{:S(2)}, u32[]{:S(2)}) collective-permute-start(bf16[32,1024]{1,0:T(8,128)(2,1)S(1)} %get-tuple-element.70), channel_id=1, source_target_pairs={{0,2},{1,3},{2,0},{3,1},{4,6},{5,7},{6,4},{7,5},{8,10},{9,11},{10,... | collective-permute-start | bytes 196616 | tf_op jit(solution)/shard_map/ppermute | solution.py:28
  47.5 6.4 %collective-permute-start.18 = (bf16[32,1024]{1,0:T(8,128)(2,1)S(1)}, bf16[32,1024]{1,0:T(8,128)(2,1)S(1)}, u32[]{:S(2)}, u32[]{:S(2)}) collective-permute-start(bf16[32,1024]{1,0:T(8,128)(2,1)S(1)} %get-tuple-element.68), channel_id=1, source_target_pairs={{0,3},{1,2},{2,1},{3,0},{4,7},{5,6},{6,5},{7,4},{8,11},{9,10},{10,... | collective-permute-start | bytes 196616 | tf_op jit(solution)/shard_map/ppermute | solution.py:28
  51.5 4.3 %collective-permute-start.21 = (bf16[32,1024]{1,0:T(8,128)(2,1)S(1)}, bf16[32,1024]{1,0:T(8,128)(2,1)S(1)}, u32[]{:S(2)}, u32[]{:S(2)}) collective-permute-start(bf16[32,1024]{1,0:T(8,128)(2,1)S(1)} %get-tuple-element.71), channel_id=1, source_target_pairs={{0,1},{1,0},{2,3},{3,2},{4,5},{5,4},{6,7},{7,6},{8,9},{9,8},{10,11... | collective-permute-start | bytes 196616 | tf_op jit(solution)/shard_map/ppermute | solution.py:28
  51.6 5.2 %collective-permute-start.22 = (bf16[32,1024]{1,0:T(8,128)(2,1)S(1)}, bf16[32,1024]{1,0:T(8,128)(2,1)S(1)}, u32[]{:S(2)}, u32[]{:S(2)}) collective-permute-start(bf16[32,1024]{1,0:T(8,128)(2,1)S(1)} %get-tuple-element.72), channel_id=1, source_target_pairs={{0,2},{1,3},{2,0},{3,1},{4,6},{5,7},{6,4},{7,5},{8,10},{9,11},{10,... | collective-permute-start | bytes 196616 | tf_op jit(solution)/shard_map/ppermute | solution.py:28
  (3 other events, 12.8 us)

commit v7 on v6

--- a/solution.py
+++ b/solution.py
@@ -17,6 +17,14 @@
 KERNEL_FLOPS = 4 * 10**9
 WIDE_SCORES = 8 << 20
 FULL_ROWS = 128
+LANES = 128
+
+POOL_ORDER = (0, 3, 1, 2)
+SELF_SUM_ORDER = (0, 2, 1, 3)
+CROSS_ROWS_ORDER = (0, 3, 1, 2)
+CROSS_SUM_ORDER = (0, 1, 3, 2)
+HIDDEN_ROWS_ORDER = (0, 3, 2, 1)
+HIDDEN_SUM_ORDER = (0, 3, 1, 2)
 
 bf16 = jnp.bfloat16
 f32 = jnp.float32
@@ -33,12 +41,8 @@
     return lax.ppermute(array, axis, [(i, (i + by) % count) for i in range(count)])
 
 
-def rounds(count):
-    return [0, count - 1, *range(1, count - 1)]
-
-
-def exchange_heads(pieces):
-    return [pieces[0]] + [swap(p, "head", by) for p, by in zip(pieces[1:], rounds(len(pieces))[1:])]
+def exchange_heads(pieces, order):
+    return [swap(pieces[by], "head", by) if by else pieces[0] for by in order]
 
 
 def partner(by):
@@ -82,37 +86,45 @@
     return lax.broadcasted_iota(i32, shape, len(shape) - 1) // HEAD_DIM
 
 
-def attend_heads(queries, keys, values, bias, heads):
-    rows, width = queries.shape
-    lanes = head_lanes((rows, width))
+def head_sets(rows, width, keys):
+    heads = list(range(width // HEAD_DIM))
+    if len(heads) * rows * keys * 4 <= WIDE_SCORES:
+        return [heads]
+    return [[h] for h in heads]
+
+
+def head_scores(queries, keys, bias, heads):
+    lanes = head_lanes(queries.shape)
     stacked = jnp.concatenate(
         [jnp.where(lanes == h, queries, jnp.zeros_like(queries)) for h in heads], axis=0
     )
     scores = lax.dot_general(
         stacked, keys, (((1,), (1,)), ((), ())), preferred_element_type=f32
-    ).reshape(len(heads), rows, keys.shape[0])
+    ).reshape(len(heads), queries.shape[0], keys.shape[0])
     scores = scores * SCALE
-    if bias is not None:
-        scores = scores + bias[None]
-    row_max = jnp.max(scores, axis=-1, keepdims=True)
-    weights = jnp.exp(scores - row_max)
-    row_sum = jnp.sum(weights, axis=-1, keepdims=True)
-    summed = dot(weights.astype(bf16).reshape(len(heads) * rows, -1), values)
-    summed = summed.reshape(len(heads), rows, width) / row_sum
-    result = jnp.zeros((rows, width), f32)
+    return scores if bias is None else scores + bias[None]
+
+
+def weigh(weights, values):
+    heads, rows, keys = weights.shape
+    return dot(weights.astype(bf16).reshape(heads * rows, keys), values).reshape(heads, rows, -1)
+
+
+def own_lanes(per_head, heads):
+    lanes = head_lanes(per_head.shape[1:])
+    result = jnp.zeros(per_head.shape[1:], f32)
     for i, h in enumerate(heads):
-        result = jnp.where(lanes == h, summed[i], result)
+        result = jnp.where(lanes == h, per_head[i], result)
     return result
 
 
-def attend(queries, keys, values, bias):
-    rows, width = queries.shape
-    heads = list(range(width // HEAD_DIM))
-    if len(heads) * rows * keys.shape[0] * 4 <= WIDE_SCORES:
-        return attend_heads(queries, keys, values, bias, heads).astype(bf16)
-    result = attend_heads(queries, keys, values, bias, heads[:1])
-    for h in heads[1:]:
-        result = result + attend_heads(queries, keys, values, bias, [h])
+def attend(queries, keys, values):
+    result = 0.0
+    for heads in head_sets(*queries.shape, keys.shape[0]):
+        scores = head_scores(queries, keys, None, heads)
+        weights = jnp.exp(scores - jnp.max(scores, axis=-1, keepdims=True))
+        row_sum = jnp.sum(weights, axis=-1, keepdims=True)
+        result = result + own_lanes(weigh(weights, values) / row_sum, heads)
     return result.astype(bf16)
 
 
@@ -130,13 +142,13 @@
 
 def columns_body(pool, *outs):
     width = outs[0].shape[-1]
-    for by, out in zip(rounds(len(outs)), outs):
+    for by, out in enumerate(outs):
         first = pl.multiple_of(partner(by) * width, width)
         out[...] = pool[0, :, :, :, pl.ds(first, width)]
 
 
 def project_body(
-    sizes, lengths_in, table_in, tokens, w_query, w_keyvalue, queries, keyvalue, bias, residual,
+    sizes, lengths_in, table_in, tokens, w_query, w_keyvalue, queries, keyvalue, bias, far_bias, residual,
     lengths, table, sems,
 ):
     near, tok_count, head_count, shard_blocks, block_len = sizes
@@ -174,7 +186,8 @@
             & (ids <= own_ids)
             & (own_ids - ids < WINDOW)
         )
-        bias[:, distance * rows : (distance + 1) * rows] = jnp.where(allowed, 0.0, -jnp.inf)
+        out, first = (far_bias, (distance - 1) * rows) if distance else (bias, 0)
+        out[:, first : first + rows] = jnp.where(allowed, 0.0, -jnp.inf)
     shard = head_count * shard_blocks * block_len
     prefix_len = tok_count * shard
     slot = lax.broadcasted_iota(i32, (1, shard), 1)
@@ -182,32 +195,63 @@
         places = slot % block_len
         for block in range(head_count * shard_blocks):
             owner = (tok_index ^ far) * head_count + partner(
-                rounds(head_count)[block // shard_blocks]
+                POOL_ORDER[block // shard_blocks]
             )
             logical = table[0, owner * shard_blocks + block % shard_blocks]
             places = places + jnp.where(slot // block_len == block, logical * block_len, 0)
         allowed = (places < SINK) | (places > prefix_len + own_offset - WINDOW)
-        first = near * rows + far * shard
-        bias[:, first : first + shard] = jnp.where(allowed, 0.0, -jnp.inf)
-
-
-def self_body(near, head_count, queries, bias, w_out, *refs):
-    term, refs = refs[-1], refs[:-1]
-    near_refs, refs = refs[:near], refs[near:]
+        out, first = (far_bias, (near - 1) * rows + (far - 1) * shard) if far else (bias, rows)
+        out[:, first : first + shard] = jnp.where(allowed, 0.0, -jnp.inf)
+
+
+def gather_keys(suffix_refs, slot_refs, width):
+    pairs = [split_pair(r[...].reshape(r.shape[0] * r.shape[1], 2, width)) for r in slot_refs]
+    keys = [ref[:, :width] for ref in suffix_refs] + [key for key, _ in pairs]
+    values = [ref[:, width:] for ref in suffix_refs] + [value for _, value in pairs]
+    return jnp.concatenate(keys, axis=0), jnp.concatenate(values, axis=0)
+
+
+def near_body(queries, bias, keyvalue, *refs):
+    *slot_refs, maxima, sums, weighted = refs
+    rows, width = queries.shape
+    keys, values = gather_keys([keyvalue], slot_refs, width)
+    for heads in head_sets(rows, width, keys.shape[0]):
+        scores = head_scores(queries[...], keys, bias[...], heads)
+        row_max = jnp.max(scores, axis=-1, keepdims=True)
+        weights = jnp.exp(scores - row_max)
+        row_sum = jnp.sum(weights, axis=-1, keepdims=True)
+        chosen = slice(heads[0], heads[-1] + 1)
+        shape = (len(heads), rows, LANES)
+        maxima[chosen] = jnp.broadcast_to(row_max, shape)
+        sums[chosen] = jnp.broadcast_to(row_sum, shape)
+        weighted[chosen] = weigh(weights, values)
+
+
+def far_body(behind, head_count, queries, bias, w_out, maxima, sums, weighted, *refs):
+    *refs, term = refs
     slot_refs, outs = refs[:-head_count], refs[-head_count:]
     rows, width = queries.shape
-    keys = [ref[:, :width] for ref in near_refs]
-    values = [ref[:, width:] for ref in near_refs]
-    for ref in slot_refs:
-        key, value = split_pair(ref[...].reshape(ref.shape[0] * ref.shape[1], 2, width))
-        keys.append(key)
-        values.append(value)
-    attended = attend(
-        queries[...], jnp.concatenate(keys, axis=0), jnp.concatenate(values, axis=0), bias[...]
-    )
+    keys, values = gather_keys(slot_refs[:behind], slot_refs[behind:], width)
+
+    def spread(array, size):
+        return jnp.concatenate([array] * (size // LANES), axis=-1)
+
+    attended = 0.0
+    for heads in head_sets(rows, width, keys.shape[0]):
+        chosen = slice(heads[0], heads[-1] + 1)
+        scores = head_scores(queries[...], keys, bias[...], heads)
+        before = maxima[chosen]
+        row_max = jnp.maximum(before, jnp.max(scores, axis=-1, keepdims=True))
+        weights = jnp.exp(scores - spread(row_max, keys.shape[0]))
+        scale = jnp.exp(before - row_max)
+        row_sum = jnp.sum(weights, axis=-1, keepdims=True) + scale * sums[chosen]
+        total = weigh(weights, values) + spread(scale, width) * weighted[chosen]
+        here = own_lanes(jnp.ones_like(total), heads)
+        total, row_sum = own_lanes(total, heads), own_lanes(spread(row_sum, width), heads)
+        attended = attended + total / jnp.where(here > 0, row_sum, 1.0)
     share = rows // head_count
-    term[...] = dot(attended, w_out[...]).astype(bf16)
-    for by, out in zip(rounds(head_count), outs):
+    term[...] = dot(attended.astype(bf16), w_out[...]).astype(bf16)
+    for by, out in enumerate(outs):
         start = pl.multiple_of(partner(by) * share, share)
         out[...] = term[pl.ds(start, share), :]
 
@@ -217,7 +261,7 @@
     normed = jnp.concatenate([ref[...] for ref in rows_in], axis=0)
     queries = dot(normed, w_cross_query[...]).astype(bf16)
     keys, values = split_pair(cross_cache[0])
-    cross_out = attend(queries, keys, values, None)
+    cross_out = attend(queries, keys, values)
     term = dot(cross_out, w_cross_out[...]).astype(bf16)
     share = rows_in[0].shape[0]
     for i, out in enumerate(outs):
@@ -231,6 +275,11 @@
     normed = layer_norm(total).astype(bf16)
     for out in outs:
         out[...] = normed
+
+
+def result_body(before, *refs):
+    *terms, out = refs
+    out[0] = (before[...] + sum(term[...].astype(f32) for term in terms)).astype(bf16)
 
 
 def hidden_body(w_up, w_down, *refs):
@@ -265,7 +314,7 @@
     share = rows // head_count
     shard_blocks, block_len = prefix_pool.shape[1:3]
     near_count = 1 + min(SPAN, tok_count - 1)
-    key_count = near_count * rows + block_position.shape[1] * block_len
+    slot_count = head_count * shard_blocks * block_len
     sizes = (near_count, tok_count, head_count, shard_blocks, block_len)
     shape = jax.ShapeDtypeStruct
     row_pieces = [shape((share, model_width), bf16)] * head_count
@@ -280,13 +329,14 @@
         None,
         prefix_pool,
     )
-    slots = exchange_heads(pool_columns)
-    queries, keyvalue, bias, residual = kernel_call(
+    slots = exchange_heads(pool_columns, POOL_ORDER)
+    queries, keyvalue, bias, far_bias, residual = kernel_call(
         functools.partial(project_body, sizes),
         [
             shape((rows, width), bf16),
             shape((rows, 2 * width), bf16),
-            shape((rows, key_count), f32),
+            shape((rows, rows + slot_count), f32),
+            shape((rows, (near_count - 1) * rows + (tok_count - 1) * slot_count), f32),
             shape((share, model_width), f32),
         ],
         2 * SMALL_VMEM,
@@ -303,34 +353,47 @@
         w_query,
         w_keyvalue,
     )
-    near = [keyvalue] + [
-        from_behind(keyvalue, "tok", distance) for distance in range(1, near_count)
-    ]
-    all_slots = list(slots)
+    behind = [from_behind(keyvalue, "tok", distance) for distance in range(1, near_count)]
+    far_slots = []
     for by in range(1, tok_count):
         for i, piece in enumerate(slots):
-            ready = keyvalue if i < 3 else all_slots[-2]
+            ready = far_slots[-2] if i == len(slots) - 1 else keyvalue
             piece, _ = lax.optimization_barrier((piece, ready))
-            all_slots.append(swap(piece, "tok", by))
-    terms = kernel_call(
-        functools.partial(self_body, near_count, head_count),
-        row_pieces,
-        SMALL_VMEM + 36 * rows * key_count,
-        [pltpu.VMEM((rows, model_width), bf16)],
+            far_slots.append(swap(piece, "tok", by))
+    heads = width // HEAD_DIM
+    partial = kernel_call(
+        near_body,
+        [shape((heads, rows, LANES), f32)] * 2 + [shape((heads, rows, width), f32)],
+        SMALL_VMEM + 36 * bias.size,
+        [],
         [],
         None,
         queries,
         bias,
+        keyvalue,
+        *slots,
+    )
+    terms = kernel_call(
+        functools.partial(far_body, len(behind), head_count),
+        row_pieces,
+        SMALL_VMEM + 36 * far_bias.size,
+        [pltpu.VMEM((rows, model_width), bf16)],
+        [],
+        None,
+        queries,
+        far_bias,
         w_out,
-        *near,
-        *all_slots,
+        *partial,
+        *behind,
+        *far_slots,
     )
     after_self, *normed = kernel_call(
-        functools.partial(after_body, head_count), stats, SMALL_VMEM, [], [], None, residual, *exchange_heads(terms)
-    )
-    arrived = exchange_heads(normed)
+        functools.partial(after_body, head_count), stats, SMALL_VMEM, [], [], None, residual, *exchange_heads(terms, SELF_SUM_ORDER)
+    )
+    arrived = exchange_heads(normed, CROSS_ROWS_ORDER)
     terms = []
     for rows_in in (arrived[: head_count // 2], arrived[head_count // 2 :]):
+        *rows_in, _ = lax.optimization_barrier((*rows_in, terms))
         terms += kernel_call(
             cross_body,
             row_pieces[: len(rows_in)],
@@ -343,12 +406,14 @@
             w_cross_out,
             *rows_in,
         )
+    terms = [terms[CROSS_ROWS_ORDER.index(by)] for by in range(head_count)]
     after_cross, *normed = kernel_call(
-        functools.partial(after_body, head_count), stats, SMALL_VMEM, [], [], None, after_self, *exchange_heads(terms)
-    )
-    arrived = exchange_heads(normed)
+        functools.partial(after_body, head_count), stats, SMALL_VMEM, [], [], None, after_self, *exchange_heads(terms, CROSS_SUM_ORDER)
+    )
+    arrived = exchange_heads(normed, HIDDEN_ROWS_ORDER)
     terms = []
     for rows_in in (arrived[: head_count // 2], arrived[head_count // 2 :]):
+        *rows_in, _ = lax.optimization_barrier((*rows_in, terms))
         terms += kernel_call(
             hidden_body,
             row_pieces[: len(rows_in)],
@@ -360,8 +425,17 @@
             w_down,
             *rows_in,
         )
-    result = after_cross + sum(term.astype(f32) for term in exchange_heads(terms))
-    return result.astype(bf16)[None]
+    terms = [terms[HIDDEN_ROWS_ORDER.index(by)] for by in range(head_count)]
+    return kernel_call(
+        result_body,
+        [shape((1, share, model_width), bf16)],
+        SMALL_VMEM,
+        [],
+        [],
+        None,
+        after_cross,
+        *exchange_heads(terms, HIDDEN_SUM_ORDER),
+    )[0]
 
 
 def solution(mesh):

time: 57.6 us -> 56.4 us (0.979)
  waiting for transfers between devices: 19.5 us -> 17.9 us
  Pallas kernels: 7.37 us -> 8.48 us
  other arithmetic: 0.67 us -> 0 us
    ppermute x22, waiting for transfers between devices: 19.5 us -> 17.9 us  [swap(): return lax.ppermute(array, axis, [(i, i ^ by) for i in range(count)])]
    pallas_call x9 -> x11, Pallas kernels: 7.37 us -> 8.48 us  [kernel_call(): pl.pallas_call(body, out_shape=outs, in_specs=list(specs) + [pl.BlockSpec...]
    broadcast_in_dim x1 -> x0, other arithmetic: 0.67 us -> none  [on_device(): return result.astype(bf16)[None]]
  transfers between devices with their start and end apart: 23 -> 23, of which waited for: 17 -> 13; matrix products, arithmetic and copies ran while one was open for 0% -> 0% of each run, Pallas kernels for 9% -> 11%
where the time goes in v7:
time: 56.4 us; the launch traced here: 56.3 us
  starting transfers between devices  28.6 us (51%)
  waiting for transfers between devices  17.9 us (32%)
  Pallas kernels  8.48 us (15%)
  local copies, waits for them, and re-layouts  1.11 us (2%)
    ppermute x22, starting transfers between devices, swap(): return lax.ppermute(array, axis, [(i, i ^ by) for i in range(count)])  28.1 us
    ppermute x22, waiting for transfers between devices, swap(): return lax.ppermute(array, axis, [(i, i ^ by) for i in range(count)])  17.9 us
    pallas_call x11, Pallas kernels, kernel_call(): pl.pallas_call(body, out_shape=outs, in_specs=list(specs) + [pl.BlockSpec...  8.48 us
  transfers between devices with their start and end apart: 23, of which 13 were waited for; matrix products, arithmetic and copies ran while one was open for 0% of the time, Pallas kernels for 11%

profile of v7, /device:TPU:0, one launch (start us, length us, event | category | flops | bytes accessed | tf_op | source)
XLA Modules:
  0.0 56.3 jit_solution(1855124456787388491)
XLA Ops:
  0.0 1.1 %copy-done.7 = bf16[1,4,16,2,1024]{4,3,2,1,0:T(2,128)(2,1)S(1)} copy-done((bf16[1,4,16,2,1024]{4,3,2,1,0:T(2,128)(2,1)S(1)}, bf16[1,4,16,2,1024]{4,3,2,1,0:T(2,128)(2,1)}, u32[]{:S(2)}) %copy-start.7) | copy-done | bytes 262168
  1.2 5.1 %collective-permute-start = (bf16[4,16,2,256]{3,2,1,0:T(2,128)(2,1)S(1)}, bf16[4,16,2,256]{3,2,1,0:T(2,128)(2,1)S(1)}, u32[]{:S(2)}, u32[]{:S(2)}) collective-permute-start(bf16[4,16,2,256]{3,2,1,0:T(2,128)(2,1)S(1)} %get-tuple-element.57), channel_id=1, source_target_pairs={{0,3},{1,2},{2,1},{3,0},{4,7},{5,6},{6,5},{7,4},{8,11},{9,10},{10,... | collective-permute-start | bytes 196616 | tf_op jit(solution)/shard_map/ppermute | solution.py:36
  7.0 1.2 %shard_map.118 = (bf16[128,256]{1,0:T(8,128)(2,1)S(1)}, bf16[128,512]{1,0:T(8,128)(2,1)S(1)}, f32[128,384]{1,0:T(8,128)S(1)}, f32[128,384]{1,0:T(8,128)S(1)}, f32[32,1024]{1,0:T(8,128)S(1)}) custom-call(s32[1,8]{1,0:T(1,128)S(1)} %copy-done.10, s32[1,32]{1,0:T(1,128)S(1)} %copy-done.11, bf16[1,128,1024]{2,1,0:T(8,128)(2,1)S(1)} %copy-done.8, ...), custom_call_target="tpu_custom_call" | custom-call | flops 4000000000 | bytes 1835168 | tf_op jit(solution)/shard_map/pallas_call | solution.py:53
  8.2 1.0 %collective-permute-done.refs_1_ = bf16[4,16,2,256]{3,2,1,0:T(2,128)(2,1)S(1)} collective-permute-done((bf16[4,16,2,256]{3,2,1,0:T(2,128)(2,1)S(1)}, bf16[4,16,2,256]{3,2,1,0:T(2,128)(2,1)S(1)}, u32[]{:S(2)}, u32[]{:S(2)}) %collective-permute-start) | collective-permute-done | bytes 65568 | tf_op jit(solution)/shard_map/ppermute | solution.py:36
  9.7 1.2 %collective-permute-done.1.refs_2_ = bf16[4,16,2,256]{3,2,1,0:T(2,128)(2,1)S(1)} collective-permute-done((bf16[4,16,2,256]{3,2,1,0:T(2,128)(2,1)S(1)}, bf16[4,16,2,256]{3,2,1,0:T(2,128)(2,1)S(1)}, u32[]{:S(2)}, u32[]{:S(2)}) %collective-permute-start.1) | collective-permute-done | bytes 65568 | tf_op jit(solution)/shard_map/ppermute | solution.py:36
  11.0 1.0 %collective-permute-done.2.refs_3_ = bf16[4,16,2,256]{3,2,1,0:T(2,128)(2,1)S(1)} collective-permute-done((bf16[4,16,2,256]{3,2,1,0:T(2,128)(2,1)S(1)}, bf16[4,16,2,256]{3,2,1,0:T(2,128)(2,1)S(1)}, u32[]{:S(2)}, u32[]{:S(2)}) %collective-permute-start.2) | collective-permute-done | bytes 65568 | tf_op jit(solution)/shard_map/ppermute | solution.py:36
  11.9 0.7 %shard_map.120 = (f32[4,128,128]{2,1,0:T(8,128)S(1)}, f32[4,128,128]{2,1,0:T(8,128)S(1)}, f32[4,128,256]{2,1,0:T(8,128)S(1)}) custom-call(bf16[128,256]{1,0:T(8,128)(2,1)S(1)} %get-tuple-element.52.queries, f32[128,384]{1,0:T(8,128)S(1)} %get-tuple-element.54.bias, bf16[128,512]{1,0:T(8,128)(2,1)S(1)} %get-tuple-element.55.keyvalue, ...), custom_call_target="tpu_custom_call" | custom-call | flops 4000000000 | bytes 655360 | tf_op jit(solution)/shard_map/pallas_call | solution.py:53
  13.2 1.1 %shard_map.121 = (bf16[32,1024]{1,0:T(8,128)(2,1)S(1)}, bf16[32,1024]{1,0:T(8,128)(2,1)S(1)}, bf16[32,1024]{1,0:T(8,128)(2,1)S(1)}, bf16[32,1024]{1,0:T(8,128)(2,1)S(1)}) custom-call(bf16[128,256]{1,0:T(8,128)(2,1)S(1)} %get-tuple-element.52.queries, f32[128,384]{1,0:T(8,128)S(1)} %get-tuple-element.53.bias, bf16[256,1024]{1,0:T(8,128)(2,1)S(1)} %copy-done.4, ...), custom_call_target="tpu_custom_call" | custom-call | flops 4000000000 | bytes 2228224 | tf_op jit(solution)/shard_map/pallas_call | solution.py:53
  14.3 2.0 %collective-permute-start.8 = (bf16[32,1024]{1,0:T(8,128)(2,1)S(1)}, bf16[32,1024]{1,0:T(8,128)(2,1)S(1)}, u32[]{:S(2)}, u32[]{:S(2)}) collective-permute-start(bf16[32,1024]{1,0:T(8,128)(2,1)S(1)} %get-tuple-element.68), channel_id=1, source_target_pairs={{0,2},{1,3},{2,0},{3,1},{4,6},{5,7},{6,4},{7,5},{8,10},{9,11},{10,... | collective-permute-start | bytes 196616 | tf_op jit(solution)/shard_map/ppermute | solution.py:36
  16.3 1.0 %collective-permute-start.9 = (bf16[32,1024]{1,0:T(8,128)(2,1)S(1)}, bf16[32,1024]{1,0:T(8,128)(2,1)S(1)}, u32[]{:S(2)}, u32[]{:S(2)}) collective-permute-start(bf16[32,1024]{1,0:T(8,128)(2,1)S(1)} %get-tuple-element.69), channel_id=1, source_target_pairs={{0,1},{1,0},{2,3},{3,2},{4,5},{5,4},{6,7},{7,6},{8,9},{9,8},{10,11... | collective-permute-start | bytes 196616 | tf_op jit(solution)/shard_map/ppermute | solution.py:36
  17.3 1.4 %collective-permute-start.10 = (bf16[32,1024]{1,0:T(8,128)(2,1)S(1)}, bf16[32,1024]{1,0:T(8,128)(2,1)S(1)}, u32[]{:S(2)}, u32[]{:S(2)}) collective-permute-start(bf16[32,1024]{1,0:T(8,128)(2,1)S(1)} %get-tuple-element.70), channel_id=1, source_target_pairs={{0,3},{1,2},{2,1},{3,0},{4,7},{5,6},{6,5},{7,4},{8,11},{9,10},{10,... | collective-permute-start | bytes 196616 | tf_op jit(solution)/shard_map/ppermute | solution.py:36
  18.7 2.5 %collective-permute-done.8.refs_1_ = bf16[32,1024]{1,0:T(8,128)(2,1)S(1)} collective-permute-done((bf16[32,1024]{1,0:T(8,128)(2,1)S(1)}, bf16[32,1024]{1,0:T(8,128)(2,1)S(1)}, u32[]{:S(2)}, u32[]{:S(2)}) %collective-permute-start.8) | collective-permute-done | bytes 65568 | tf_op jit(solution)/shard_map/ppermute | solution.py:36
  21.2 2.2 %collective-permute-done.10.refs_3_ = bf16[32,1024]{1,0:T(8,128)(2,1)S(1)} collective-permute-done((bf16[32,1024]{1,0:T(8,128)(2,1)S(1)}, bf16[32,1024]{1,0:T(8,128)(2,1)S(1)}, u32[]{:S(2)}, u32[]{:S(2)}) %collective-permute-start.10) | collective-permute-done | bytes 65568 | tf_op jit(solution)/shard_map/ppermute | solution.py:36
  23.7 1.9 %collective-permute-start.11 = (bf16[32,1024]{1,0:T(8,128)(2,1)S(1)}, bf16[32,1024]{1,0:T(8,128)(2,1)S(1)}, u32[]{:S(2)}, u32[]{:S(2)}) collective-permute-start(bf16[32,1024]{1,0:T(8,128)(2,1)S(1)} %get-tuple-element.73), channel_id=1, source_target_pairs={{0,3},{1,2},{2,1},{3,0},{4,7},{5,6},{6,5},{7,4},{8,11},{9,10},{10,... | collective-permute-start | bytes 196616 | tf_op jit(solution)/shard_map/ppermute | solution.py:36
  26.1 2.0 %collective-permute-start.13 = (bf16[32,1024]{1,0:T(8,128)(2,1)S(1)}, bf16[32,1024]{1,0:T(8,128)(2,1)S(1)}, u32[]{:S(2)}, u32[]{:S(2)}) collective-permute-start(bf16[32,1024]{1,0:T(8,128)(2,1)S(1)} %get-tuple-element.78), channel_id=1, source_target_pairs={{0,2},{1,3},{2,0},{3,1},{4,6},{5,7},{6,4},{7,5},{8,10},{9,11},{10,... | collective-permute-start | bytes 196616 | tf_op jit(solution)/shard_map/ppermute | solution.py:36
  28.1 2.2 %collective-permute-done.11.refs_1_ = bf16[32,1024]{1,0:T(8,128)(2,1)S(1)} collective-permute-done((bf16[32,1024]{1,0:T(8,128)(2,1)S(1)}, bf16[32,1024]{1,0:T(8,128)(2,1)S(1)}, u32[]{:S(2)}, u32[]{:S(2)}) %collective-permute-start.11) | collective-permute-done | bytes 65568 | tf_op jit(solution)/shard_map/ppermute | solution.py:36
  30.3 0.8 %shard_map.123 = (bf16[32,1024]{1,0:T(8,128)(2,1)S(1)}, bf16[32,1024]{1,0:T(8,128)(2,1)S(1)}) custom-call(bf16[1024,256]{1,0:T(8,128)(2,1)S(1)} %copy-done.5, bf16[1,256,2,256]{3,2,1,0:T(2,128)(2,1)S(1)} %copy-done.9, bf16[256,1024]{1,0:T(8,128)(2,1)S(1)} %copy-done.6, bf16[32,1024]{1,0:T(8,128)(2,1)S(1)} %get-tuple-element.74.refs_0_, ...), custom_call_target="tpu_custom_call" | custom-call | flops 4000000000 | bytes 1441792 | tf_op jit(solution)/shard_map/pallas_call | solution.py:53
  31.2 2.1 %collective-permute-start.15 = (bf16[32,1024]{1,0:T(8,128)(2,1)S(1)}, bf16[32,1024]{1,0:T(8,128)(2,1)S(1)}, u32[]{:S(2)}, u32[]{:S(2)}) collective-permute-start(bf16[32,1024]{1,0:T(8,128)(2,1)S(1)} %get-tuple-element.79), channel_id=1, source_target_pairs={{0,3},{1,2},{2,1},{3,0},{4,7},{5,6},{6,5},{7,4},{8,11},{9,10},{10,... | collective-permute-start | bytes 196616 | tf_op jit(solution)/shard_map/ppermute | solution.py:36
  33.3 0.8 %shard_map.124 = (bf16[32,1024]{1,0:T(8,128)(2,1)S(1)}, bf16[32,1024]{1,0:T(8,128)(2,1)S(1)}) custom-call(bf16[1024,256]{1,0:T(8,128)(2,1)S(1)} %copy-done.5, bf16[1,256,2,256]{3,2,1,0:T(2,128)(2,1)S(1)} %copy-done.9, bf16[256,1024]{1,0:T(8,128)(2,1)S(1)} %copy-done.6, bf16[32,1024]{1,0:T(8,128)(2,1)S(1)} %collective-permute-done.12.refs_0_, ...), custom_call_target="tpu_custom_call" | custom-call | flops 4000000000 | bytes 1441792 | tf_op jit(solution)/shard_map/pallas_call | solution.py:53
  34.4 2.2 %collective-permute-start.16 = (bf16[32,1024]{1,0:T(8,128)(2,1)S(1)}, bf16[32,1024]{1,0:T(8,128)(2,1)S(1)}, u32[]{:S(2)}, u32[]{:S(2)}) collective-permute-start(bf16[32,1024]{1,0:T(8,128)(2,1)S(1)} %get-tuple-element.83), channel_id=1, source_target_pairs={{0,2},{1,3},{2,0},{3,1},{4,6},{5,7},{6,4},{7,5},{8,10},{9,11},{10,... | collective-permute-start | bytes 196616 | tf_op jit(solution)/shard_map/ppermute | solution.py:36
  36.5 1.9 %collective-permute-done.14.refs_1_ = bf16[32,1024]{1,0:T(8,128)(2,1)S(1)} collective-permute-done((bf16[32,1024]{1,0:T(8,128)(2,1)S(1)}, bf16[32,1024]{1,0:T(8,128)(2,1)S(1)}, u32[]{:S(2)}, u32[]{:S(2)}) %collective-permute-start.14) | collective-permute-done | bytes 65568 | tf_op jit(solution)/shard_map/ppermute | solution.py:36
  38.5 1.1 %collective-permute-done.16.refs_3_ = bf16[32,1024]{1,0:T(8,128)(2,1)S(1)} collective-permute-done((bf16[32,1024]{1,0:T(8,128)(2,1)S(1)}, bf16[32,1024]{1,0:T(8,128)(2,1)S(1)}, u32[]{:S(2)}, u32[]{:S(2)}) %collective-permute-start.16) | collective-permute-done | bytes 65568 | tf_op jit(solution)/shard_map/ppermute | solution.py:36
  39.8 1.7 %collective-permute-start.17 = (bf16[32,1024]{1,0:T(8,128)(2,1)S(1)}, bf16[32,1024]{1,0:T(8,128)(2,1)S(1)}, u32[]{:S(2)}, u32[]{:S(2)}) collective-permute-start(bf16[32,1024]{1,0:T(8,128)(2,1)S(1)} %get-tuple-element.86), channel_id=1, source_target_pairs={{0,3},{1,2},{2,1},{3,0},{4,7},{5,6},{6,5},{7,4},{8,11},{9,10},{10,... | collective-permute-start | bytes 196616 | tf_op jit(solution)/shard_map/ppermute | solution.py:36
  41.5 1.8 %collective-permute-start.19 = (bf16[32,1024]{1,0:T(8,128)(2,1)S(1)}, bf16[32,1024]{1,0:T(8,128)(2,1)S(1)}, u32[]{:S(2)}, u32[]{:S(2)}) collective-permute-start(bf16[32,1024]{1,0:T(8,128)(2,1)S(1)} %get-tuple-element.91), channel_id=1, source_target_pairs={{0,2},{1,3},{2,0},{3,1},{4,6},{5,7},{6,4},{7,5},{8,10},{9,11},{10,... | collective-permute-start | bytes 196616 | tf_op jit(solution)/shard_map/ppermute | solution.py:36
  43.2 1.0 %collective-permute-start.20 = (bf16[32,1024]{1,0:T(8,128)(2,1)S(1)}, bf16[32,1024]{1,0:T(8,128)(2,1)S(1)}, u32[]{:S(2)}, u32[]{:S(2)}) collective-permute-start(bf16[32,1024]{1,0:T(8,128)(2,1)S(1)} %get-tuple-element.92), channel_id=1, source_target_pairs={{0,1},{1,0},{2,3},{3,2},{4,5},{5,4},{6,7},{7,6},{8,9},{9,8},{10,11... | collective-permute-start | bytes 196616 | tf_op jit(solution)/shard_map/ppermute | solution.py:36
  44.2 1.8 %collective-permute-done.17.refs_1_ = bf16[32,1024]{1,0:T(8,128)(2,1)S(1)} collective-permute-done((bf16[32,1024]{1,0:T(8,128)(2,1)S(1)}, bf16[32,1024]{1,0:T(8,128)(2,1)S(1)}, u32[]{:S(2)}, u32[]{:S(2)}) %collective-permute-start.17) | collective-permute-done | bytes 65568 | tf_op jit(solution)/shard_map/ppermute | solution.py:36
  46.0 1.3 %shard_map.126 = (bf16[32,1024]{1,0:T(8,128)(2,1)S(1)}, bf16[32,1024]{1,0:T(8,128)(2,1)S(1)}) custom-call(bf16[1024,2048]{1,0:T(8,128)(2,1)S(1)} %copy-done, bf16[2048,1024]{1,0:T(8,128)(2,1)S(1)} %copy-done.1, bf16[32,1024]{1,0:T(8,128)(2,1)S(1)} %get-tuple-element.87.refs_0_, bf16[32,1024]{1,0:T(8,128)(2,1)S(1)} %collective-permute-done.17.refs_1_), custom_call_target="tpu_custom_call" | custom-call | flops 4000000000 | bytes 8519680 | tf_op jit(solution)/shard_map/pallas_call | solution.py:53
  47.3 1.7 %collective-permute-start.18 = (bf16[32,1024]{1,0:T(8,128)(2,1)S(1)}, bf16[32,1024]{1,0:T(8,128)(2,1)S(1)}, u32[]{:S(2)}, u32[]{:S(2)}) collective-permute-start(bf16[32,1024]{1,0:T(8,128)(2,1)S(1)} %get-tuple-element.90), channel_id=1, source_target_pairs={{0,3},{1,2},{2,1},{3,0},{4,7},{5,6},{6,5},{7,4},{8,11},{9,10},{10,... | collective-permute-start | bytes 196616 | tf_op jit(solution)/shard_map/ppermute | solution.py:36
  49.0 1.3 %shard_map.127 = (bf16[32,1024]{1,0:T(8,128)(2,1)S(1)}, bf16[32,1024]{1,0:T(8,128)(2,1)S(1)}) custom-call(bf16[1024,2048]{1,0:T(8,128)(2,1)S(1)} %copy-done, bf16[2048,1024]{1,0:T(8,128)(2,1)S(1)} %copy-done.1, bf16[32,1024]{1,0:T(8,128)(2,1)S(1)} %collective-permute-done.19.refs_0_, bf16[32,1024]{1,0:T(8,128)(2,1)S(1)} %collective-permute-done.20.refs_1_), custom_call_target="tpu_custom_call" | custom-call | flops 4000000000 | bytes 8519680 | tf_op jit(solution)/shard_map/pallas_call | solution.py:53
  50.4 2.7 %collective-permute-start.22 = (bf16[32,1024]{1,0:T(8,128)(2,1)S(1)}, bf16[32,1024]{1,0:T(8,128)(2,1)S(1)}, u32[]{:S(2)}, u32[]{:S(2)}) collective-permute-start(bf16[32,1024]{1,0:T(8,128)(2,1)S(1)} %get-tuple-element.96), channel_id=1, source_target_pairs={{0,2},{1,3},{2,0},{3,1},{4,6},{5,7},{6,4},{7,5},{8,10},{9,11},{10,... | collective-permute-start | bytes 196616 | tf_op jit(solution)/shard_map/ppermute | solution.py:36
  53.7 0.9 %collective-permute-done.21.refs_2_ = bf16[32,1024]{1,0:T(8,128)(2,1)S(1)} collective-permute-done((bf16[32,1024]{1,0:T(8,128)(2,1)S(1)}, bf16[32,1024]{1,0:T(8,128)(2,1)S(1)}, u32[]{:S(2)}, u32[]{:S(2)}) %collective-permute-start.21) | collective-permute-done | bytes 65568 | tf_op jit(solution)/shard_map/ppermute | solution.py:36
  54.6 1.0 %collective-permute-done.22.refs_3_ = bf16[32,1024]{1,0:T(8,128)(2,1)S(1)} collective-permute-done((bf16[32,1024]{1,0:T(8,128)(2,1)S(1)}, bf16[32,1024]{1,0:T(8,128)(2,1)S(1)}, u32[]{:S(2)}, u32[]{:S(2)}) %collective-permute-start.22) | collective-permute-done | bytes 65568 | tf_op jit(solution)/shard_map/ppermute | solution.py:36
  (49 shorter events, 4.3 us)
Async XLA Ops:
  0.0 6.9 %copy-start.3 = (bf16[1024,256]{1,0:T(8,128)(2,1)S(1)}, bf16[1024,256]{1,0:T(8,128)(2,1)}, u32[]{:S(2)}) copy-start(bf16[1024,256]{1,0:T(8,128)(2,1)} %w_query.1) | copy-start | bytes 1572868
  0.0 6.9 %copy-start.2 = (bf16[1024,2,256]{2,1,0:T(2,128)(2,1)S(1)}, bf16[1024,2,256]{2,1,0:T(2,128)(2,1)}, u32[]{:S(2)}) copy-start(bf16[1024,2,256]{2,1,0:T(2,128)(2,1)} %w_keyvalue.1) | copy-start | bytes 3145732
  1.1 5.9 %copy-start.10 = (s32[1,8]{1,0:T(1,128)S(1)}, s32[1,8]{1,0:T(1,128)}, u32[]{:S(2)}) copy-start(s32[1,8]{1,0:T(1,128)} %lengths_in.1) | copy-start | bytes 100
  1.1 5.9 %copy-start.11 = (s32[1,32]{1,0:T(1,128)S(1)}, s32[1,32]{1,0:T(1,128)}, u32[]{:S(2)}) copy-start(s32[1,32]{1,0:T(1,128)} %table_in.1) | copy-start | bytes 388
  1.2 8.0 %collective-permute-start = (bf16[4,16,2,256]{3,2,1,0:T(2,128)(2,1)S(1)}, bf16[4,16,2,256]{3,2,1,0:T(2,128)(2,1)S(1)}, u32[]{:S(2)}, u32[]{:S(2)}) collective-permute-start(bf16[4,16,2,256]{3,2,1,0:T(2,128)(2,1)S(1)} %get-tuple-element.57), channel_id=1, source_target_pairs={{0,3},{1,2},{2,1},{3,0},{4,7},{5,6},{6,5},{7,4},{8,11},{9,10},{10,... | collective-permute-start | bytes 196616 | tf_op jit(solution)/shard_map/ppermute | solution.py:36
  6.3 4.7 %collective-permute-start.1 = (bf16[4,16,2,256]{3,2,1,0:T(2,128)(2,1)S(1)}, bf16[4,16,2,256]{3,2,1,0:T(2,128)(2,1)S(1)}, u32[]{:S(2)}, u32[]{:S(2)}) collective-permute-start(bf16[4,16,2,256]{3,2,1,0:T(2,128)(2,1)S(1)} %get-tuple-element.58), channel_id=1, source_target_pairs={{0,1},{1,0},{2,3},{3,2},{4,5},{5,4},{6,7},{7,6},{8,9},{9,8},{10,11... | collective-permute-start | bytes 196616 | tf_op jit(solution)/shard_map/ppermute | solution.py:36
  6.3 5.6 %collective-permute-start.2 = (bf16[4,16,2,256]{3,2,1,0:T(2,128)(2,1)S(1)}, bf16[4,16,2,256]{3,2,1,0:T(2,128)(2,1)S(1)}, u32[]{:S(2)}, u32[]{:S(2)}) collective-permute-start(bf16[4,16,2,256]{3,2,1,0:T(2,128)(2,1)S(1)} %get-tuple-element.59), channel_id=1, source_target_pairs={{0,2},{1,3},{2,0},{3,1},{4,6},{5,7},{6,4},{7,5},{8,10},{9,11},{10,... | collective-permute-start | bytes 196616 | tf_op jit(solution)/shard_map/ppermute | solution.py:36
  9.2 2.7 %collective-permute-start.5 = (bf16[4,16,2,256]{3,2,1,0:T(2,128)(2,1)S(1)}, bf16[4,16,2,256]{3,2,1,0:T(2,128)(2,1)S(1)}, u32[]{:S(2)}, u32[]{:S(2)}) collective-permute-start(bf16[4,16,2,256]{3,2,1,0:T(2,128)(2,1)S(1)} %collective-permute-done.refs_1_), channel_id=1, source_target_pairs={{0,4},{4,0},{1,5},{5,1},{2,6},{6,2},{3,7},{7,3},{8,12},{12,8},{9,1... | collective-permute-start | bytes 196616 | tf_op jit(solution)/shard_map/ppermute | solution.py:36
  9.2 3.5 %collective-permute-start.3 = (bf16[128,512]{1,0:T(8,128)(2,1)S(1)}, bf16[128,512]{1,0:T(8,128)(2,1)S(1)}, u32[]{:S(2)}, u32[]{:S(2)}) collective-permute-start(bf16[128,512]{1,0:T(8,128)(2,1)S(1)} %get-tuple-element.55.keyvalue), channel_id=1, source_target_pairs={{0,4},{4,0},{1,5},{5,1},{2,6},{6,2},{3,7},{7,3},{8,12},{12,8},{9,1... | collective-permute-start | bytes 393224 | tf_op jit(solution)/shard_map/ppermute | solution.py:41
  9.7 3.0 %collective-permute-start.4 = (bf16[4,16,2,256]{3,2,1,0:T(2,128)(2,1)S(1)}, bf16[4,16,2,256]{3,2,1,0:T(2,128)(2,1)S(1)}, u32[]{:S(2)}, u32[]{:S(2)}) collective-permute-start(bf16[4,16,2,256]{3,2,1,0:T(2,128)(2,1)S(1)} %get-tuple-element.63.refs_0_), channel_id=1, source_target_pairs={{0,4},{4,0},{1,5},{5,1},{2,6},{6,2},{3,7},{7,3},{8,12},{12,8},{9,1... | collective-permute-start | bytes 196616 | tf_op jit(solution)/shard_map/ppermute | solution.py:36
  11.0 1.8 %collective-permute-start.6 = (bf16[4,16,2,256]{3,2,1,0:T(2,128)(2,1)S(1)}, bf16[4,16,2,256]{3,2,1,0:T(2,128)(2,1)S(1)}, u32[]{:S(2)}, u32[]{:S(2)}) collective-permute-start(bf16[4,16,2,256]{3,2,1,0:T(2,128)(2,1)S(1)} %collective-permute-done.1.refs_2_), channel_id=1, source_target_pairs={{0,4},{4,0},{1,5},{5,1},{2,6},{6,2},{3,7},{7,3},{8,12},{12,8},{9,1... | collective-permute-start | bytes 196616 | tf_op jit(solution)/shard_map/ppermute | solution.py:36
  11.9 1.3 %collective-permute-start.7 = (bf16[4,16,2,256]{3,2,1,0:T(2,128)(2,1)S(1)}, bf16[4,16,2,256]{3,2,1,0:T(2,128)(2,1)S(1)}, u32[]{:S(2)}, u32[]{:S(2)}) collective-permute-start(bf16[4,16,2,256]{3,2,1,0:T(2,128)(2,1)S(1)} %collective-permute-done.2.refs_3_), channel_id=1, source_target_pairs={{0,4},{4,0},{1,5},{5,1},{2,6},{6,2},{3,7},{7,3},{8,12},{12,8},{9,1... | collective-permute-start | bytes 196616 | tf_op jit(solution)/shard_map/ppermute | solution.py:36
  14.3 6.9 %collective-permute-start.8 = (bf16[32,1024]{1,0:T(8,128)(2,1)S(1)}, bf16[32,1024]{1,0:T(8,128)(2,1)S(1)}, u32[]{:S(2)}, u32[]{:S(2)}) collective-permute-start(bf16[32,1024]{1,0:T(8,128)(2,1)S(1)} %get-tuple-element.68), channel_id=1, source_target_pairs={{0,2},{1,3},{2,0},{3,1},{4,6},{5,7},{6,4},{7,5},{8,10},{9,11},{10,... | collective-permute-start | bytes 196616 | tf_op jit(solution)/shard_map/ppermute | solution.py:36
  16.3 4.9 %collective-permute-start.9 = (bf16[32,1024]{1,0:T(8,128)(2,1)S(1)}, bf16[32,1024]{1,0:T(8,128)(2,1)S(1)}, u32[]{:S(2)}, u32[]{:S(2)}) collective-permute-start(bf16[32,1024]{1,0:T(8,128)(2,1)S(1)} %get-tuple-element.69), channel_id=1, source_target_pairs={{0,1},{1,0},{2,3},{3,2},{4,5},{5,4},{6,7},{7,6},{8,9},{9,8},{10,11... | collective-permute-start | bytes 196616 | tf_op jit(solution)/shard_map/ppermute | solution.py:36
  17.3 6.1 %collective-permute-start.10 = (bf16[32,1024]{1,0:T(8,128)(2,1)S(1)}, bf16[32,1024]{1,0:T(8,128)(2,1)S(1)}, u32[]{:S(2)}, u32[]{:S(2)}) collective-permute-start(bf16[32,1024]{1,0:T(8,128)(2,1)S(1)} %get-tuple-element.70), channel_id=1, source_target_pairs={{0,3},{1,2},{2,1},{3,0},{4,7},{5,6},{6,5},{7,4},{8,11},{9,10},{10,... | collective-permute-start | bytes 196616 | tf_op jit(solution)/shard_map/ppermute | solution.py:36
  23.4 6.9 %copy-start.5 = (bf16[1024,256]{1,0:T(8,128)(2,1)S(1)}, bf16[1024,256]{1,0:T(8,128)(2,1)}, u32[]{:S(2)}) copy-start(bf16[1024,256]{1,0:T(8,128)(2,1)} %w_cross_query.3) | copy-start | bytes 1572868
  23.4 6.9 %copy-start.6 = (bf16[256,1024]{1,0:T(8,128)(2,1)S(1)}, bf16[256,1024]{1,0:T(8,128)(2,1)}, u32[]{:S(2)}) copy-start(bf16[256,1024]{1,0:T(8,128)(2,1)} %w_cross_out.3) | copy-start | bytes 1572868
  23.4 6.9 %copy-start.9 = (bf16[1,256,2,256]{3,2,1,0:T(2,128)(2,1)S(1)}, bf16[1,256,2,256]{3,2,1,0:T(2,128)(2,1)}, u32[]{:S(2)}) copy-start(bf16[1,256,2,256]{3,2,1,0:T(2,128)(2,1)} %cross_cache.3) | copy-start | bytes 786436
  23.7 6.6 %collective-permute-start.11 = (bf16[32,1024]{1,0:T(8,128)(2,1)S(1)}, bf16[32,1024]{1,0:T(8,128)(2,1)S(1)}, u32[]{:S(2)}, u32[]{:S(2)}) collective-permute-start(bf16[32,1024]{1,0:T(8,128)(2,1)S(1)} %get-tuple-element.73), channel_id=1, source_target_pairs={{0,3},{1,2},{2,1},{3,0},{4,7},{5,6},{6,5},{7,4},{8,11},{9,10},{10,... | collective-permute-start | bytes 196616 | tf_op jit(solution)/shard_map/ppermute | solution.py:36
  25.6 7.7 %collective-permute-start.12 = (bf16[32,1024]{1,0:T(8,128)(2,1)S(1)}, bf16[32,1024]{1,0:T(8,128)(2,1)S(1)}, u32[]{:S(2)}, u32[]{:S(2)}) collective-permute-start(bf16[32,1024]{1,0:T(8,128)(2,1)S(1)} %get-tuple-element.77), channel_id=1, source_target_pairs={{0,1},{1,0},{2,3},{3,2},{4,5},{5,4},{6,7},{7,6},{8,9},{9,8},{10,11... | collective-permute-start | bytes 196616 | tf_op jit(solution)/shard_map/ppermute | solution.py:36
  26.1 7.2 %collective-permute-start.13 = (bf16[32,1024]{1,0:T(8,128)(2,1)S(1)}, bf16[32,1024]{1,0:T(8,128)(2,1)S(1)}, u32[]{:S(2)}, u32[]{:S(2)}) collective-permute-start(bf16[32,1024]{1,0:T(8,128)(2,1)S(1)} %get-tuple-element.78), channel_id=1, source_target_pairs={{0,2},{1,3},{2,0},{3,1},{4,6},{5,7},{6,4},{7,5},{8,10},{9,11},{10,... | collective-permute-start | bytes 196616 | tf_op jit(solution)/shard_map/ppermute | solution.py:36
  31.2 7.3 %collective-permute-start.15 = (bf16[32,1024]{1,0:T(8,128)(2,1)S(1)}, bf16[32,1024]{1,0:T(8,128)(2,1)S(1)}, u32[]{:S(2)}, u32[]{:S(2)}) collective-permute-start(bf16[32,1024]{1,0:T(8,128)(2,1)S(1)} %get-tuple-element.79), channel_id=1, source_target_pairs={{0,3},{1,2},{2,1},{3,0},{4,7},{5,6},{6,5},{7,4},{8,11},{9,10},{10,... | collective-permute-start | bytes 196616 | tf_op jit(solution)/shard_map/ppermute | solution.py:36
  34.1 4.3 %collective-permute-start.14 = (bf16[32,1024]{1,0:T(8,128)(2,1)S(1)}, bf16[32,1024]{1,0:T(8,128)(2,1)S(1)}, u32[]{:S(2)}, u32[]{:S(2)}) collective-permute-start(bf16[32,1024]{1,0:T(8,128)(2,1)S(1)} %get-tuple-element.82), channel_id=1, source_target_pairs={{0,1},{1,0},{2,3},{3,2},{4,5},{5,4},{6,7},{7,6},{8,9},{9,8},{10,11... | collective-permute-start | bytes 196616 | tf_op jit(solution)/shard_map/ppermute | solution.py:36
  34.4 5.2 %collective-permute-start.16 = (bf16[32,1024]{1,0:T(8,128)(2,1)S(1)}, bf16[32,1024]{1,0:T(8,128)(2,1)S(1)}, u32[]{:S(2)}, u32[]{:S(2)}) collective-permute-start(bf16[32,1024]{1,0:T(8,128)(2,1)S(1)} %get-tuple-element.83), channel_id=1, source_target_pairs={{0,2},{1,3},{2,0},{3,1},{4,6},{5,7},{6,4},{7,5},{8,10},{9,11},{10,... | collective-permute-start | bytes 196616 | tf_op jit(solution)/shard_map/ppermute | solution.py:36
  39.5 6.5 %copy-start = (bf16[1024,2048]{1,0:T(8,128)(2,1)S(1)}, bf16[1024,2048]{1,0:T(8,128)(2,1)}, u32[]{:S(2)}) copy-start(bf16[1024,2048]{1,0:T(8,128)(2,1)} %w_up.3) | copy-start | bytes 12582916
  39.5 6.5 %copy-start.1 = (bf16[2048,1024]{1,0:T(8,128)(2,1)S(1)}, bf16[2048,1024]{1,0:T(8,128)(2,1)}, u32[]{:S(2)}) copy-start(bf16[2048,1024]{1,0:T(8,128)(2,1)} %w_down.3) | copy-start | bytes 12582916
  39.8 6.2 %collective-permute-start.17 = (bf16[32,1024]{1,0:T(8,128)(2,1)S(1)}, bf16[32,1024]{1,0:T(8,128)(2,1)S(1)}, u32[]{:S(2)}, u32[]{:S(2)}) collective-permute-start(bf16[32,1024]{1,0:T(8,128)(2,1)S(1)} %get-tuple-element.86), channel_id=1, source_target_pairs={{0,3},{1,2},{2,1},{3,0},{4,7},{5,6},{6,5},{7,4},{8,11},{9,10},{10,... | collective-permute-start | bytes 196616 | tf_op jit(solution)/shard_map/ppermute | solution.py:36
  41.5 7.5 %collective-permute-start.19 = (bf16[32,1024]{1,0:T(8,128)(2,1)S(1)}, bf16[32,1024]{1,0:T(8,128)(2,1)S(1)}, u32[]{:S(2)}, u32[]{:S(2)}) collective-permute-start(bf16[32,1024]{1,0:T(8,128)(2,1)S(1)} %get-tuple-element.91), channel_id=1, source_target_pairs={{0,2},{1,3},{2,0},{3,1},{4,6},{5,7},{6,4},{7,5},{8,10},{9,11},{10,... | collective-permute-start | bytes 196616 | tf_op jit(solution)/shard_map/ppermute | solution.py:36
  43.2 5.8 %collective-permute-start.20 = (bf16[32,1024]{1,0:T(8,128)(2,1)S(1)}, bf16[32,1024]{1,0:T(8,128)(2,1)S(1)}, u32[]{:S(2)}, u32[]{:S(2)}) collective-permute-start(bf16[32,1024]{1,0:T(8,128)(2,1)S(1)} %get-tuple-element.92), channel_id=1, source_target_pairs={{0,1},{1,0},{2,3},{3,2},{4,5},{5,4},{6,7},{7,6},{8,9},{9,8},{10,11... | collective-permute-start | bytes 196616 | tf_op jit(solution)/shard_map/ppermute | solution.py:36
  47.3 6.4 %collective-permute-start.18 = (bf16[32,1024]{1,0:T(8,128)(2,1)S(1)}, bf16[32,1024]{1,0:T(8,128)(2,1)S(1)}, u32[]{:S(2)}, u32[]{:S(2)}) collective-permute-start(bf16[32,1024]{1,0:T(8,128)(2,1)S(1)} %get-tuple-element.90), channel_id=1, source_target_pairs={{0,3},{1,2},{2,1},{3,0},{4,7},{5,6},{6,5},{7,4},{8,11},{9,10},{10,... | collective-permute-start | bytes 196616 | tf_op jit(solution)/shard_map/ppermute | solution.py:36
  50.3 4.3 %collective-permute-start.21 = (bf16[32,1024]{1,0:T(8,128)(2,1)S(1)}, bf16[32,1024]{1,0:T(8,128)(2,1)S(1)}, u32[]{:S(2)}, u32[]{:S(2)}) collective-permute-start(bf16[32,1024]{1,0:T(8,128)(2,1)S(1)} %get-tuple-element.95), channel_id=1, source_target_pairs={{0,1},{1,0},{2,3},{3,2},{4,5},{5,4},{6,7},{7,6},{8,9},{9,8},{10,11... | collective-permute-start | bytes 196616 | tf_op jit(solution)/shard_map/ppermute | solution.py:36
  50.4 5.2 %collective-permute-start.22 = (bf16[32,1024]{1,0:T(8,128)(2,1)S(1)}, bf16[32,1024]{1,0:T(8,128)(2,1)S(1)}, u32[]{:S(2)}, u32[]{:S(2)}) collective-permute-start(bf16[32,1024]{1,0:T(8,128)(2,1)S(1)} %get-tuple-element.96), channel_id=1, source_target_pairs={{0,2},{1,3},{2,0},{3,1},{4,6},{5,7},{6,4},{7,5},{8,10},{9,11},{10,... | collective-permute-start | bytes 196616 | tf_op jit(solution)/shard_map/ppermute | solution.py:36
  (3 other events, 8.2 us)

commit v8 on v7

--- a/solution.py
+++ b/solution.py
@@ -330,6 +330,7 @@
         prefix_pool,
     )
     slots = exchange_heads(pool_columns, POOL_ORDER)
+    w_keyvalue, w_query, _ = lax.optimization_barrier((w_keyvalue, w_query, pool_columns[0]))
     queries, keyvalue, bias, far_bias, residual = kernel_call(
         functools.partial(project_body, sizes),
         [

time: 56.4 us -> 56.4 us (level)
  no operation moved by 1% of the time
where the time goes in v8:
time: 56.4 us; the launch traced here: 56.3 us
  starting transfers between devices  28.6 us (51%)
  waiting for transfers between devices  17.9 us (32%)
  Pallas kernels  8.48 us (15%)
  local copies, waits for them, and re-layouts  1.11 us (2%)
    ppermute x22, starting transfers between devices, swap(): return lax.ppermute(array, axis, [(i, i ^ by) for i in range(count)])  28.1 us
    ppermute x22, waiting for transfers between devices, swap(): return lax.ppermute(array, axis, [(i, i ^ by) for i in range(count)])  17.9 us
    pallas_call x11, Pallas kernels, kernel_call(): pl.pallas_call(body, out_shape=outs, in_specs=list(specs) + [pl.BlockSpec...  8.48 us
  transfers between devices with their start and end apart: 23, of which 13 were waited for; matrix products, arithmetic and copies ran while one was open for 0% of the time, Pallas kernels for 11%

profile of v8, /device:TPU:0, one launch (start us, length us, event | category | flops | bytes accessed | tf_op | source)
XLA Modules:
  0.0 56.3 jit_solution(15185111797332203922)
XLA Ops:
  0.0 1.1 %copy-done.7 = bf16[1,4,16,2,1024]{4,3,2,1,0:T(2,128)(2,1)S(1)} copy-done((bf16[1,4,16,2,1024]{4,3,2,1,0:T(2,128)(2,1)S(1)}, bf16[1,4,16,2,1024]{4,3,2,1,0:T(2,128)(2,1)}, u32[]{:S(2)}) %copy-start.7) | copy-done | bytes 262168
  1.2 5.1 %collective-permute-start = (bf16[4,16,2,256]{3,2,1,0:T(2,128)(2,1)S(1)}, bf16[4,16,2,256]{3,2,1,0:T(2,128)(2,1)S(1)}, u32[]{:S(2)}, u32[]{:S(2)}) collective-permute-start(bf16[4,16,2,256]{3,2,1,0:T(2,128)(2,1)S(1)} %get-tuple-element.61), channel_id=1, source_target_pairs={{0,3},{1,2},{2,1},{3,0},{4,7},{5,6},{6,5},{7,4},{8,11},{9,10},{10,... | collective-permute-start | bytes 196616 | tf_op jit(solution)/shard_map/ppermute | solution.py:36
  7.0 1.2 %shard_map.119 = (bf16[128,256]{1,0:T(8,128)(2,1)S(1)}, bf16[128,512]{1,0:T(8,128)(2,1)S(1)}, f32[128,384]{1,0:T(8,128)S(1)}, f32[128,384]{1,0:T(8,128)S(1)}, f32[32,1024]{1,0:T(8,128)S(1)}) custom-call(s32[1,8]{1,0:T(1,128)S(1)} %copy-done.10, s32[1,32]{1,0:T(1,128)S(1)} %copy-done.11, bf16[1,128,1024]{2,1,0:T(8,128)(2,1)S(1)} %copy-done.8, ...), custom_call_target="tpu_custom_call" | custom-call | flops 4000000000 | bytes 1835168 | tf_op jit(solution)/shard_map/pallas_call | solution.py:53
  8.2 1.0 %collective-permute-done.refs_1_ = bf16[4,16,2,256]{3,2,1,0:T(2,128)(2,1)S(1)} collective-permute-done((bf16[4,16,2,256]{3,2,1,0:T(2,128)(2,1)S(1)}, bf16[4,16,2,256]{3,2,1,0:T(2,128)(2,1)S(1)}, u32[]{:S(2)}, u32[]{:S(2)}) %collective-permute-start) | collective-permute-done | bytes 65568 | tf_op jit(solution)/shard_map/ppermute | solution.py:36
  9.7 1.2 %collective-permute-done.1.refs_2_ = bf16[4,16,2,256]{3,2,1,0:T(2,128)(2,1)S(1)} collective-permute-done((bf16[4,16,2,256]{3,2,1,0:T(2,128)(2,1)S(1)}, bf16[4,16,2,256]{3,2,1,0:T(2,128)(2,1)S(1)}, u32[]{:S(2)}, u32[]{:S(2)}) %collective-permute-start.1) | collective-permute-done | bytes 65568 | tf_op jit(solution)/shard_map/ppermute | solution.py:36
  11.0 1.0 %collective-permute-done.2.refs_3_ = bf16[4,16,2,256]{3,2,1,0:T(2,128)(2,1)S(1)} collective-permute-done((bf16[4,16,2,256]{3,2,1,0:T(2,128)(2,1)S(1)}, bf16[4,16,2,256]{3,2,1,0:T(2,128)(2,1)S(1)}, u32[]{:S(2)}, u32[]{:S(2)}) %collective-permute-start.2) | collective-permute-done | bytes 65568 | tf_op jit(solution)/shard_map/ppermute | solution.py:36
  11.9 0.7 %shard_map.120 = (f32[4,128,128]{2,1,0:T(8,128)S(1)}, f32[4,128,128]{2,1,0:T(8,128)S(1)}, f32[4,128,256]{2,1,0:T(8,128)S(1)}) custom-call(bf16[128,256]{1,0:T(8,128)(2,1)S(1)} %get-tuple-element.57.queries, f32[128,384]{1,0:T(8,128)S(1)} %get-tuple-element.59.bias, bf16[128,512]{1,0:T(8,128)(2,1)S(1)} %get-tuple-element.60.keyvalue, ...), custom_call_target="tpu_custom_call" | custom-call | flops 4000000000 | bytes 655360 | tf_op jit(solution)/shard_map/pallas_call | solution.py:53
  13.2 1.1 %shard_map.121 = (bf16[32,1024]{1,0:T(8,128)(2,1)S(1)}, bf16[32,1024]{1,0:T(8,128)(2,1)S(1)}, bf16[32,1024]{1,0:T(8,128)(2,1)S(1)}, bf16[32,1024]{1,0:T(8,128)(2,1)S(1)}) custom-call(bf16[128,256]{1,0:T(8,128)(2,1)S(1)} %get-tuple-element.57.queries, f32[128,384]{1,0:T(8,128)S(1)} %get-tuple-element.58.bias, bf16[256,1024]{1,0:T(8,128)(2,1)S(1)} %copy-done.4, ...), custom_call_target="tpu_custom_call" | custom-call | flops 4000000000 | bytes 2228224 | tf_op jit(solution)/shard_map/pallas_call | solution.py:53
  14.3 2.0 %collective-permute-start.8 = (bf16[32,1024]{1,0:T(8,128)(2,1)S(1)}, bf16[32,1024]{1,0:T(8,128)(2,1)S(1)}, u32[]{:S(2)}, u32[]{:S(2)}) collective-permute-start(bf16[32,1024]{1,0:T(8,128)(2,1)S(1)} %get-tuple-element.72), channel_id=1, source_target_pairs={{0,2},{1,3},{2,0},{3,1},{4,6},{5,7},{6,4},{7,5},{8,10},{9,11},{10,... | collective-permute-start | bytes 196616 | tf_op jit(solution)/shard_map/ppermute | solution.py:36
  16.3 1.0 %collective-permute-start.9 = (bf16[32,1024]{1,0:T(8,128)(2,1)S(1)}, bf16[32,1024]{1,0:T(8,128)(2,1)S(1)}, u32[]{:S(2)}, u32[]{:S(2)}) collective-permute-start(bf16[32,1024]{1,0:T(8,128)(2,1)S(1)} %get-tuple-element.73), channel_id=1, source_target_pairs={{0,1},{1,0},{2,3},{3,2},{4,5},{5,4},{6,7},{7,6},{8,9},{9,8},{10,11... | collective-permute-start | bytes 196616 | tf_op jit(solution)/shard_map/ppermute | solution.py:36
  17.3 1.4 %collective-permute-start.10 = (bf16[32,1024]{1,0:T(8,128)(2,1)S(1)}, bf16[32,1024]{1,0:T(8,128)(2,1)S(1)}, u32[]{:S(2)}, u32[]{:S(2)}) collective-permute-start(bf16[32,1024]{1,0:T(8,128)(2,1)S(1)} %get-tuple-element.74), channel_id=1, source_target_pairs={{0,3},{1,2},{2,1},{3,0},{4,7},{5,6},{6,5},{7,4},{8,11},{9,10},{10,... | collective-permute-start | bytes 196616 | tf_op jit(solution)/shard_map/ppermute | solution.py:36
  18.7 2.5 %collective-permute-done.8.refs_1_ = bf16[32,1024]{1,0:T(8,128)(2,1)S(1)} collective-permute-done((bf16[32,1024]{1,0:T(8,128)(2,1)S(1)}, bf16[32,1024]{1,0:T(8,128)(2,1)S(1)}, u32[]{:S(2)}, u32[]{:S(2)}) %collective-permute-start.8) | collective-permute-done | bytes 65568 | tf_op jit(solution)/shard_map/ppermute | solution.py:36
  21.2 2.2 %collective-permute-done.10.refs_3_ = bf16[32,1024]{1,0:T(8,128)(2,1)S(1)} collective-permute-done((bf16[32,1024]{1,0:T(8,128)(2,1)S(1)}, bf16[32,1024]{1,0:T(8,128)(2,1)S(1)}, u32[]{:S(2)}, u32[]{:S(2)}) %collective-permute-start.10) | collective-permute-done | bytes 65568 | tf_op jit(solution)/shard_map/ppermute | solution.py:36
  23.7 1.9 %collective-permute-start.11 = (bf16[32,1024]{1,0:T(8,128)(2,1)S(1)}, bf16[32,1024]{1,0:T(8,128)(2,1)S(1)}, u32[]{:S(2)}, u32[]{:S(2)}) collective-permute-start(bf16[32,1024]{1,0:T(8,128)(2,1)S(1)} %get-tuple-element.77), channel_id=1, source_target_pairs={{0,3},{1,2},{2,1},{3,0},{4,7},{5,6},{6,5},{7,4},{8,11},{9,10},{10,... | collective-permute-start | bytes 196616 | tf_op jit(solution)/shard_map/ppermute | solution.py:36
  26.1 2.0 %collective-permute-start.13 = (bf16[32,1024]{1,0:T(8,128)(2,1)S(1)}, bf16[32,1024]{1,0:T(8,128)(2,1)S(1)}, u32[]{:S(2)}, u32[]{:S(2)}) collective-permute-start(bf16[32,1024]{1,0:T(8,128)(2,1)S(1)} %get-tuple-element.82), channel_id=1, source_target_pairs={{0,2},{1,3},{2,0},{3,1},{4,6},{5,7},{6,4},{7,5},{8,10},{9,11},{10,... | collective-permute-start | bytes 196616 | tf_op jit(solution)/shard_map/ppermute | solution.py:36
  28.1 2.2 %collective-permute-done.11.refs_1_ = bf16[32,1024]{1,0:T(8,128)(2,1)S(1)} collective-permute-done((bf16[32,1024]{1,0:T(8,128)(2,1)S(1)}, bf16[32,1024]{1,0:T(8,128)(2,1)S(1)}, u32[]{:S(2)}, u32[]{:S(2)}) %collective-permute-start.11) | collective-permute-done | bytes 65568 | tf_op jit(solution)/shard_map/ppermute | solution.py:36
  30.3 0.8 %shard_map.123 = (bf16[32,1024]{1,0:T(8,128)(2,1)S(1)}, bf16[32,1024]{1,0:T(8,128)(2,1)S(1)}) custom-call(bf16[1024,256]{1,0:T(8,128)(2,1)S(1)} %copy-done.5, bf16[1,256,2,256]{3,2,1,0:T(2,128)(2,1)S(1)} %copy-done.9, bf16[256,1024]{1,0:T(8,128)(2,1)S(1)} %copy-done.6, bf16[32,1024]{1,0:T(8,128)(2,1)S(1)} %get-tuple-element.78.refs_0_, ...), custom_call_target="tpu_custom_call" | custom-call | flops 4000000000 | bytes 1441792 | tf_op jit(solution)/shard_map/pallas_call | solution.py:53
  31.2 2.1 %collective-permute-start.15 = (bf16[32,1024]{1,0:T(8,128)(2,1)S(1)}, bf16[32,1024]{1,0:T(8,128)(2,1)S(1)}, u32[]{:S(2)}, u32[]{:S(2)}) collective-permute-start(bf16[32,1024]{1,0:T(8,128)(2,1)S(1)} %get-tuple-element.83), channel_id=1, source_target_pairs={{0,3},{1,2},{2,1},{3,0},{4,7},{5,6},{6,5},{7,4},{8,11},{9,10},{10,... | collective-permute-start | bytes 196616 | tf_op jit(solution)/shard_map/ppermute | solution.py:36
  33.3 0.8 %shard_map.124 = (bf16[32,1024]{1,0:T(8,128)(2,1)S(1)}, bf16[32,1024]{1,0:T(8,128)(2,1)S(1)}) custom-call(bf16[1024,256]{1,0:T(8,128)(2,1)S(1)} %copy-done.5, bf16[1,256,2,256]{3,2,1,0:T(2,128)(2,1)S(1)} %copy-done.9, bf16[256,1024]{1,0:T(8,128)(2,1)S(1)} %copy-done.6, bf16[32,1024]{1,0:T(8,128)(2,1)S(1)} %collective-permute-done.12.refs_0_, ...), custom_call_target="tpu_custom_call" | custom-call | flops 4000000000 | bytes 1441792 | tf_op jit(solution)/shard_map/pallas_call | solution.py:53
  34.4 2.2 %collective-permute-start.16 = (bf16[32,1024]{1,0:T(8,128)(2,1)S(1)}, bf16[32,1024]{1,0:T(8,128)(2,1)S(1)}, u32[]{:S(2)}, u32[]{:S(2)}) collective-permute-start(bf16[32,1024]{1,0:T(8,128)(2,1)S(1)} %get-tuple-element.87), channel_id=1, source_target_pairs={{0,2},{1,3},{2,0},{3,1},{4,6},{5,7},{6,4},{7,5},{8,10},{9,11},{10,... | collective-permute-start | bytes 196616 | tf_op jit(solution)/shard_map/ppermute | solution.py:36
  36.5 1.9 %collective-permute-done.14.refs_1_ = bf16[32,1024]{1,0:T(8,128)(2,1)S(1)} collective-permute-done((bf16[32,1024]{1,0:T(8,128)(2,1)S(1)}, bf16[32,1024]{1,0:T(8,128)(2,1)S(1)}, u32[]{:S(2)}, u32[]{:S(2)}) %collective-permute-start.14) | collective-permute-done | bytes 65568 | tf_op jit(solution)/shard_map/ppermute | solution.py:36
  38.5 1.1 %collective-permute-done.16.refs_3_ = bf16[32,1024]{1,0:T(8,128)(2,1)S(1)} collective-permute-done((bf16[32,1024]{1,0:T(8,128)(2,1)S(1)}, bf16[32,1024]{1,0:T(8,128)(2,1)S(1)}, u32[]{:S(2)}, u32[]{:S(2)}) %collective-permute-start.16) | collective-permute-done | bytes 65568 | tf_op jit(solution)/shard_map/ppermute | solution.py:36
  39.8 1.7 %collective-permute-start.17 = (bf16[32,1024]{1,0:T(8,128)(2,1)S(1)}, bf16[32,1024]{1,0:T(8,128)(2,1)S(1)}, u32[]{:S(2)}, u32[]{:S(2)}) collective-permute-start(bf16[32,1024]{1,0:T(8,128)(2,1)S(1)} %get-tuple-element.90), channel_id=1, source_target_pairs={{0,3},{1,2},{2,1},{3,0},{4,7},{5,6},{6,5},{7,4},{8,11},{9,10},{10,... | collective-permute-start | bytes 196616 | tf_op jit(solution)/shard_map/ppermute | solution.py:36
  41.5 1.8 %collective-permute-start.19 = (bf16[32,1024]{1,0:T(8,128)(2,1)S(1)}, bf16[32,1024]{1,0:T(8,128)(2,1)S(1)}, u32[]{:S(2)}, u32[]{:S(2)}) collective-permute-start(bf16[32,1024]{1,0:T(8,128)(2,1)S(1)} %get-tuple-element.95), channel_id=1, source_target_pairs={{0,2},{1,3},{2,0},{3,1},{4,6},{5,7},{6,4},{7,5},{8,10},{9,11},{10,... | collective-permute-start | bytes 196616 | tf_op jit(solution)/shard_map/ppermute | solution.py:36
  43.2 1.0 %collective-permute-start.20 = (bf16[32,1024]{1,0:T(8,128)(2,1)S(1)}, bf16[32,1024]{1,0:T(8,128)(2,1)S(1)}, u32[]{:S(2)}, u32[]{:S(2)}) collective-permute-start(bf16[32,1024]{1,0:T(8,128)(2,1)S(1)} %get-tuple-element.96), channel_id=1, source_target_pairs={{0,1},{1,0},{2,3},{3,2},{4,5},{5,4},{6,7},{7,6},{8,9},{9,8},{10,11... | collective-permute-start | bytes 196616 | tf_op jit(solution)/shard_map/ppermute | solution.py:36
  44.2 1.8 %collective-permute-done.17.refs_1_ = bf16[32,1024]{1,0:T(8,128)(2,1)S(1)} collective-permute-done((bf16[32,1024]{1,0:T(8,128)(2,1)S(1)}, bf16[32,1024]{1,0:T(8,128)(2,1)S(1)}, u32[]{:S(2)}, u32[]{:S(2)}) %collective-permute-start.17) | collective-permute-done | bytes 65568 | tf_op jit(solution)/shard_map/ppermute | solution.py:36
  46.0 1.3 %shard_map.126 = (bf16[32,1024]{1,0:T(8,128)(2,1)S(1)}, bf16[32,1024]{1,0:T(8,128)(2,1)S(1)}) custom-call(bf16[1024,2048]{1,0:T(8,128)(2,1)S(1)} %copy-done, bf16[2048,1024]{1,0:T(8,128)(2,1)S(1)} %copy-done.1, bf16[32,1024]{1,0:T(8,128)(2,1)S(1)} %get-tuple-element.91.refs_0_, bf16[32,1024]{1,0:T(8,128)(2,1)S(1)} %collective-permute-done.17.refs_1_), custom_call_target="tpu_custom_call" | custom-call | flops 4000000000 | bytes 8519680 | tf_op jit(solution)/shard_map/pallas_call | solution.py:53
  47.3 1.7 %collective-permute-start.18 = (bf16[32,1024]{1,0:T(8,128)(2,1)S(1)}, bf16[32,1024]{1,0:T(8,128)(2,1)S(1)}, u32[]{:S(2)}, u32[]{:S(2)}) collective-permute-start(bf16[32,1024]{1,0:T(8,128)(2,1)S(1)} %get-tuple-element.94), channel_id=1, source_target_pairs={{0,3},{1,2},{2,1},{3,0},{4,7},{5,6},{6,5},{7,4},{8,11},{9,10},{10,... | collective-permute-start | bytes 196616 | tf_op jit(solution)/shard_map/ppermute | solution.py:36
  49.0 1.3 %shard_map.127 = (bf16[32,1024]{1,0:T(8,128)(2,1)S(1)}, bf16[32,1024]{1,0:T(8,128)(2,1)S(1)}) custom-call(bf16[1024,2048]{1,0:T(8,128)(2,1)S(1)} %copy-done, bf16[2048,1024]{1,0:T(8,128)(2,1)S(1)} %copy-done.1, bf16[32,1024]{1,0:T(8,128)(2,1)S(1)} %collective-permute-done.19.refs_0_, bf16[32,1024]{1,0:T(8,128)(2,1)S(1)} %collective-permute-done.20.refs_1_), custom_call_target="tpu_custom_call" | custom-call | flops 4000000000 | bytes 8519680 | tf_op jit(solution)/shard_map/pallas_call | solution.py:53
  50.4 2.7 %collective-permute-start.22 = (bf16[32,1024]{1,0:T(8,128)(2,1)S(1)}, bf16[32,1024]{1,0:T(8,128)(2,1)S(1)}, u32[]{:S(2)}, u32[]{:S(2)}) collective-permute-start(bf16[32,1024]{1,0:T(8,128)(2,1)S(1)} %get-tuple-element.100), channel_id=1, source_target_pairs={{0,2},{1,3},{2,0},{3,1},{4,6},{5,7},{6,4},{7,5},{8,10},{9,11},{10,... | collective-permute-start | bytes 196616 | tf_op jit(solution)/shard_map/ppermute | solution.py:36
  53.7 0.9 %collective-permute-done.21.refs_2_ = bf16[32,1024]{1,0:T(8,128)(2,1)S(1)} collective-permute-done((bf16[32,1024]{1,0:T(8,128)(2,1)S(1)}, bf16[32,1024]{1,0:T(8,128)(2,1)S(1)}, u32[]{:S(2)}, u32[]{:S(2)}) %collective-permute-start.21) | collective-permute-done | bytes 65568 | tf_op jit(solution)/shard_map/ppermute | solution.py:36
  54.6 1.0 %collective-permute-done.22.refs_3_ = bf16[32,1024]{1,0:T(8,128)(2,1)S(1)} collective-permute-done((bf16[32,1024]{1,0:T(8,128)(2,1)S(1)}, bf16[32,1024]{1,0:T(8,128)(2,1)S(1)}, u32[]{:S(2)}, u32[]{:S(2)}) %collective-permute-start.22) | collective-permute-done | bytes 65568 | tf_op jit(solution)/shard_map/ppermute | solution.py:36
  (49 shorter events, 4.3 us)
Async XLA Ops:
  0.0 6.9 %copy-start.2 = (bf16[1024,2,256]{2,1,0:T(2,128)(2,1)S(1)}, bf16[1024,2,256]{2,1,0:T(2,128)(2,1)}, u32[]{:S(2)}) copy-start(bf16[1024,2,256]{2,1,0:T(2,128)(2,1)} %w_keyvalue) | copy-start | bytes 3145732
  0.0 6.9 %copy-start.3 = (bf16[1024,256]{1,0:T(8,128)(2,1)S(1)}, bf16[1024,256]{1,0:T(8,128)(2,1)}, u32[]{:S(2)}) copy-start(bf16[1024,256]{1,0:T(8,128)(2,1)} %w_query) | copy-start | bytes 1572868
  1.1 5.9 %copy-start.10 = (s32[1,8]{1,0:T(1,128)S(1)}, s32[1,8]{1,0:T(1,128)}, u32[]{:S(2)}) copy-start(s32[1,8]{1,0:T(1,128)} %lengths_in.1) | copy-start | bytes 100
  1.1 5.9 %copy-start.11 = (s32[1,32]{1,0:T(1,128)S(1)}, s32[1,32]{1,0:T(1,128)}, u32[]{:S(2)}) copy-start(s32[1,32]{1,0:T(1,128)} %table_in.1) | copy-start | bytes 388
  1.2 8.0 %collective-permute-start = (bf16[4,16,2,256]{3,2,1,0:T(2,128)(2,1)S(1)}, bf16[4,16,2,256]{3,2,1,0:T(2,128)(2,1)S(1)}, u32[]{:S(2)}, u32[]{:S(2)}) collective-permute-start(bf16[4,16,2,256]{3,2,1,0:T(2,128)(2,1)S(1)} %get-tuple-element.61), channel_id=1, source_target_pairs={{0,3},{1,2},{2,1},{3,0},{4,7},{5,6},{6,5},{7,4},{8,11},{9,10},{10,... | collective-permute-start | bytes 196616 | tf_op jit(solution)/shard_map/ppermute | solution.py:36
  6.3 4.7 %collective-permute-start.1 = (bf16[4,16,2,256]{3,2,1,0:T(2,128)(2,1)S(1)}, bf16[4,16,2,256]{3,2,1,0:T(2,128)(2,1)S(1)}, u32[]{:S(2)}, u32[]{:S(2)}) collective-permute-start(bf16[4,16,2,256]{3,2,1,0:T(2,128)(2,1)S(1)} %get-tuple-element.62), channel_id=1, source_target_pairs={{0,1},{1,0},{2,3},{3,2},{4,5},{5,4},{6,7},{7,6},{8,9},{9,8},{10,11... | collective-permute-start | bytes 196616 | tf_op jit(solution)/shard_map/ppermute | solution.py:36
  6.3 5.6 %collective-permute-start.2 = (bf16[4,16,2,256]{3,2,1,0:T(2,128)(2,1)S(1)}, bf16[4,16,2,256]{3,2,1,0:T(2,128)(2,1)S(1)}, u32[]{:S(2)}, u32[]{:S(2)}) collective-permute-start(bf16[4,16,2,256]{3,2,1,0:T(2,128)(2,1)S(1)} %get-tuple-element.63), channel_id=1, source_target_pairs={{0,2},{1,3},{2,0},{3,1},{4,6},{5,7},{6,4},{7,5},{8,10},{9,11},{10,... | collective-permute-start | bytes 196616 | tf_op jit(solution)/shard_map/ppermute | solution.py:36
  9.2 2.7 %collective-permute-start.5 = (bf16[4,16,2,256]{3,2,1,0:T(2,128)(2,1)S(1)}, bf16[4,16,2,256]{3,2,1,0:T(2,128)(2,1)S(1)}, u32[]{:S(2)}, u32[]{:S(2)}) collective-permute-start(bf16[4,16,2,256]{3,2,1,0:T(2,128)(2,1)S(1)} %collective-permute-done.refs_1_), channel_id=1, source_target_pairs={{0,4},{4,0},{1,5},{5,1},{2,6},{6,2},{3,7},{7,3},{8,12},{12,8},{9,1... | collective-permute-start | bytes 196616 | tf_op jit(solution)/shard_map/ppermute | solution.py:36
  9.2 3.5 %collective-permute-start.3 = (bf16[128,512]{1,0:T(8,128)(2,1)S(1)}, bf16[128,512]{1,0:T(8,128)(2,1)S(1)}, u32[]{:S(2)}, u32[]{:S(2)}) collective-permute-start(bf16[128,512]{1,0:T(8,128)(2,1)S(1)} %get-tuple-element.60.keyvalue), channel_id=1, source_target_pairs={{0,4},{4,0},{1,5},{5,1},{2,6},{6,2},{3,7},{7,3},{8,12},{12,8},{9,1... | collective-permute-start | bytes 393224 | tf_op jit(solution)/shard_map/ppermute | solution.py:41
  9.7 3.0 %collective-permute-start.4 = (bf16[4,16,2,256]{3,2,1,0:T(2,128)(2,1)S(1)}, bf16[4,16,2,256]{3,2,1,0:T(2,128)(2,1)S(1)}, u32[]{:S(2)}, u32[]{:S(2)}) collective-permute-start(bf16[4,16,2,256]{3,2,1,0:T(2,128)(2,1)S(1)} %get-tuple-element.67.refs_0_), channel_id=1, source_target_pairs={{0,4},{4,0},{1,5},{5,1},{2,6},{6,2},{3,7},{7,3},{8,12},{12,8},{9,1... | collective-permute-start | bytes 196616 | tf_op jit(solution)/shard_map/ppermute | solution.py:36
  11.0 1.8 %collective-permute-start.6 = (bf16[4,16,2,256]{3,2,1,0:T(2,128)(2,1)S(1)}, bf16[4,16,2,256]{3,2,1,0:T(2,128)(2,1)S(1)}, u32[]{:S(2)}, u32[]{:S(2)}) collective-permute-start(bf16[4,16,2,256]{3,2,1,0:T(2,128)(2,1)S(1)} %collective-permute-done.1.refs_2_), channel_id=1, source_target_pairs={{0,4},{4,0},{1,5},{5,1},{2,6},{6,2},{3,7},{7,3},{8,12},{12,8},{9,1... | collective-permute-start | bytes 196616 | tf_op jit(solution)/shard_map/ppermute | solution.py:36
  11.9 1.3 %collective-permute-start.7 = (bf16[4,16,2,256]{3,2,1,0:T(2,128)(2,1)S(1)}, bf16[4,16,2,256]{3,2,1,0:T(2,128)(2,1)S(1)}, u32[]{:S(2)}, u32[]{:S(2)}) collective-permute-start(bf16[4,16,2,256]{3,2,1,0:T(2,128)(2,1)S(1)} %collective-permute-done.2.refs_3_), channel_id=1, source_target_pairs={{0,4},{4,0},{1,5},{5,1},{2,6},{6,2},{3,7},{7,3},{8,12},{12,8},{9,1... | collective-permute-start | bytes 196616 | tf_op jit(solution)/shard_map/ppermute | solution.py:36
  14.3 6.9 %collective-permute-start.8 = (bf16[32,1024]{1,0:T(8,128)(2,1)S(1)}, bf16[32,1024]{1,0:T(8,128)(2,1)S(1)}, u32[]{:S(2)}, u32[]{:S(2)}) collective-permute-start(bf16[32,1024]{1,0:T(8,128)(2,1)S(1)} %get-tuple-element.72), channel_id=1, source_target_pairs={{0,2},{1,3},{2,0},{3,1},{4,6},{5,7},{6,4},{7,5},{8,10},{9,11},{10,... | collective-permute-start | bytes 196616 | tf_op jit(solution)/shard_map/ppermute | solution.py:36
  16.3 4.9 %collective-permute-start.9 = (bf16[32,1024]{1,0:T(8,128)(2,1)S(1)}, bf16[32,1024]{1,0:T(8,128)(2,1)S(1)}, u32[]{:S(2)}, u32[]{:S(2)}) collective-permute-start(bf16[32,1024]{1,0:T(8,128)(2,1)S(1)} %get-tuple-element.73), channel_id=1, source_target_pairs={{0,1},{1,0},{2,3},{3,2},{4,5},{5,4},{6,7},{7,6},{8,9},{9,8},{10,11... | collective-permute-start | bytes 196616 | tf_op jit(solution)/shard_map/ppermute | solution.py:36
  17.3 6.1 %collective-permute-start.10 = (bf16[32,1024]{1,0:T(8,128)(2,1)S(1)}, bf16[32,1024]{1,0:T(8,128)(2,1)S(1)}, u32[]{:S(2)}, u32[]{:S(2)}) collective-permute-start(bf16[32,1024]{1,0:T(8,128)(2,1)S(1)} %get-tuple-element.74), channel_id=1, source_target_pairs={{0,3},{1,2},{2,1},{3,0},{4,7},{5,6},{6,5},{7,4},{8,11},{9,10},{10,... | collective-permute-start | bytes 196616 | tf_op jit(solution)/shard_map/ppermute | solution.py:36
  23.4 6.9 %copy-start.5 = (bf16[1024,256]{1,0:T(8,128)(2,1)S(1)}, bf16[1024,256]{1,0:T(8,128)(2,1)}, u32[]{:S(2)}) copy-start(bf16[1024,256]{1,0:T(8,128)(2,1)} %w_cross_query.3) | copy-start | bytes 1572868
  23.4 6.9 %copy-start.6 = (bf16[256,1024]{1,0:T(8,128)(2,1)S(1)}, bf16[256,1024]{1,0:T(8,128)(2,1)}, u32[]{:S(2)}) copy-start(bf16[256,1024]{1,0:T(8,128)(2,1)} %w_cross_out.3) | copy-start | bytes 1572868
  23.4 6.9 %copy-start.9 = (bf16[1,256,2,256]{3,2,1,0:T(2,128)(2,1)S(1)}, bf16[1,256,2,256]{3,2,1,0:T(2,128)(2,1)}, u32[]{:S(2)}) copy-start(bf16[1,256,2,256]{3,2,1,0:T(2,128)(2,1)} %cross_cache.3) | copy-start | bytes 786436
  23.7 6.6 %collective-permute-start.11 = (bf16[32,1024]{1,0:T(8,128)(2,1)S(1)}, bf16[32,1024]{1,0:T(8,128)(2,1)S(1)}, u32[]{:S(2)}, u32[]{:S(2)}) collective-permute-start(bf16[32,1024]{1,0:T(8,128)(2,1)S(1)} %get-tuple-element.77), channel_id=1, source_target_pairs={{0,3},{1,2},{2,1},{3,0},{4,7},{5,6},{6,5},{7,4},{8,11},{9,10},{10,... | collective-permute-start | bytes 196616 | tf_op jit(solution)/shard_map/ppermute | solution.py:36
  25.6 7.7 %collective-permute-start.12 = (bf16[32,1024]{1,0:T(8,128)(2,1)S(1)}, bf16[32,1024]{1,0:T(8,128)(2,1)S(1)}, u32[]{:S(2)}, u32[]{:S(2)}) collective-permute-start(bf16[32,1024]{1,0:T(8,128)(2,1)S(1)} %get-tuple-element.81), channel_id=1, source_target_pairs={{0,1},{1,0},{2,3},{3,2},{4,5},{5,4},{6,7},{7,6},{8,9},{9,8},{10,11... | collective-permute-start | bytes 196616 | tf_op jit(solution)/shard_map/ppermute | solution.py:36
  26.1 7.2 %collective-permute-start.13 = (bf16[32,1024]{1,0:T(8,128)(2,1)S(1)}, bf16[32,1024]{1,0:T(8,128)(2,1)S(1)}, u32[]{:S(2)}, u32[]{:S(2)}) collective-permute-start(bf16[32,1024]{1,0:T(8,128)(2,1)S(1)} %get-tuple-element.82), channel_id=1, source_target_pairs={{0,2},{1,3},{2,0},{3,1},{4,6},{5,7},{6,4},{7,5},{8,10},{9,11},{10,... | collective-permute-start | bytes 196616 | tf_op jit(solution)/shard_map/ppermute | solution.py:36
  31.2 7.3 %collective-permute-start.15 = (bf16[32,1024]{1,0:T(8,128)(2,1)S(1)}, bf16[32,1024]{1,0:T(8,128)(2,1)S(1)}, u32[]{:S(2)}, u32[]{:S(2)}) collective-permute-start(bf16[32,1024]{1,0:T(8,128)(2,1)S(1)} %get-tuple-element.83), channel_id=1, source_target_pairs={{0,3},{1,2},{2,1},{3,0},{4,7},{5,6},{6,5},{7,4},{8,11},{9,10},{10,... | collective-permute-start | bytes 196616 | tf_op jit(solution)/shard_map/ppermute | solution.py:36
  34.1 4.3 %collective-permute-start.14 = (bf16[32,1024]{1,0:T(8,128)(2,1)S(1)}, bf16[32,1024]{1,0:T(8,128)(2,1)S(1)}, u32[]{:S(2)}, u32[]{:S(2)}) collective-permute-start(bf16[32,1024]{1,0:T(8,128)(2,1)S(1)} %get-tuple-element.86), channel_id=1, source_target_pairs={{0,1},{1,0},{2,3},{3,2},{4,5},{5,4},{6,7},{7,6},{8,9},{9,8},{10,11... | collective-permute-start | bytes 196616 | tf_op jit(solution)/shard_map/ppermute | solution.py:36
  34.4 5.2 %collective-permute-start.16 = (bf16[32,1024]{1,0:T(8,128)(2,1)S(1)}, bf16[32,1024]{1,0:T(8,128)(2,1)S(1)}, u32[]{:S(2)}, u32[]{:S(2)}) collective-permute-start(bf16[32,1024]{1,0:T(8,128)(2,1)S(1)} %get-tuple-element.87), channel_id=1, source_target_pairs={{0,2},{1,3},{2,0},{3,1},{4,6},{5,7},{6,4},{7,5},{8,10},{9,11},{10,... | collective-permute-start | bytes 196616 | tf_op jit(solution)/shard_map/ppermute | solution.py:36
  39.5 6.5 %copy-start = (bf16[1024,2048]{1,0:T(8,128)(2,1)S(1)}, bf16[1024,2048]{1,0:T(8,128)(2,1)}, u32[]{:S(2)}) copy-start(bf16[1024,2048]{1,0:T(8,128)(2,1)} %w_up.3) | copy-start | bytes 12582916
  39.5 6.5 %copy-start.1 = (bf16[2048,1024]{1,0:T(8,128)(2,1)S(1)}, bf16[2048,1024]{1,0:T(8,128)(2,1)}, u32[]{:S(2)}) copy-start(bf16[2048,1024]{1,0:T(8,128)(2,1)} %w_down.3) | copy-start | bytes 12582916
  39.8 6.2 %collective-permute-start.17 = (bf16[32,1024]{1,0:T(8,128)(2,1)S(1)}, bf16[32,1024]{1,0:T(8,128)(2,1)S(1)}, u32[]{:S(2)}, u32[]{:S(2)}) collective-permute-start(bf16[32,1024]{1,0:T(8,128)(2,1)S(1)} %get-tuple-element.90), channel_id=1, source_target_pairs={{0,3},{1,2},{2,1},{3,0},{4,7},{5,6},{6,5},{7,4},{8,11},{9,10},{10,... | collective-permute-start | bytes 196616 | tf_op jit(solution)/shard_map/ppermute | solution.py:36
  41.5 7.5 %collective-permute-start.19 = (bf16[32,1024]{1,0:T(8,128)(2,1)S(1)}, bf16[32,1024]{1,0:T(8,128)(2,1)S(1)}, u32[]{:S(2)}, u32[]{:S(2)}) collective-permute-start(bf16[32,1024]{1,0:T(8,128)(2,1)S(1)} %get-tuple-element.95), channel_id=1, source_target_pairs={{0,2},{1,3},{2,0},{3,1},{4,6},{5,7},{6,4},{7,5},{8,10},{9,11},{10,... | collective-permute-start | bytes 196616 | tf_op jit(solution)/shard_map/ppermute | solution.py:36
  43.2 5.8 %collective-permute-start.20 = (bf16[32,1024]{1,0:T(8,128)(2,1)S(1)}, bf16[32,1024]{1,0:T(8,128)(2,1)S(1)}, u32[]{:S(2)}, u32[]{:S(2)}) collective-permute-start(bf16[32,1024]{1,0:T(8,128)(2,1)S(1)} %get-tuple-element.96), channel_id=1, source_target_pairs={{0,1},{1,0},{2,3},{3,2},{4,5},{5,4},{6,7},{7,6},{8,9},{9,8},{10,11... | collective-permute-start | bytes 196616 | tf_op jit(solution)/shard_map/ppermute | solution.py:36
  47.3 6.4 %collective-permute-start.18 = (bf16[32,1024]{1,0:T(8,128)(2,1)S(1)}, bf16[32,1024]{1,0:T(8,128)(2,1)S(1)}, u32[]{:S(2)}, u32[]{:S(2)}) collective-permute-start(bf16[32,1024]{1,0:T(8,128)(2,1)S(1)} %get-tuple-element.94), channel_id=1, source_target_pairs={{0,3},{1,2},{2,1},{3,0},{4,7},{5,6},{6,5},{7,4},{8,11},{9,10},{10,... | collective-permute-start | bytes 196616 | tf_op jit(solution)/shard_map/ppermute | solution.py:36
  50.3 4.3 %collective-permute-start.21 = (bf16[32,1024]{1,0:T(8,128)(2,1)S(1)}, bf16[32,1024]{1,0:T(8,128)(2,1)S(1)}, u32[]{:S(2)}, u32[]{:S(2)}) collective-permute-start(bf16[32,1024]{1,0:T(8,128)(2,1)S(1)} %get-tuple-element.99), channel_id=1, source_target_pairs={{0,1},{1,0},{2,3},{3,2},{4,5},{5,4},{6,7},{7,6},{8,9},{9,8},{10,11... | collective-permute-start | bytes 196616 | tf_op jit(solution)/shard_map/ppermute | solution.py:36
  50.4 5.2 %collective-permute-start.22 = (bf16[32,1024]{1,0:T(8,128)(2,1)S(1)}, bf16[32,1024]{1,0:T(8,128)(2,1)S(1)}, u32[]{:S(2)}, u32[]{:S(2)}) collective-permute-start(bf16[32,1024]{1,0:T(8,128)(2,1)S(1)} %get-tuple-element.100), channel_id=1, source_target_pairs={{0,2},{1,3},{2,0},{3,1},{4,6},{5,7},{6,4},{7,5},{8,10},{9,11},{10,... | collective-permute-start | bytes 196616 | tf_op jit(solution)/shard_map/ppermute | solution.py:36
  (3 other events, 8.2 us)
